TPU v7x, 256 devices: a whole 4x4x8 slice. The times are simulated.
256 devices in a mesh: seq: 32 (over y, z), mp: 8 (over x, core).
Axes of the slice: x: 4, y: 4, z: 8, core: 2. Of those that a mesh axis runs over, the one named last changes fastest.
Arguments:
- queries: bfloat16 [16384, 6144], P('seq', 'mp'), may hold values from -8 to 8
- keys: bfloat16 [16384, 6144], P('seq', 'mp'), may hold values from -8 to 8
- values: bfloat16 [16384, 6144], P('seq', 'mp'), may hold values from -10 to 10
- residual: bfloat16 [16384, 6144], P('seq', 'mp'), may hold values from -42 to 42
- out_weight: bfloat16 [6144, 6144], P('mp', 'seq'), may hold values from -0.078125 to 0.078125
- gate: bfloat16 [32, 6144], P(None, 'mp'), may hold values from -4 to 4
- mod_scale: bfloat16 [32, 6144], P(None, 'mp'), may hold values from -2.5 to 2.5
- mod_shift: bfloat16 [32, 6144], P(None, 'mp'), may hold values from -4 to 4
- frame_counts: int32 [32], replicated, may hold values from 1 to 8, 128 in all
- patch_counts: int32 [32], replicated, may hold values from 32 to 128, as said below
Outputs:
- updated: bfloat16 [16384, 6144], P('seq', 'mp')
- normed: bfloat16 [16384, 6144], P('seq', 'mp')
Inputs may be any that keep to these rules, and one draw needn't show every extreme that they name: `patch_counts`: some clip has 128 live cells a frame.
All inputs are finite; a program needn't handle non-finite values.
Results may differ from a plain program's by a relative error of at most 0.0042.
Values may be sent and summed in bfloat16 or wider, within the bound.
No kernel may reach another device: no remote copies, remote signals or barrier semaphores. Data moves between devices by JAX's collectives and lax.ppermute only.
A program may use at most 128 MiB of HBM per device.

v0:
```python
import math

import jax
import jax.numpy as jnp
from jax import lax
from jax.sharding import PartitionSpec as P

D = 6144
HEAD_DIM = 128
S = 128
FR = 4


eps = 1e-06
negative = -1e30


def clip_index(frame_counts, frame_ids):
    ends = jnp.cumsum(frame_counts)
    return jnp.sum((ends[None, :] <= frame_ids[:, None]).astype(jnp.int32), axis=1)


def one_hot(clip_ids, clip_total):
    return (clip_ids[:, None] == jnp.arange(clip_total, dtype=jnp.int32)[None, :]).astype(
        jnp.bfloat16
    )


def softmax_rows(scores, key_mask):
    scores = jnp.where(key_mask, scores, negative)
    highest = jnp.max(scores, axis=-1, keepdims=True)
    raised = jnp.exp(scores - highest)
    return (raised / jnp.sum(raised, axis=-1, keepdims=True)).astype(jnp.bfloat16)


def lookup(hot_rows, table):
    return jnp.dot(hot_rows, table, preferred_element_type=jnp.float32)


def local(
    queries,
    keys,
    values,
    residual,
    out_weight,
    gate,
    mod_scale,
    mod_shift,
    frame_counts,
    patch_counts,
):
    seq_size = lax.axis_size("seq")
    seq_index = lax.axis_index("seq")
    local_rows, local_cols = queries.shape
    pair_count = local_cols // (2 * HEAD_DIM)
    all_frames = FR * seq_size
    clip_total = frame_counts.shape[0]
    inv_scale = 1.0 / math.sqrt(HEAD_DIM)

    def split_pairs(array):
        shaped = array.reshape(FR, S, pair_count, 2, HEAD_DIM)
        return (shaped[:, :, :, 0, :], shaped[:, :, :, 1, :])

    q_space, q_time = split_pairs(queries)
    k_space, k_time = split_pairs(keys)
    v_space, v_time = split_pairs(values)
    own_clips = clip_index(frame_counts, seq_index * FR + jnp.arange(FR, dtype=jnp.int32))
    own_hot = one_hot(own_clips, clip_total)
    own_grid = jnp.take(patch_counts, own_clips, axis=0)
    live_own = jnp.arange(S, dtype=jnp.int32)[None, :] < own_grid[:, None]
    moved_q, moved_k, moved_v = (
        lax.all_to_all(q_time, "seq", split_axis=1, concat_axis=0, tiled=True),
        lax.all_to_all(k_time, "seq", split_axis=1, concat_axis=0, tiled=True),
        lax.all_to_all(v_time, "seq", split_axis=1, concat_axis=0, tiled=True),
    )
    space_scores = (
        jnp.einsum("fphd,fqhd->fhpq", q_space, k_space, preferred_element_type=jnp.float32)
        * inv_scale
    )
    space_w = softmax_rows(space_scores, live_own[:, None, None, :])
    space_out = jnp.einsum("fhpq,fqhd->fphd", space_w, v_space, preferred_element_type=jnp.float32)
    space_out = jnp.where(live_own[:, :, None, None], space_out, 0.0).astype(jnp.bfloat16)
    slot_width = S // seq_size
    slot_ids = seq_index * slot_width + jnp.arange(slot_width, dtype=jnp.int32)
    all_clips = clip_index(frame_counts, jnp.arange(all_frames, dtype=jnp.int32))
    all_grid = jnp.take(patch_counts, all_clips, axis=0)
    live_all = slot_ids[None, :] < all_grid[:, None]
    same_clip = all_clips[:, None] == all_clips[None, :]
    time_scores = (
        jnp.einsum("fphd,gphd->phfg", moved_q, moved_k, preferred_element_type=jnp.float32)
        * inv_scale
    )
    time_mask = same_clip[None, None, :, :] & live_all.T[:, None, None, :]
    time_w = softmax_rows(time_scores, time_mask)
    time_out = jnp.einsum("phfg,gphd->fphd", time_w, moved_v, preferred_element_type=jnp.float32)
    time_out = jnp.where(live_all[:, :, None, None], time_out, 0.0).astype(jnp.bfloat16)
    returned = lax.all_to_all(time_out, "seq", split_axis=0, concat_axis=1, tiled=True)
    attended = jnp.stack([space_out, returned], axis=3).reshape(local_rows, local_cols)
    partial_terms = jnp.dot(
        attended,
        lax.all_gather(out_weight, "seq", axis=1, tiled=True),
        preferred_element_type=jnp.float32,
    )
    summed = lax.psum_scatter(partial_terms, "mp", scatter_dimension=1, tiled=True)
    width_local = summed.shape[1]
    gate_frames = lookup(own_hot, gate)
    scale_frames = lookup(own_hot, mod_scale)
    shift_frames = lookup(own_hot, mod_shift)
    combined = residual.astype(jnp.float32).reshape(FR, S, width_local) + gate_frames[
        :, None, :
    ] * summed.reshape(FR, S, width_local)
    updated = combined.astype(jnp.bfloat16)
    widened = updated.astype(jnp.float32)
    local_squares = jnp.sum(widened * widened, axis=2)
    total_squares = lax.psum(local_squares, "mp")
    mean_sq = total_squares / D
    normed = (
        widened * lax.rsqrt(mean_sq + eps)[:, :, None] * (1.0 + scale_frames[:, None, :])
        + shift_frames[:, None, :]
    )
    return (
        updated.reshape(local_rows, width_local),
        normed.astype(jnp.bfloat16).reshape(local_rows, width_local),
    )


def solution(mesh):
    in_specs = (
        P("seq", "mp"),
        P("seq", "mp"),
        P("seq", "mp"),
        P("seq", "mp"),
        P("mp", "seq"),
        P(None, "mp"),
        P(None, "mp"),
        P(None, "mp"),
        P(),
        P(),
    )
    out_specs = (P("seq", "mp"), P("seq", "mp"))
    return jax.shard_map(local, mesh=mesh, in_specs=in_specs, out_specs=out_specs, check_vma=False)
```

profile of v0, /device:TPU:8, one launch (start us, length us, event | category | flops | bytes accessed | tf_op | source)
XLA Modules:
  0.0 243.0 jit_solution(8762318112469712653)
XLA Ops:
  7.2 0.0 copy-start
  7.2 0.0 all-gather.2.cloned.1.call-start
  7.2 0.7 all-gather.2.cloned.1.call-update
  7.9 2.0 reshape.247
  10.0 0.0 copy-done.5
  10.0 0.2 reshape.248
  10.1 3.1 %fusion.30 = (bf16[4,128,3,1,128]{4,3,2,1,0:T(2,128)(2,1)}, bf16[4,128,3,1,128]{4,3,2,1,0:T(2,128)(2,1)S(1)}, bf16[4,128,3,1,128]{4,3,2,1,0:T(2,128)(2,1)S(1)}, bf16[4,128,3,1,128]{4,3,2,1,0:T(2,128)(2,1)}) fusion(bf16[4,128,3,2,128]{4,3,2,1,0:T(2,128)(2,1)S(1)} %reshape.247, bf16[4,128,3,2,128]{4,3,2,1,0:T(2,128)(2,1)S(1)} %reshape.248), kind=kLoop, calls=%fused_computation.67 | loop fusion | bytes 3145728 | tf_op jit(solution)/shard_map/slice | solution.py:62
  13.3 0.1 copy.122
  13.4 1.1 copy.86
  14.4 11.7 %all-to-all-start = ((bf16[4,128,3,128]{3,0,2,1:T(4,128)(2,1)}), bf16[4,128,3,128]{3,0,2,1:T(4,128)(2,1)S(1)}, u32[]{:S(2)}, u32[]{:S(2)}) async-start(bf16[4,128,3,128]{3,0,2,1:T(4,128)(2,1)} %copy.86), calls=%async_computation | async-start | bytes 786432 | tf_op jit(solution)/shard_map/all_to_all | solution.py:72
  26.1 0.1 copy.80
  26.2 0.1 reduce-window.8
  26.3 0.1 reduce.1
  26.4 0.2 reshape.249
  26.6 0.1 copy.121
  26.7 1.1 copy.89
  27.7 1.1 fusion.32
  28.8 0.0 copy-start.1
  28.8 0.1 copy.120
  28.9 1.0 copy.92
  30.0 0.1 convert_reduce_fusion
  30.1 0.2 convert_reduce_fusion.1
  30.3 12.2 %all-to-all-done = bf16[4,128,3,128]{3,0,2,1:T(4,128)(2,1)S(1)} async-done(((bf16[4,128,3,128]{3,0,2,1:T(4,128)(2,1)}), bf16[4,128,3,128]{3,0,2,1:T(4,128)(2,1)S(1)}, u32[]{:S(2)}, u32[]{:S(2)}) %all-to-all-start) | async-done | bytes 393248 | tf_op jit(solution)/shard_map/all_to_all | solution.py:72
  42.5 7.1 %all-to-all-start.1 = ((bf16[4,128,3,128]{3,0,2,1:T(4,128)(2,1)}), bf16[4,128,3,128]{3,0,2,1:T(4,128)(2,1)S(1)}, u32[]{:S(2)}, u32[]{:S(2)}) async-start(bf16[4,128,3,128]{3,0,2,1:T(4,128)(2,1)} %copy.89), calls=%async_computation.1 | async-start | bytes 786432 | tf_op jit(solution)/shard_map/all_to_all | solution.py:73
  49.6 1.2 gather_fusion.1
  50.9 0.1 broadcast_compare_fusion.1
  50.9 0.1 broadcast_compare_fusion.2
  51.0 12.7 %all-to-all-done.1 = bf16[4,128,3,128]{3,0,2,1:T(4,128)(2,1)S(1)} async-done(((bf16[4,128,3,128]{3,0,2,1:T(4,128)(2,1)}), bf16[4,128,3,128]{3,0,2,1:T(4,128)(2,1)S(1)}, u32[]{:S(2)}, u32[]{:S(2)}) %all-to-all-start.1) | async-done | bytes 393248 | tf_op jit(solution)/shard_map/all_to_all | solution.py:73
  63.7 6.9 %all-to-all-start.2 = ((bf16[4,128,3,128]{3,0,2,1:T(4,128)(2,1)}), bf16[4,128,3,128]{3,0,2,1:T(4,128)(2,1)S(1)}, u32[]{:S(2)}, u32[]{:S(2)}) async-start(bf16[4,128,3,128]{3,0,2,1:T(4,128)(2,1)} %copy.92), calls=%async_computation.2 | async-start | bytes 786432 | tf_op jit(solution)/shard_map/all_to_all | solution.py:74
  70.6 0.6 gather_fusion
  71.3 0.1 broadcast_compare_fusion
  71.4 0.1 broadcast_and_fusion
  71.5 0.2 copy.87
  71.7 0.2 copy.90
  71.9 14.4 %all-to-all-done.2 = bf16[4,128,3,128]{3,0,2,1:T(4,128)(2,1)S(1)} async-done(((bf16[4,128,3,128]{3,0,2,1:T(4,128)(2,1)}), bf16[4,128,3,128]{3,0,2,1:T(4,128)(2,1)S(1)}, u32[]{:S(2)}, u32[]{:S(2)}) %all-to-all-start.2) | async-done | bytes 393248 | tf_op jit(solution)/shard_map/all_to_all | solution.py:74
  86.3 0.2 copy.93
  86.5 0.4 fusion.14
  86.9 0.2 fusion.33
  87.0 0.4 fusion.16
  87.4 0.0 copy-start.3
  87.5 0.0 copy-start.4
  87.5 1.0 copy.95
  88.5 6.9 %all-to-all-start.3 = ((bf16[128,4,3,128]{3,1,2,0:T(4,128)(2,1)}), bf16[128,4,3,128]{3,1,2,0:T(4,128)(2,1)S(1)}, u32[]{:S(2)}, u32[]{:S(2)}) async-start(bf16[128,4,3,128]{3,1,2,0:T(4,128)(2,1)} %copy.95), calls=%async_computation.3 | async-start | bytes 786432 | tf_op jit(solution)/shard_map/all_to_all | solution.py:97
  95.4 0.2 reduce-scatter.2.cloned.1.call-start
  95.7 0.1 iota_compare_fusion.1
  95.7 0.5 fusion.34
  96.2 1.3 fusion.13
  97.5 1.9 fusion.17
  99.4 11.6 %all-to-all-done.3 = bf16[128,4,3,128]{3,1,2,0:T(4,128)(2,1)S(1)} async-done(((bf16[128,4,3,128]{3,1,2,0:T(4,128)(2,1)}), bf16[128,4,3,128]{3,1,2,0:T(4,128)(2,1)S(1)}, u32[]{:S(2)}, u32[]{:S(2)}) %all-to-all-start.3) | async-done | bytes 393248 | tf_op jit(solution)/shard_map/all_to_all | solution.py:97
  111.0 0.2 copy.96
  111.2 0.1 pad_maximum_fusion
  111.3 0.8 copy.97
  112.1 0.4 reshape.250
  112.4 22.7 %all-gather.2.cloned.1.call-done = bf16[768,6144]{0,1:T(8,128)(2,1)} async-done(((bf16[768,192]{0,1:T(8,128)(2,1)}), bf16[768,6144]{0,1:T(8,128)(2,1)}) %all-gather.2.cloned.1.call-update) | async-done | bytes 9437200 | tf_op jit(solution)/shard_map/all_gather | solution.py:101
  135.1 11.6 %fusion.35 = f32[512,6144]{1,0:T(8,128)} fusion(bf16[512,768]{1,0:T(8,128)(2,1)S(1)} %reshape.250, bf16[768,6144]{0,1:T(8,128)(2,1)} %all-gather.2.cloned.1.call-done), kind=kOutput, calls=%fused_computation.72 | convolution fusion | flops 4831838208 | bytes 22806528 | tf_op jit(solution)/shard_map/dot_general | solution.py:99
  146.8 0.0 reduce-scatter.2.cloned.1.call-update
  146.8 0.2 fusion.21
  147.0 0.6 copy-done.9
  147.5 0.2 convolution_add_fusion
  147.7 0.2 fusion.20
  147.9 72.5 %reduce-scatter.2.cloned.1.call-done = f32[512,768]{1,0:T(8,128)} async-done(((f32[512,6144]{1,0:T(8,128)}), f32[512,768]{1,0:T(8,128)}) %reduce-scatter.2.cloned.1.call-update) | async-done | bytes 1572880 | tf_op jit(solution)/shard_map/reduce_scatter | solution.py:104
  220.4 1.8 fusion.2
  222.2 12.8 %psum.7 = f32[4,128]{1,0:T(4,128)S(1)} all-reduce(f32[4,128]{1,0:T(4,128)S(1)} %bitcast.97), channel_id=1, replica_groups=mesh['seq'=32,'mp'=8] {'mp'}, use_global_device_ids=true, to_apply=%region_9.10 | all-reduce | flops 512 | bytes 4096 | tf_op jit(solution)/shard_map/psum | solution.py:115
  235.0 1.2 fusion.5
  (24 shorter events, 0.1 us)
Async XLA Ops:
  7.2 139.6 %copy-start = (bf16[32,768]{1,0:T(8,128)(2,1)S(1)}, bf16[32,768]{1,0:T(8,128)(2,1)}, u32[]{:S(2)}) copy-start(bf16[32,768]{1,0:T(8,128)(2,1)} %param.15) | copy-start | bytes 147460
  7.2 2.8 %copy-start.5 = (bf16[512,768]{1,0:T(8,128)(2,1)S(1)}, bf16[512,768]{1,0:T(8,128)(2,1)}, u32[]{:S(2)}) copy-start(bf16[512,768]{1,0:T(8,128)(2,1)} %param.11) | copy-start | bytes 2359300
  7.2 127.9 %all-gather.2.cloned.1.call-start = ((), (), s32[]{:S(2)}) async-start(), calls=%async_computation.5 | async-start | bytes 9732096 | tf_op jit(solution)/shard_map/all_gather | solution.py:101
  13.3 12.9 %copy-start.8 = (s32[32]{0:T(128)S(1)}, s32[32]{0:T(128)}, u32[]{:S(2)}) copy-start(s32[32]{0:T(128)} %param.18) | copy-start | bytes 388
  13.3 13.1 %copy-start.6 = (bf16[512,768]{1,0:T(8,128)(2,1)S(1)}, bf16[512,768]{1,0:T(8,128)(2,1)}, u32[]{:S(2)}) copy-start(bf16[512,768]{1,0:T(8,128)(2,1)} %param.12) | copy-start | bytes 2359300
  14.4 28.1 %all-to-all-start = ((bf16[4,128,3,128]{3,0,2,1:T(4,128)(2,1)}), bf16[4,128,3,128]{3,0,2,1:T(4,128)(2,1)S(1)}, u32[]{:S(2)}, u32[]{:S(2)}) async-start(bf16[4,128,3,128]{3,0,2,1:T(4,128)(2,1)} %copy.86), calls=%async_computation | async-start | bytes 786432 | tf_op jit(solution)/shard_map/all_to_all | solution.py:72
  28.8 20.8 %copy-start.1 = (s32[32]{0:T(128)S(1)}, s32[32]{0:T(128)}, u32[]{:S(2)}) copy-start(s32[32]{0:T(128)} %param.19) | copy-start | bytes 388
  42.5 21.2 %all-to-all-start.1 = ((bf16[4,128,3,128]{3,0,2,1:T(4,128)(2,1)}), bf16[4,128,3,128]{3,0,2,1:T(4,128)(2,1)S(1)}, u32[]{:S(2)}, u32[]{:S(2)}) async-start(bf16[4,128,3,128]{3,0,2,1:T(4,128)(2,1)} %copy.89), calls=%async_computation.1 | async-start | bytes 786432 | tf_op jit(solution)/shard_map/all_to_all | solution.py:73
  63.7 22.6 %all-to-all-start.2 = ((bf16[4,128,3,128]{3,0,2,1:T(4,128)(2,1)}), bf16[4,128,3,128]{3,0,2,1:T(4,128)(2,1)S(1)}, u32[]{:S(2)}, u32[]{:S(2)}) async-start(bf16[4,128,3,128]{3,0,2,1:T(4,128)(2,1)} %copy.92), calls=%async_computation.2 | async-start | bytes 786432 | tf_op jit(solution)/shard_map/all_to_all | solution.py:74
  87.4 8.3 %copy-start.3 = (bf16[4,128,3,1,128]{4,3,2,1,0:T(2,128)(2,1)S(1)}, bf16[4,128,3,1,128]{4,3,2,1,0:T(2,128)(2,1)}, u32[]{:S(2)}) copy-start(bf16[4,128,3,1,128]{4,3,2,1,0:T(2,128)(2,1)} %get-tuple-element.4) | copy-start | bytes 1179652
  87.5 8.3 %copy-start.4 = (bf16[4,128,3,1,128]{4,3,2,1,0:T(2,128)(2,1)S(1)}, bf16[4,128,3,1,128]{4,3,2,1,0:T(2,128)(2,1)}, u32[]{:S(2)}) copy-start(bf16[4,128,3,1,128]{4,3,2,1,0:T(2,128)(2,1)} %get-tuple-element.11) | copy-start | bytes 1179652
  88.5 22.5 %all-to-all-start.3 = ((bf16[128,4,3,128]{3,1,2,0:T(4,128)(2,1)}), bf16[128,4,3,128]{3,1,2,0:T(4,128)(2,1)S(1)}, u32[]{:S(2)}, u32[]{:S(2)}) async-start(bf16[128,4,3,128]{3,1,2,0:T(4,128)(2,1)} %copy.95), calls=%async_computation.3 | async-start | bytes 786432 | tf_op jit(solution)/shard_map/all_to_all | solution.py:97
  95.4 125.0 %reduce-scatter.2.cloned.1.call-start = ((), (), s32[]{:S(2)}) async-start(), calls=%async_computation.6 | async-start | bytes 14155776 | tf_op jit(solution)/shard_map/reduce_scatter | solution.py:104
  146.7 0.8 copy-start.9
  146.7 1.0 copy-start.10
  146.8 73.6 %copy-start.7 = (bf16[512,768]{1,0:T(8,128)(2,1)S(1)}, bf16[512,768]{1,0:T(8,128)(2,1)}, u32[]{:S(2)}) copy-start(bf16[512,768]{1,0:T(8,128)(2,1)} %param.13) | copy-start | bytes 2359300
  222.2 14.0 %copy-start.2 = (bf16[512,768]{1,0:T(8,128)(2,1)}, bf16[512,768]{1,0:T(8,128)(2,1)S(1)}, u32[]{:S(2)}) copy-start(bf16[512,768]{1,0:T(8,128)(2,1)S(1)} %get-tuple-element.3) | copy-start | bytes 2359300
Sparse Core Ops, SparseCore 0:
  10.6 124.4 all-gather.1
  146.9 73.4 reduce-scatter.1
where the time goes:
time: 244 us; the launch traced here: 243 us
  waiting for transfers between devices  147 us (60%)
  starting transfers between devices  32.8 us (13%)
  matrix products  16.7 us (7%)
  local copies, waits for them, and re-layouts  15.4 us (6%)
  between operations  14.3 us (6%)
  blocking collectives  12.8 us (5%)
  other arithmetic  4.14 us (2%)
    reduce_scatter x1, waiting for transfers between devices, local(): lax.psum_scatter(partial_terms, 'mp', scatter_dimension=1, tiled=True)  72.5 us
    all_gather x1, waiting for transfers between devices, local(): lax.all_gather(out_weight, 'seq', axis=1, tiled=True)  22.7 us
    all_to_all x1, waiting for transfers between devices, local(): lax.all_to_all(v_time, 'seq', split_axis=1, concat_axis=0, tiled=True)  14.4 us
    psum x1, blocking collectives, local(): total_squares = lax.psum(local_squares, 'mp')  12.8 us
    all_to_all x1, waiting for transfers between devices, local(): lax.all_to_all(k_time, 'seq', split_axis=1, concat_axis=0, tiled=True)  12.7 us
    all_to_all x1, waiting for transfers between devices, local(): lax.all_to_all(q_time, 'seq', split_axis=1, concat_axis=0, tiled=True)  12.2 us
    all_to_all x1, starting transfers between devices, local(): lax.all_to_all(q_time, 'seq', split_axis=1, concat_axis=0, tiled=True)  11.7 us
    dot_general x1, matrix products, local(): jnp.dot(attended, lax.all_gather(out_weight, 'seq', axis=1, tiled=True),...  11.6 us
  transfers between devices with their start and end apart: 6, of which 6 were waited for; matrix products, arithmetic and copies ran while one was open for 9% of the time, Pallas kernels for 0%

commit v1 on v0

v1 whole, which is shorter than its diff:
```python
import functools
import math

import jax
import jax.numpy as jnp
from jax import lax
from jax.experimental import pallas as pl
from jax.experimental.pallas import tpu as pltpu
from jax.sharding import PartitionSpec as P

D = 6144
HD = 128
S = 128
FR = 4
X, Y, Z, CORES = 4, 4, 8, 2
ROWS = FR * S
COLS = D // (X * CORES)
HALF = COLS // 2
WB = D // (Y * Z)
GROUP = 16
eps = 1e-06
negative = -1e30
NT = (((1,), (1,)), ((), ()))
VM = 60 * 1024 * 1024


def seq_perm(dy, dz):
    return [
        (y * Z + z, (y + dy) % Y * Z + (z + dz) % Z) for y in range(Y) for z in range(Z)
    ]


def ring_perm(d):
    n = Y * Z
    return [(i, (i + d) % n) for i in range(n)]


def mp_perm(dx, dc):
    return [
        (x * CORES + c, (x + dx) % X * CORES + (c + dc) % CORES)
        for x in range(X)
        for c in range(CORES)
    ]


def swap_perm():
    pairs = []
    for x in range(X):
        for y in range(Y):
            for z in range(Z):
                for c in range(CORES):
                    src = (y * Z + z) * X * CORES + x * CORES + c
                    dst = (x * Z + z) * X * CORES + y * CORES + c
                    pairs.append((src, dst))
    return pairs


def seq_move(a, dy, dz):
    return lax.ppermute(a, "seq", seq_perm(dy, dz))


def mp_move(a, dx, dc=0):
    return lax.ppermute(a, "mp", mp_perm(dx, dc))


def clip_index(frame_counts, frame_ids):
    ends = jnp.cumsum(frame_counts)
    return jnp.sum((ends[None, :] <= frame_ids[:, None]).astype(jnp.int32), axis=1)


def cost(flops, nbytes):
    return pl.CostEstimate(flops=flops, bytes_accessed=nbytes, transcendentals=0)


def pack_kv_kernel(k_ref, v_ref, o_ref):
    o_ref[0] = k_ref[...]
    o_ref[1] = v_ref[...]


def pack_kv(keys, values):
    return pl.pallas_call(
        pack_kv_kernel,
        grid=(3,),
        in_specs=[pl.BlockSpec((ROWS, HD), lambda j: (0, 2 * j + 1))] * 2,
        out_specs=pl.BlockSpec((2, ROWS, HD), lambda j: (0, 0, j)),
        out_shape=jax.ShapeDtypeStruct((2, ROWS, HALF), jnp.bfloat16),
        cost_estimate=cost(0, 4 * ROWS * HALF * 2),
        name="pack_kv",
    )(keys, values)


def pack_w_kernel(w_ref, o_ref):
    for j in range(COLS // HD):
        at = (j // 2) * HD + (j % 2) * HALF
        o_ref[:, at : at + HD] = w_ref[j * HD : (j + 1) * HD, :].T


def pack_w(weight):
    return pl.pallas_call(
        pack_w_kernel,
        out_shape=jax.ShapeDtypeStruct((WB, COLS), jnp.bfloat16),
        cost_estimate=cost(0, 2 * WB * COLS * 2),
        name="pack_w",
    )(weight)


def softmax_weights(scores):
    highest = jnp.max(scores, axis=-1, keepdims=True)
    raised = jnp.exp(scores - highest)
    return (raised / jnp.sum(raised, axis=-1, keepdims=True)).astype(jnp.bfloat16)


def even_kernel(grid_ref, q_ref, k_ref, v_ref, o_ref):
    count = grid_ref[pl.program_id(0)]
    key_live = lax.broadcasted_iota(jnp.int32, (S, S), 1) < count
    row_live = lax.broadcasted_iota(jnp.int32, (S, HD), 0) < count
    for h in range(3):
        at = slice(2 * h * HD, (2 * h + 1) * HD)
        scores = lax.dot_general(
            q_ref[:, at], k_ref[:, at], NT, preferred_element_type=jnp.float32
        ) * (1.0 / math.sqrt(HD))
        weights = softmax_weights(jnp.where(key_live, scores, negative))
        out = jnp.dot(weights, v_ref[:, at], preferred_element_type=jnp.float32)
        o_ref[:, h * HD : (h + 1) * HD] = jnp.where(row_live, out, 0.0).astype(jnp.bfloat16)


def even_attention(own_grid, queries, keys, values):
    block = pl.BlockSpec((S, COLS), lambda f, g: (f, 0))
    return pl.pallas_call(
        even_kernel,
        grid_spec=pltpu.PrefetchScalarGridSpec(
            num_scalar_prefetch=1,
            grid=(FR,),
            in_specs=[block] * 3,
            out_specs=pl.BlockSpec((S, HALF), lambda f, g: (f, 0)),
        ),
        out_shape=jax.ShapeDtypeStruct((ROWS, HALF), jnp.bfloat16),
        cost_estimate=cost(FR * 3 * 4 * S * S * HD, 4 * ROWS * COLS * 2),
        name="even_attention",
    )(own_grid, queries, keys, values)


WINDOW = 18


def odd_kernel(grid_ref, mask_ref, q_ref, k_ref, v_ref, l1_ref, r1_ref, l2_ref, r2_ref, o_ref):
    base = pl.program_id(0) * GROUP
    allowed = mask_ref[...] > 0.5
    cell = base + lax.broadcasted_iota(jnp.int32, (GROUP, HD), 0)
    for h in range(3):
        wide = slice((2 * h + 1) * HD, (2 * h + 2) * HD)
        at = slice(h * HD, (h + 1) * HD)

        def window(own_ref, which):
            parts = [
                own_ref[:, :, wide],
                l1_ref[which, :, :, at],
                r1_ref[which, :, :, at],
                l2_ref[which, :, :, at],
                r2_ref[which, :, :, at],
            ]
            return jnp.concatenate([p.reshape(-1, HD) for p in parts], axis=0)

        q = q_ref[:, :, wide].reshape(FR * GROUP, HD)
        scores = lax.dot_general(
            q, window(k_ref, 0), NT, preferred_element_type=jnp.float32
        ) * (1.0 / math.sqrt(HD))
        weights = softmax_weights(jnp.where(allowed, scores, negative))
        out = jnp.dot(weights, window(v_ref, 1), preferred_element_type=jnp.float32)
        for f in range(FR):
            part = jnp.where(cell < grid_ref[f], out[f * GROUP : (f + 1) * GROUP], 0.0)
            o_ref[f, :, at] = part.astype(jnp.bfloat16)


def odd_attention(own_grid, mask, queries, keys, values, left1, right1, left2, right2):
    def frames(a):
        return a.reshape(FR, S, COLS)

    own = pl.BlockSpec((FR, GROUP, COLS), lambda i, g: (0, i, 0))
    near = pl.BlockSpec((2, FR, GROUP, HALF), lambda i, g: (0, 0, i, 0))
    far = pl.BlockSpec((2, FR - 1, GROUP, HALF), lambda i, g: (0, 0, i, 0))
    out = pl.pallas_call(
        odd_kernel,
        grid_spec=pltpu.PrefetchScalarGridSpec(
            num_scalar_prefetch=1,
            grid=(S // GROUP,),
            in_specs=[
                pl.BlockSpec((FR * GROUP, WINDOW * GROUP), lambda i, g: (0, 0)),
                own,
                own,
                own,
                near,
                near,
                far,
                far,
            ],
            out_specs=pl.BlockSpec((FR, GROUP, HALF), lambda i, g: (0, i, 0)),
        ),
        out_shape=jax.ShapeDtypeStruct((FR, S, HALF), jnp.bfloat16),
        cost_estimate=cost(ROWS * 3 * 4 * WINDOW * GROUP * HD, 10 * ROWS * COLS * 2),
        name="odd_attention",
    )(own_grid, mask, frames(queries), frames(keys), frames(values), left1, right1, left2, right2)
    return out.reshape(ROWS, HALF)


def project_kernel(w_places, out_type, place_ref, *refs):
    a_refs = refs[:8]
    w_refs = refs[8 : 8 + len(w_places)]
    o_ref, a_buf, w_buf, acc, a_sem, w_sem = refs[8 + len(w_places) :]
    x, y, z, half = place_ref[0], place_ref[1], place_ref[2], place_ref[3]
    for r in range(X):
        slot = lax.rem(x + r, X)
        for part in range(2):
            pltpu.make_async_copy(
                a_refs[2 * r + part],
                a_buf.at[slot, :, part * HALF : (part + 1) * HALF],
                a_sem.at[slot],
            ).start()
    for ref, blocks in zip(w_refs, w_places):
        start = 0
        for dy, dz, first, rows in blocks:
            slot = lax.rem(y + dy + Y, Y)
            column = lax.rem(z + dz + Z, Z)
            at = pl.multiple_of(lax.rem(column, Z // 2) * WB + first, 32)
            source = ref.at[start : start + rows]

            @pl.when(column // (Z // 2) == half)
            def _(source=source, slot=slot, at=at, rows=rows):
                pltpu.make_async_copy(
                    source, w_buf.at[slot, pl.ds(at, rows)], w_sem.at[slot]
                ).start()

            start += rows
    acc[...] = jnp.zeros_like(acc)

    @pl.loop(0, Y)
    def _(j):
        pltpu.make_async_copy(a_buf.at[j], a_buf.at[j], a_sem.at[j]).wait()
        pltpu.make_async_copy(w_buf.at[j], w_buf.at[j], w_sem.at[j]).wait()
        acc[...] += lax.dot_general(
            a_buf[j], w_buf[j], NT, preferred_element_type=jnp.float32
        )

    o_ref[...] = acc[...].astype(out_type)


def project(place, a_parts, w_parts, w_places, out_type):
    hbm = pl.BlockSpec(memory_space=pl.ANY)
    return pl.pallas_call(
        functools.partial(project_kernel, w_places, out_type),
        grid_spec=pltpu.PrefetchScalarGridSpec(
            num_scalar_prefetch=1,
            grid=(1,),
            in_specs=[hbm] * (len(a_parts) + len(w_parts)),
            out_specs=pl.BlockSpec((ROWS, COLS), lambda i, p: (0, 0)),
            scratch_shapes=[
                pltpu.VMEM((X, ROWS, COLS), jnp.bfloat16),
                pltpu.VMEM((Y, COLS, COLS), jnp.bfloat16),
                pltpu.VMEM((ROWS, COLS), jnp.float32),
                pltpu.SemaphoreType.DMA((X,)),
                pltpu.SemaphoreType.DMA((Y,)),
            ],
        ),
        out_shape=jax.ShapeDtypeStruct((ROWS, COLS), out_type),
        compiler_params=pltpu.CompilerParams(vmem_limit_bytes=32 * 1024 * 1024),
        cost_estimate=cost(2 * ROWS * COLS * COLS * 4, 9 * 1024 * 1024),
        name="project",
    )(place, *a_parts, *w_parts)


def update_kernel(own_ref, other_ref, residual_ref, gate_ref, u_ref, sq_ref):
    total = own_ref[...] + other_ref[...].astype(jnp.float32)
    combined = residual_ref[...].astype(jnp.float32) + gate_ref[0] * total
    updated = combined.astype(jnp.bfloat16)
    u_ref[...] = updated
    wide = updated.astype(jnp.float32)
    squares = wide * wide
    folded = squares[:, :HD]
    for j in range(1, COLS // HD):
        folded = folded + squares[:, j * HD : (j + 1) * HD]
    sq_ref[0] = jnp.sum(folded.T, axis=0, keepdims=True)


def update(own, other, residual, gate_rows):
    block = pl.BlockSpec((S, COLS), lambda f: (f, 0))
    return pl.pallas_call(
        update_kernel,
        grid=(FR,),
        in_specs=[block, block, block, pl.BlockSpec((1, 1, COLS), lambda f: (f, 0, 0))],
        out_specs=[block, pl.BlockSpec((1, 1, S), lambda f: (f, 0, 0))],
        out_shape=[
            jax.ShapeDtypeStruct((ROWS, COLS), jnp.bfloat16),
            jax.ShapeDtypeStruct((FR, 1, S), jnp.float32),
        ],
        cost_estimate=cost(0, ROWS * COLS * 10),
        name="update",
    )(own, other, residual, gate_rows)


def norm_kernel(u_ref, s0_ref, s1_ref, s2_ref, s3_ref, scale_ref, shift_ref, o_ref):
    total = s0_ref[0] + s1_ref[0] + s2_ref[0] + s3_ref[0]
    inverse = lax.rsqrt(total * (1.0 / D) + eps)
    inverse = jnp.broadcast_to(inverse, (S, S)).T
    for j in range(COLS // HD):
        at = slice(j * HD, (j + 1) * HD)
        wide = u_ref[:, at].astype(jnp.float32)
        normed = wide * inverse * (1.0 + scale_ref[0, :, at]) + shift_ref[0, :, at]
        o_ref[:, at] = normed.astype(jnp.bfloat16)


def norm(updated, sums, scale_rows, shift_rows):
    block = pl.BlockSpec((S, COLS), lambda f: (f, 0))
    row = pl.BlockSpec((1, 1, COLS), lambda f: (f, 0, 0))
    lane = pl.BlockSpec((1, 1, S), lambda f: (f, 0, 0))
    return pl.pallas_call(
        norm_kernel,
        grid=(FR,),
        in_specs=[block, lane, lane, lane, lane, row, row],
        out_specs=block,
        out_shape=jax.ShapeDtypeStruct((ROWS, COLS), jnp.bfloat16),
        cost_estimate=cost(0, ROWS * COLS * 4),
        name="norm",
    )(updated, *sums, scale_rows, shift_rows)


def gather_weight(weight):
    parts, places = [], []

    def keep(a, *blocks):
        parts.append(a)
        places.append(tuple(blocks))

    def whole(dy, dz):
        return (dy, dz, 0, WB)

    own = lax.ppermute(pack_w(weight), ("seq", "mp"), swap_perm())
    far = seq_move(own, 2, 0)
    pair = jnp.concatenate([own, far], axis=0)
    keep(pair, whole(0, 0), whole(2, 0))
    up, down = seq_move(own, 1, 0), seq_move(own, -1, 0)
    keep(up, whole(-1, 0))
    keep(down, whole(1, 0))
    right1, left1 = seq_move(pair, 0, 1), seq_move(pair, 0, -1)
    keep(right1, whole(0, -1), whole(2, -1))
    keep(left1, whole(0, 1), whole(2, 1))
    chunk = jnp.concatenate([right1[:WB], left1[:WB]], axis=0)
    up, down = seq_move(chunk, 1, 0), seq_move(chunk, -1, 0)
    keep(up, whole(-1, -1), whole(-1, 1))
    keep(down, whole(1, -1), whole(1, 1))
    right2, left2 = seq_move(right1, 0, 1), seq_move(left1, 0, -1)
    keep(right2, whole(0, -2), whole(2, -2))
    keep(left2, whole(0, 2), whole(2, 2))
    chunk = jnp.concatenate([right2[:WB], left2[:WB]], axis=0)
    up, down = seq_move(chunk, 1, 0), seq_move(chunk, -1, 0)
    keep(up, whole(-1, -2), whole(-1, 2))
    keep(down, whole(1, -2), whole(1, 2))
    right3, left3 = seq_move(right2[:WB], 0, 1), seq_move(left2[:WB], 0, -1)
    keep(right3, whole(0, -3))
    keep(left3, whole(0, 3))
    right4 = seq_move(right3, 0, 1)
    keep(right4, whole(0, -4))
    chunk = jnp.concatenate([right3, left3, right4], axis=0)
    up, down = seq_move(chunk, 1, 0), seq_move(chunk, -1, 0)
    keep(up, whole(-1, -3), whole(-1, 3), whole(-1, -4))
    keep(down, whole(1, -3), whole(1, 3), whole(1, -4))
    h = WB // 2
    first = jnp.concatenate([down[:WB], down[2 * WB : 2 * WB + h]], axis=0)
    second = jnp.concatenate([up[WB : 2 * WB], up[2 * WB + h :]], axis=0)
    keep(seq_move(first, -1, 0), whole(2, -3), (2, -4, 0, h))
    keep(seq_move(second, 1, 0), whole(2, 3), (2, -4, h, h))
    return parts, places


def gather_x(a):
    return [a, mp_move(a, -1), mp_move(a, 2), mp_move(a, 1)]


def local(
    queries,
    keys,
    values,
    residual,
    out_weight,
    gate,
    mod_scale,
    mod_shift,
    frame_counts,
    patch_counts,
):
    s = lax.axis_index("seq")
    m = lax.axis_index("mp")
    x, core = m // CORES, m % CORES
    y, z = s // Z, s % Z
    clip_total = frame_counts.shape[0]

    kv = pack_kv(keys, values).reshape(2, FR, S, HALF)
    from_left = lax.ppermute(kv, "seq", ring_perm(1))
    from_right = lax.ppermute(kv, "seq", ring_perm(-1))
    from_left2 = lax.ppermute(from_left[:, 1:], "seq", ring_perm(1))
    from_right2 = lax.ppermute(from_right[:, : FR - 1], "seq", ring_perm(-1))
    w_parts, w_places = gather_weight(out_weight)

    first = s * FR
    own_ids = first + jnp.arange(FR, dtype=jnp.int32)
    own_clips = clip_index(frame_counts, own_ids)
    hot = own_clips[:, None] == jnp.arange(clip_total, dtype=jnp.int32)[None, :]
    own_grid = jnp.sum(jnp.where(hot, patch_counts[None, :], 0), axis=1)
    rel = [0, 1, 2, 3, -4, -3, -2, -1, 4, 5, 6, 7, -7, -6, -5, 8, 9, 10]
    key_ids = first + jnp.array(rel, dtype=jnp.int32)
    inside = (key_ids >= 0) & (key_ids < FR * Y * Z)
    key_clips = jnp.where(inside, clip_index(frame_counts, key_ids), -1)
    same_clip = own_clips[:, None] == key_clips[None, :]
    cells = jnp.arange(GROUP, dtype=jnp.int32)
    mask = same_clip[:, None, :, None] & (cells[None, :, None, None] == cells[None, None, None, :])
    mask = mask.astype(jnp.float32).reshape(FR * GROUP, WINDOW * GROUP)

    even = even_attention(own_grid, queries, keys, values)
    even_parts = gather_x(even)
    odd = odd_attention(
        own_grid, mask, queries, keys, values, from_left, from_right, from_left2, from_right2
    )
    odd_parts = gather_x(odd)
    a_parts = [a for pair in zip(even_parts, odd_parts) for a in pair]

    other_place = jnp.stack([x, y, z, 1 - core]).astype(jnp.int32)
    own_place = jnp.stack([x, y, z, core]).astype(jnp.int32)
    other_half = project(other_place, a_parts, w_parts, w_places, jnp.bfloat16)
    swapped = mp_move(other_half, 0, 1)
    own_half = project(own_place, a_parts, w_parts, w_places, jnp.float32)

    hot = hot.astype(jnp.bfloat16)

    def lookup(table):
        rows = jnp.dot(hot, table, preferred_element_type=jnp.float32)
        return rows.reshape(FR, 1, COLS)

    updated, squares = update(own_half, swapped, residual, lookup(gate))
    squares = squares + mp_move(squares, 0, 1)
    sums = gather_x(squares)
    normed = norm(updated, sums, lookup(mod_scale), lookup(mod_shift))
    return updated, normed


def solution(mesh):
    in_specs = (
        P("seq", "mp"),
        P("seq", "mp"),
        P("seq", "mp"),
        P("seq", "mp"),
        P("mp", "seq"),
        P(None, "mp"),
        P(None, "mp"),
        P(None, "mp"),
        P(),
        P(),
    )
    out_specs = (P("seq", "mp"), P("seq", "mp"))
    return jax.shard_map(local, mesh=mesh, in_specs=in_specs, out_specs=out_specs, check_vma=False)
```

time: 244 us -> 228 us (0.934)
  waiting for transfers between devices: 147 us -> 84.2 us
  Pallas kernels: 0 us -> 42.6 us
  starting transfers between devices: 32.8 us -> 58.8 us
  matrix products: 16.7 us -> 0.56 us
  local copies, waits for them, and re-layouts: 15.4 us -> 30.2 us
  between operations: 14.3 us -> 1.03 us
  blocking collectives: 12.8 us -> 0 us
  other arithmetic: 4.14 us -> 7.52 us
    ppermute x0 -> x34, waiting for transfers between devices: none -> 84.2 us  [the longest x18 62.5 us: seq_move(): return lax.ppermute(a, 'seq', seq_perm(dy, dz))]
    reduce_scatter x1 -> x0, waiting for transfers between devices: 72.5 us -> none  [local(): lax.psum_scatter(partial_terms, 'mp', scatter_dimension=1, tiled=True)]
    ppermute x0 -> x34, starting transfers between devices: none -> 58.8 us  [the longest x18 34.6 us: seq_move(): return lax.ppermute(a, 'seq', seq_perm(dy, dz))]
    all_to_all x4 -> x0, waiting for transfers between devices: 50.9 us -> none  [the longest x1 14.4 us: local(): lax.all_to_all(v_time, 'seq', split_axis=1, concat_axis=0, tiled=True)]
    pallas_call x0 -> x8, Pallas kernels: none -> 42.6 us  [the longest x1 11.8 us: odd_attention(): pl.pallas_call(odd_kernel, grid_spec=pltpu.PrefetchScalarGridSpec(num_sca...]
    all_to_all x4 -> x0, starting transfers between devices: 32.6 us -> none  [the longest x1 11.7 us: local(): lax.all_to_all(q_time, 'seq', split_axis=1, concat_axis=0, tiled=True)]
    all_gather x1 -> x0, waiting for transfers between devices: 22.7 us -> none  [local(): lax.all_gather(out_weight, 'seq', axis=1, tiled=True)]
    unnamed x22 -> x96, local copies, waits for them, and re-layouts: 0.62 us -> 21.5 us
  transfers between devices with their start and end apart: 6 -> 34, of which waited for: 6 -> 16; matrix products, arithmetic and copies ran while one was open for 9% -> 8% of each run, Pallas kernels for 0% -> 12%
where the time goes in v1:
time: 228 us; the launch traced here: 225 us
  waiting for transfers between devices  84.2 us (37%)
  starting transfers between devices  58.8 us (26%)
  Pallas kernels  42.6 us (19%)
  local copies, waits for them, and re-layouts  30.2 us (13%)
  other arithmetic  7.52 us (3%)
    ppermute x18, waiting for transfers between devices, seq_move(): return lax.ppermute(a, 'seq', seq_perm(dy, dz))  62.5 us
    ppermute x18, starting transfers between devices, seq_move(): return lax.ppermute(a, 'seq', seq_perm(dy, dz))  34.6 us
    unnamed x96, local copies, waits for them, and re-layouts  21.5 us
    ppermute x1, waiting for transfers between devices, gather_weight(): own = lax.ppermute(pack_w(weight), ('seq', 'mp'), swap_perm())  13.3 us
    pallas_call x1, Pallas kernels, odd_attention(): pl.pallas_call(odd_kernel, grid_spec=pltpu.PrefetchScalarGridSpec(num_sca...  11.8 us
    pallas_call x2, Pallas kernels, project(): pl.pallas_call(functools.partial(project_kernel, w_places, out_type), gri...  11.6 us
    ppermute x11, starting transfers between devices, mp_move(): return lax.ppermute(a, 'mp', mp_perm(dx, dc))  11.2 us
    ppermute x11, waiting for transfers between devices, mp_move(): return lax.ppermute(a, 'mp', mp_perm(dx, dc))  8.37 us
  transfers between devices with their start and end apart: 34, of which 16 were waited for; matrix products, arithmetic and copies ran while one was open for 8% of the time, Pallas kernels for 12%

profile of v1, /device:TPU:8, one launch (start us, length us, event | category | flops | bytes accessed | tf_op | source)
XLA Modules:
  0.0 224.9 jit_solution(1449023646679939235)
XLA Ops:
  0.6 1.9 copy.20.w_ref
  2.5 1.9 pack_w.1
  4.4 3.3 %collective-permute-start.10 = (bf16[192,768]{1,0:T(8,128)(2,1)}, bf16[192,768]{1,0:T(8,128)(2,1)}, u32[]{:S(2)}, u32[]{:S(2)}) collective-permute-start(bf16[192,768]{1,0:T(8,128)(2,1)} %pack_w.1), channel_id=1, source_target_pairs={{0,0},{1,1},{8,8},{9,9},{16,16},{17,17},{24,24},{25,25},{32,32},{3... | collective-permute-start | bytes 884744 | tf_op jit(solution)/shard_map/ppermute | solution.py:336
  7.7 13.3 %collective-permute-done.10 = bf16[192,768]{1,0:T(8,128)(2,1)} collective-permute-done((bf16[192,768]{1,0:T(8,128)(2,1)}, bf16[192,768]{1,0:T(8,128)(2,1)}, u32[]{:S(2)}, u32[]{:S(2)}) %collective-permute-start.10) | collective-permute-done | bytes 294944 | tf_op jit(solution)/shard_map/ppermute | solution.py:336
  21.0 6.3 %collective-permute-start.11 = (bf16[192,768]{1,0:T(8,128)(2,1)}, bf16[192,768]{1,0:T(8,128)(2,1)S(1)}, u32[]{:S(2)}, u32[]{:S(2)}) collective-permute-start(bf16[192,768]{1,0:T(8,128)(2,1)} %collective-permute-done.10), channel_id=1, source_target_pairs={{0,128},{8,136},{16,144},{24,152},{32,160},{40,168},{48,176},{56,1... | collective-permute-start | bytes 884744 | tf_op jit(solution)/shard_map/ppermute | solution.py:59
  27.3 1.0 constant_dynamic-update-slice_fusion.1
  28.3 5.9 %collective-permute-done.11 = bf16[192,768]{1,0:T(8,128)(2,1)S(1)} collective-permute-done((bf16[192,768]{1,0:T(8,128)(2,1)}, bf16[192,768]{1,0:T(8,128)(2,1)S(1)}, u32[]{:S(2)}, u32[]{:S(2)}) %collective-permute-start.11) | collective-permute-done | bytes 294944 | tf_op jit(solution)/shard_map/ppermute | solution.py:59
  34.2 2.0 collective-permute-start.14
  36.2 4.0 %collective-permute-start.15 = (bf16[384,768]{1,0:T(8,128)(2,1)S(1)}, bf16[384,768]{1,0:T(8,128)(2,1)S(1)}, u32[]{:S(2)}, u32[]{:S(2)}) collective-permute-start(bf16[384,768]{1,0:T(8,128)(2,1)S(1)} %constant_dynamic-update-slice_fusion.refs_8_), channel_id=1, source_target_pairs={{0,56},{8,0},{16,8},{24,16},{32,24},{40,32},{48,40},{56,48},{64,12... | collective-permute-start | bytes 1769480 | tf_op jit(solution)/shard_map/ppermute | solution.py:59
  40.3 12.3 %collective-permute-done.14.refs_11_ = bf16[384,768]{1,0:T(8,128)(2,1)S(1)} collective-permute-done((bf16[384,768]{1,0:T(8,128)(2,1)S(1)}, bf16[384,768]{1,0:T(8,128)(2,1)S(1)}, u32[]{:S(2)}, u32[]{:S(2)}) %collective-permute-start.14) | collective-permute-done | bytes 589856 | tf_op jit(solution)/shard_map/ppermute | solution.py:59
  52.6 2.9 %pack_kv.1 = bf16[2,512,384]{2,1,0:T(8,128)(2,1)} custom-call(bf16[512,768]{1,0:T(8,128)(2,1)} %k_ref.3, bf16[512,768]{1,0:T(8,128)(2,1)} %v_ref.3), custom_call_target="tpu_custom_call" | custom-call | bytes 1572864 | tf_op jit(solution)/shard_map/pack_kv/pallas_call | solution.py:81
  55.5 4.1 %collective-permute-start.1 = (bf16[2,4,128,384]{3,2,1,0:T(8,128)(2,1)}, bf16[2,4,128,384]{3,2,1,0:T(8,128)(2,1)}, u32[]{:S(2)}, u32[]{:S(2)}) collective-permute-start(bf16[2,4,128,384]{3,2,1,0:T(8,128)(2,1)} %bitcast.25), channel_id=1, source_target_pairs={{0,248},{8,0},{16,8},{24,16},{32,24},{40,32},{48,40},{56,48},{64,5... | collective-permute-start | bytes 2359304 | tf_op jit(solution)/shard_map/ppermute | solution.py:398
  59.6 1.1 collective-permute-start.19
  62.0 7.0 %even_attention.1.refs_0_ = bf16[512,384]{1,0:T(8,128)(2,1)} custom-call(s32[4]{0:T(128)} %select_reduce_fusion.grid_ref, bf16[512,768]{1,0:T(8,128)(2,1)} %q_ref.1, bf16[512,768]{1,0:T(8,128)(2,1)} %k_ref.3, bf16[512,768]{1,0:T(8,128)(2,1)} %v_ref.3), custom_call_target="tpu_custom_call" | custom-call | flops 100663296 | bytes 3145728 | tf_op jit(solution)/shard_map/even_attention/pallas_call | solution.py:129
  69.2 0.9 collective-permute-done.18.refs_15_
  70.1 1.2 collective-permute-start.22
  71.3 16.1 %collective-permute-done.19.refs_16_ = bf16[384,768]{1,0:T(8,128)(2,1)S(1)} collective-permute-done((bf16[384,768]{1,0:T(8,128)(2,1)S(1)}, bf16[384,768]{1,0:T(8,128)(2,1)S(1)}, u32[]{:S(2)}, u32[]{:S(2)}) %collective-permute-start.19) | collective-permute-done | bytes 589856 | tf_op jit(solution)/shard_map/ppermute | solution.py:59
  87.5 3.8 %collective-permute-start.23 = (bf16[192,768]{1,0:T(8,128)(2,1)S(1)}, bf16[192,768]{1,0:T(8,128)(2,1)S(1)}, u32[]{:S(2)}, u32[]{:S(2)}) collective-permute-start(bf16[192,768]{1,0:T(8,128)(2,1)S(1)} %slice.47), channel_id=1, source_target_pairs={{0,56},{8,0},{16,8},{24,16},{32,24},{40,32},{48,40},{56,48},{64,12... | collective-permute-start | bytes 884744 | tf_op jit(solution)/shard_map/ppermute | solution.py:59
  91.6 1.1 slice.42
  93.6 1.1 slice.43
  95.5 5.5 %collective-permute-start.3 = (bf16[2,3,128,384]{3,2,1,0:T(8,128)(2,1)S(1)}, bf16[2,3,128,384]{3,2,1,0:T(8,128)(2,1)}, u32[]{:S(2)}, u32[]{:S(2)}) collective-permute-start(bf16[2,3,128,384]{3,2,1,0:T(8,128)(2,1)S(1)} %slice.43), channel_id=1, source_target_pairs={{0,248},{8,0},{16,8},{24,16},{32,24},{40,32},{48,40},{56,48},{64,5... | collective-permute-start | bytes 1769480 | tf_op jit(solution)/shard_map/ppermute | solution.py:400
  102.5 9.9 %collective-permute-done.24.refs_21_ = bf16[192,768]{1,0:T(8,128)(2,1)S(1)} collective-permute-done((bf16[192,768]{1,0:T(8,128)(2,1)S(1)}, bf16[192,768]{1,0:T(8,128)(2,1)S(1)}, u32[]{:S(2)}, u32[]{:S(2)}) %collective-permute-start.24) | collective-permute-done | bytes 294944 | tf_op jit(solution)/shard_map/ppermute | solution.py:59
  114.0 2.2 collective-permute-start.25
  117.1 2.5 %collective-permute-start.12 = (bf16[192,768]{1,0:T(8,128)(2,1)}, bf16[192,768]{1,0:T(8,128)(2,1)}, u32[]{:S(2)}, u32[]{:S(2)}) collective-permute-start(bf16[192,768]{1,0:T(8,128)(2,1)} %collective-permute-done.10), channel_id=1, source_target_pairs={{0,64},{8,72},{16,80},{24,88},{32,96},{40,104},{48,112},{56,120},{... | collective-permute-start | bytes 884744 | tf_op jit(solution)/shard_map/ppermute | solution.py:59
  120.3 1.0 and_convert_fusion
  121.2 1.3 reshape.114
  124.8 11.8 %odd_attention.1 = bf16[4,128,384]{2,1,0:T(8,128)(2,1)} custom-call(s32[4]{0:T(128)} %select_reduce_fusion.grid_ref, f32[64,288]{1,0:T(8,128)} %copy.19.mask_ref, bf16[4,128,768]{2,1,0:T(8,128)(2,1)} %bitcast.23, bf16[4,128,768]{2,1,0:T(8,128)(2,1)} %bitcast.21, bf16[4,128,768]{2,1,0:T(8,128)(2,1)} %bitcast.22, ...), custom_call_target="tpu_custom_call" | custom-call | flops 226492416 | bytes 7864320 | tf_op jit(solution)/shard_map/odd_attention/pallas_call | solution.py:182
  136.6 2.7 %collective-permute-start.5 = (bf16[512,384]{1,0:T(8,128)(2,1)}, bf16[512,384]{1,0:T(8,128)(2,1)S(1)}, u32[]{:S(2)}, u32[]{:S(2)}) collective-permute-start(bf16[512,384]{1,0:T(8,128)(2,1)} %bitcast.16), channel_id=1, source_target_pairs={{0,6},{1,7},{2,0},{3,1},{4,2},{5,3},{6,4},{7,5},{8,14},{9,15},{10,... | collective-permute-start | bytes 1179656 | tf_op jit(solution)/shard_map/ppermute | solution.py:63
  139.3 2.0 collective-permute-start.7
  141.3 1.9 pad_maximum_fusion
  143.2 1.8 collective-permute-start.16
  145.8 0.9 pad_maximum_fusion.1
  146.7 4.8 %collective-permute-done.5.refs_3_ = bf16[512,384]{1,0:T(8,128)(2,1)S(1)} collective-permute-done((bf16[512,384]{1,0:T(8,128)(2,1)}, bf16[512,384]{1,0:T(8,128)(2,1)S(1)}, u32[]{:S(2)}, u32[]{:S(2)}) %collective-permute-start.5) | collective-permute-done | bytes 393248 | tf_op jit(solution)/shard_map/ppermute | solution.py:63
  151.4 2.9 %collective-permute-start.17 = (bf16[384,768]{1,0:T(8,128)(2,1)}, bf16[384,768]{1,0:T(8,128)(2,1)}, u32[]{:S(2)}, u32[]{:S(2)}) collective-permute-start(bf16[384,768]{1,0:T(8,128)(2,1)} %pad_maximum_fusion), channel_id=1, source_target_pairs={{0,192},{8,200},{16,208},{24,216},{32,224},{40,232},{48,240},{56,2... | collective-permute-start | bytes 1769480 | tf_op jit(solution)/shard_map/ppermute | solution.py:59
  154.4 2.0 collective-permute-start.21
  158.9 1.9 collective-permute-done.16.refs_13_
  160.9 0.8 copy-done.18
  161.7 3.2 %collective-permute-start.27 = (bf16[288,768]{1,0:T(8,128)(2,1)}, bf16[288,768]{1,0:T(8,128)(2,1)}, u32[]{:S(2)}, u32[]{:S(2)}) collective-permute-start(bf16[288,768]{1,0:T(8,128)(2,1)} %pad_maximum_fusion.2), channel_id=1, source_target_pairs={{0,192},{8,200},{16,208},{24,216},{32,224},{40,232},{48,240},{56,2... | collective-permute-start | bytes 1327112 | tf_op jit(solution)/shard_map/ppermute | solution.py:59
  165.0 3.4 %collective-permute-done.17.refs_14_ = bf16[384,768]{1,0:T(8,128)(2,1)} collective-permute-done((bf16[384,768]{1,0:T(8,128)(2,1)}, bf16[384,768]{1,0:T(8,128)(2,1)}, u32[]{:S(2)}, u32[]{:S(2)}) %collective-permute-start.17) | collective-permute-done | bytes 589856 | tf_op jit(solution)/shard_map/ppermute | solution.py:59
  168.5 2.9 %collective-permute-done.20.refs_17_ = bf16[384,768]{1,0:T(8,128)(2,1)} collective-permute-done((bf16[384,768]{1,0:T(8,128)(2,1)}, bf16[384,768]{1,0:T(8,128)(2,1)}, u32[]{:S(2)}, u32[]{:S(2)}) %collective-permute-start.20) | collective-permute-done | bytes 589856 | tf_op jit(solution)/shard_map/ppermute | solution.py:59
  171.3 3.7 %collective-permute-done.21.refs_18_ = bf16[384,768]{1,0:T(8,128)(2,1)} collective-permute-done((bf16[384,768]{1,0:T(8,128)(2,1)}, bf16[384,768]{1,0:T(8,128)(2,1)}, u32[]{:S(2)}, u32[]{:S(2)}) %collective-permute-start.21) | collective-permute-done | bytes 589856 | tf_op jit(solution)/shard_map/ppermute | solution.py:59
  175.0 1.1 collective-permute-done.28.refs_25_
  176.1 3.7 %collective-permute-done.27.refs_24_ = bf16[288,768]{1,0:T(8,128)(2,1)} collective-permute-done((bf16[288,768]{1,0:T(8,128)(2,1)}, bf16[288,768]{1,0:T(8,128)(2,1)}, u32[]{:S(2)}, u32[]{:S(2)}) %collective-permute-start.27) | collective-permute-done | bytes 442400 | tf_op jit(solution)/shard_map/ppermute | solution.py:59
  179.7 1.1 copy-done.3
  180.8 1.1 copy-done.6
  181.9 1.1 copy-done.8
  182.9 1.0 copy-done.12
  183.9 1.0 copy-done.15
  184.8 1.0 copy-done.17
  185.8 1.1 copy-done.19
  186.9 1.0 copy-done.21
  187.9 1.0 copy-done.24
  188.9 1.0 copy-done.27
  189.9 1.0 copy-done.29
  190.9 1.0 copy-done.31
  191.9 5.7 %project.3 = bf16[512,768]{1,0:T(8,128)(2,1)S(1)} custom-call(s32[4]{0:T(128)S(1)} %get-tuple-element.6.place_ref, bf16[512,384]{1,0:T(8,128)(2,1)} %even_attention.1.refs_0_, bf16[512,384]{1,0:T(8,128)(2,1)S(1)} %bitcast.19, bf16[512,384]{1,0:T(8,128)(2,1)S(1)} %copy-done.21, bf16[512,384]{1,0:T(8,128)(2,1)S(1)} %copy-done.27, ...), custom_call_target="tpu_custom_call" | custom-call | flops 2415919104 | bytes 9437184 | tf_op jit(solution)/shard_map/project/pallas_call | solution.py:249
  198.6 5.9 %project.2.own_ref = f32[512,768]{1,0:T(8,128)S(1)} custom-call(s32[4]{0:T(128)S(1)} %pad_add_fusion.place_ref, bf16[512,384]{1,0:T(8,128)(2,1)} %even_attention.1.refs_0_, bf16[512,384]{1,0:T(8,128)(2,1)S(1)} %bitcast.20, bf16[512,384]{1,0:T(8,128)(2,1)S(1)} %copy-done.22, bf16[512,384]{1,0:T(8,128)(2,1)S(1)} %copy-done.27, ...), custom_call_target="tpu_custom_call" | custom-call | flops 2415919104 | bytes 9437184 | tf_op jit(solution)/shard_map/project/pallas_call | solution.py:249
  204.5 1.2 copy-done.1
  205.7 3.9 %update.1 = (bf16[512,768]{1,0:T(8,128)(2,1)}, f32[4,1,128]{2,1,0:T(1,128)}) custom-call(f32[512,768]{1,0:T(8,128)} %copy-done.1, bf16[512,768]{1,0:T(8,128)(2,1)} %collective-permute-done.29.other_ref, bf16[512,768]{1,0:T(8,128)(2,1)} %residual_ref.1, f32[4,1,768]{2,1,0:T(1,128)} %reshape.111.gate_ref), custom_call_target="tpu_custom_call" | custom-call | bytes 3932160 | tf_op jit(solution)/shard_map/update/pallas_call | solution.py:286
  210.1 0.9 collective-permute-done.30
  211.6 4.1 %collective-permute-start.31 = (f32[4,1,128]{2,1,0:T(1,128)S(1)}, f32[4,1,128]{2,1,0:T(1,128)S(1)}, u32[]{:S(2)}, u32[]{:S(2)}) collective-permute-start(f32[4,1,128]{2,1,0:T(1,128)S(1)} %add.34.s0_ref), channel_id=1, source_target_pairs={{0,6},{1,7},{2,0},{3,1},{4,2},{5,3},{6,4},{7,5},{8,14},{9,15},{10,... | collective-permute-start | bytes 6152 | tf_op jit(solution)/shard_map/ppermute | solution.py:63
  215.7 0.9 collective-permute-start.33
  218.1 2.7 %collective-permute-done.32.s2_ref = f32[4,1,128]{2,1,0:T(1,128)S(1)} collective-permute-done((f32[4,1,128]{2,1,0:T(1,128)S(1)}, f32[4,1,128]{2,1,0:T(1,128)S(1)}, u32[]{:S(2)}, u32[]{:S(2)}) %collective-permute-start.32) | collective-permute-done | bytes 2080 | tf_op jit(solution)/shard_map/ppermute | solution.py:63
  221.4 3.6 %norm.1 = bf16[512,768]{1,0:T(8,128)(2,1)} custom-call(bf16[512,768]{1,0:T(8,128)(2,1)} %get-tuple-element.2.u_ref, f32[4,1,128]{2,1,0:T(1,128)} %copy-done.37, f32[4,1,128]{2,1,0:T(1,128)} %copy-done.38, f32[4,1,128]{2,1,0:T(1,128)} %copy-done.39, f32[4,1,128]{2,1,0:T(1,128)} %copy-done.40, f32[4,1,768]{2,1,0:T(1,128)} %reshape.112.scale_ref, ...), custom_call_target="tpu_custom_call" | custom-call | bytes 1572864 | tf_op jit(solution)/shard_map/norm/pallas_call | solution.py:315
  (147 shorter events, 17.9 us)
Async XLA Ops:
  0.6 197.0 %copy-start = (bf16[32,768]{1,0:T(8,128)(2,1)S(1)}, bf16[32,768]{1,0:T(8,128)(2,1)}, u32[]{:S(2)}) copy-start(bf16[32,768]{1,0:T(8,128)(2,1)} %param.16) | copy-start | bytes 147460
  4.4 16.6 %collective-permute-start.10 = (bf16[192,768]{1,0:T(8,128)(2,1)}, bf16[192,768]{1,0:T(8,128)(2,1)}, u32[]{:S(2)}, u32[]{:S(2)}) collective-permute-start(bf16[192,768]{1,0:T(8,128)(2,1)} %pack_w.1), channel_id=1, source_target_pairs={{0,0},{1,1},{8,8},{9,9},{16,16},{17,17},{24,24},{25,25},{32,32},{3... | collective-permute-start | bytes 884744 | tf_op jit(solution)/shard_map/ppermute | solution.py:336
  21.0 13.2 %collective-permute-start.11 = (bf16[192,768]{1,0:T(8,128)(2,1)}, bf16[192,768]{1,0:T(8,128)(2,1)S(1)}, u32[]{:S(2)}, u32[]{:S(2)}) collective-permute-start(bf16[192,768]{1,0:T(8,128)(2,1)} %collective-permute-done.10), channel_id=1, source_target_pairs={{0,128},{8,136},{16,144},{24,152},{32,160},{40,168},{48,176},{56,1... | collective-permute-start | bytes 884744 | tf_op jit(solution)/shard_map/ppermute | solution.py:59
  34.2 21.3 %copy-start.7 = (bf16[384,768]{1,0:T(8,128)(2,1)}, bf16[384,768]{1,0:T(8,128)(2,1)S(1)}, u32[]{:S(2)}) copy-start(bf16[384,768]{1,0:T(8,128)(2,1)S(1)} %constant_dynamic-update-slice_fusion.refs_8_) | copy-start | bytes 1769476
  34.2 26.6 %copy-start.41 = (s32[32]{0:T(128)S(1)}, s32[32]{0:T(128)}, u32[]{:S(2)}) copy-start(s32[32]{0:T(128)} %param.19) | copy-start | bytes 388
  34.2 27.0 %copy-start.45 = (s32[32]{0:T(128)S(1)}, s32[32]{0:T(128)}, u32[]{:S(2)}) copy-start(s32[32]{0:T(128)} %param.20) | copy-start | bytes 388
  34.2 18.4 %collective-permute-start.14 = (bf16[384,768]{1,0:T(8,128)(2,1)S(1)}, bf16[384,768]{1,0:T(8,128)(2,1)S(1)}, u32[]{:S(2)}, u32[]{:S(2)}) collective-permute-start(bf16[384,768]{1,0:T(8,128)(2,1)S(1)} %constant_dynamic-update-slice_fusion.refs_8_), channel_id=1, source_target_pairs={{0,8},{8,16},{16,24},{24,32},{32,40},{40,48},{48,56},{56,0},{64,72... | collective-permute-start | bytes 1769480 | tf_op jit(solution)/shard_map/ppermute | solution.py:59
  36.2 23.4 %collective-permute-start.15 = (bf16[384,768]{1,0:T(8,128)(2,1)S(1)}, bf16[384,768]{1,0:T(8,128)(2,1)S(1)}, u32[]{:S(2)}, u32[]{:S(2)}) collective-permute-start(bf16[384,768]{1,0:T(8,128)(2,1)S(1)} %constant_dynamic-update-slice_fusion.refs_8_), channel_id=1, source_target_pairs={{0,56},{8,0},{16,8},{24,16},{32,24},{40,32},{48,40},{56,48},{64,12... | collective-permute-start | bytes 1769480 | tf_op jit(solution)/shard_map/ppermute | solution.py:59
  52.6 17.5 %collective-permute-start.18 = (bf16[384,768]{1,0:T(8,128)(2,1)S(1)}, bf16[384,768]{1,0:T(8,128)(2,1)S(1)}, u32[]{:S(2)}, u32[]{:S(2)}) collective-permute-start(bf16[384,768]{1,0:T(8,128)(2,1)S(1)} %collective-permute-done.14.refs_11_), channel_id=1, source_target_pairs={{0,8},{8,16},{16,24},{24,32},{32,40},{40,48},{48,56},{56,0},{64,72... | collective-permute-start | bytes 1769480 | tf_op jit(solution)/shard_map/ppermute | solution.py:59
  55.5 35.9 %collective-permute-start = (bf16[2,4,128,384]{3,2,1,0:T(8,128)(2,1)}, bf16[2,4,128,384]{3,2,1,0:T(8,128)(2,1)}, u32[]{:S(2)}, u32[]{:S(2)}) collective-permute-start(bf16[2,4,128,384]{3,2,1,0:T(8,128)(2,1)} %bitcast.24), channel_id=1, source_target_pairs={{0,8},{8,16},{16,24},{24,32},{32,40},{40,48},{48,56},{56,64},{64,7... | collective-permute-start | bytes 2359304 | tf_op jit(solution)/shard_map/ppermute | solution.py:397
  55.5 37.2 %collective-permute-start.1 = (bf16[2,4,128,384]{3,2,1,0:T(8,128)(2,1)}, bf16[2,4,128,384]{3,2,1,0:T(8,128)(2,1)}, u32[]{:S(2)}, u32[]{:S(2)}) collective-permute-start(bf16[2,4,128,384]{3,2,1,0:T(8,128)(2,1)} %bitcast.25), channel_id=1, source_target_pairs={{0,248},{8,0},{16,8},{24,16},{32,24},{40,32},{48,40},{56,48},{64,5... | collective-permute-start | bytes 2359304 | tf_op jit(solution)/shard_map/ppermute | solution.py:398
  59.6 27.8 %collective-permute-start.19 = (bf16[384,768]{1,0:T(8,128)(2,1)S(1)}, bf16[384,768]{1,0:T(8,128)(2,1)S(1)}, u32[]{:S(2)}, u32[]{:S(2)}) collective-permute-start(bf16[384,768]{1,0:T(8,128)(2,1)S(1)} %collective-permute-done.15.refs_12_), channel_id=1, source_target_pairs={{0,56},{8,0},{16,8},{24,16},{32,24},{40,32},{48,40},{56,48},{64,12... | collective-permute-start | bytes 1769480 | tf_op jit(solution)/shard_map/ppermute | solution.py:59
  62.0 9.4 %copy-start.42 = (s32[18]{0:T(128)S(1)}, s32[18]{0:T(128)}, u32[]{:S(2)}) copy-start(s32[18]{0:T(128)} %constant.66.clone) | copy-start | bytes 220
  69.0 44.3 %collective-permute-start.4 = (bf16[512,384]{1,0:T(8,128)(2,1)}, bf16[512,384]{1,0:T(8,128)(2,1)S(1)}, u32[]{:S(2)}, u32[]{:S(2)}) collective-permute-start(bf16[512,384]{1,0:T(8,128)(2,1)} %even_attention.1.refs_0_), channel_id=1, source_target_pairs={{0,6},{1,7},{2,0},{3,1},{4,2},{5,3},{6,4},{7,5},{8,14},{9,15},{10,... | collective-permute-start | bytes 1179656 | tf_op jit(solution)/shard_map/ppermute | solution.py:63
  70.1 22.6 %copy-start.2 = (bf16[384,768]{1,0:T(8,128)(2,1)}, bf16[384,768]{1,0:T(8,128)(2,1)S(1)}, u32[]{:S(2)}) copy-start(bf16[384,768]{1,0:T(8,128)(2,1)S(1)} %collective-permute-done.18.refs_15_) | copy-start | bytes 1769476
  70.1 24.6 %copy-start.33 = (bf16[192,768]{1,0:T(8,128)(2,1)}, bf16[192,768]{1,0:T(8,128)(2,1)S(1)}, u32[]{:S(2)}) copy-start(bf16[192,768]{1,0:T(8,128)(2,1)S(1)} %slice.46) | copy-start | bytes 884740
  70.1 22.7 %collective-permute-start.22 = (bf16[192,768]{1,0:T(8,128)(2,1)S(1)}, bf16[192,768]{1,0:T(8,128)(2,1)S(1)}, u32[]{:S(2)}, u32[]{:S(2)}) collective-permute-start(bf16[192,768]{1,0:T(8,128)(2,1)S(1)} %slice.46), channel_id=1, source_target_pairs={{0,8},{8,16},{16,24},{24,32},{32,40},{40,48},{48,56},{56,0},{64,72... | collective-permute-start | bytes 884744 | tf_op jit(solution)/shard_map/ppermute | solution.py:59
  87.5 7.3 %copy-start.5 = (bf16[384,768]{1,0:T(8,128)(2,1)}, bf16[384,768]{1,0:T(8,128)(2,1)S(1)}, u32[]{:S(2)}) copy-start(bf16[384,768]{1,0:T(8,128)(2,1)S(1)} %collective-permute-done.19.refs_16_) | copy-start | bytes 1769476
  87.5 7.3 %copy-start.35 = (bf16[192,768]{1,0:T(8,128)(2,1)}, bf16[192,768]{1,0:T(8,128)(2,1)S(1)}, u32[]{:S(2)}) copy-start(bf16[192,768]{1,0:T(8,128)(2,1)S(1)} %slice.47) | copy-start | bytes 884740
  87.5 8.0 %collective-permute-start.23 = (bf16[192,768]{1,0:T(8,128)(2,1)S(1)}, bf16[192,768]{1,0:T(8,128)(2,1)S(1)}, u32[]{:S(2)}, u32[]{:S(2)}) collective-permute-start(bf16[192,768]{1,0:T(8,128)(2,1)S(1)} %slice.47), channel_id=1, source_target_pairs={{0,56},{8,0},{16,8},{24,16},{32,24},{40,32},{48,40},{56,48},{64,12... | collective-permute-start | bytes 884744 | tf_op jit(solution)/shard_map/ppermute | solution.py:59
  91.5 24.8 %collective-permute-start.6 = (bf16[512,384]{1,0:T(8,128)(2,1)}, bf16[512,384]{1,0:T(8,128)(2,1)S(1)}, u32[]{:S(2)}, u32[]{:S(2)}) collective-permute-start(bf16[512,384]{1,0:T(8,128)(2,1)} %even_attention.1.refs_0_), channel_id=1, source_target_pairs={{0,4},{1,5},{2,6},{3,7},{4,0},{5,1},{6,2},{7,3},{8,12},{9,13},{10,... | collective-permute-start | bytes 1179656 | tf_op jit(solution)/shard_map/ppermute | solution.py:63
  92.7 24.4 %collective-permute-start.2 = (bf16[2,3,128,384]{3,2,1,0:T(8,128)(2,1)S(1)}, bf16[2,3,128,384]{3,2,1,0:T(8,128)(2,1)}, u32[]{:S(2)}, u32[]{:S(2)}) collective-permute-start(bf16[2,3,128,384]{3,2,1,0:T(8,128)(2,1)S(1)} %slice.42), channel_id=1, source_target_pairs={{0,8},{8,16},{16,24},{24,32},{32,40},{40,48},{48,56},{56,64},{64,7... | collective-permute-start | bytes 1769480 | tf_op jit(solution)/shard_map/ppermute | solution.py:399
  92.8 9.7 %copy-start.11 = (bf16[192,768]{1,0:T(8,128)(2,1)}, bf16[192,768]{1,0:T(8,128)(2,1)S(1)}, u32[]{:S(2)}) copy-start(bf16[192,768]{1,0:T(8,128)(2,1)S(1)} %collective-permute-done.22.refs_19_) | copy-start | bytes 884740
  92.8 19.6 %collective-permute-start.24 = (bf16[192,768]{1,0:T(8,128)(2,1)S(1)}, bf16[192,768]{1,0:T(8,128)(2,1)S(1)}, u32[]{:S(2)}, u32[]{:S(2)}) collective-permute-start(bf16[192,768]{1,0:T(8,128)(2,1)S(1)} %collective-permute-done.22.refs_19_), channel_id=1, source_target_pairs={{0,8},{8,16},{16,24},{24,32},{32,40},{40,48},{48,56},{56,0},{64,72... | collective-permute-start | bytes 884744 | tf_op jit(solution)/shard_map/ppermute | solution.py:59
  95.5 20.7 %copy-start.14 = (bf16[192,768]{1,0:T(8,128)(2,1)}, bf16[192,768]{1,0:T(8,128)(2,1)S(1)}, u32[]{:S(2)}) copy-start(bf16[192,768]{1,0:T(8,128)(2,1)S(1)} %collective-permute-done.23.refs_20_) | copy-start | bytes 884740
  95.5 24.0 %collective-permute-start.3 = (bf16[2,3,128,384]{3,2,1,0:T(8,128)(2,1)S(1)}, bf16[2,3,128,384]{3,2,1,0:T(8,128)(2,1)}, u32[]{:S(2)}, u32[]{:S(2)}) collective-permute-start(bf16[2,3,128,384]{3,2,1,0:T(8,128)(2,1)S(1)} %slice.43), channel_id=1, source_target_pairs={{0,248},{8,0},{16,8},{24,16},{32,24},{40,32},{48,40},{56,48},{64,5... | collective-permute-start | bytes 1769480 | tf_op jit(solution)/shard_map/ppermute | solution.py:400
  112.4 24.2 %collective-permute-start.8 = (bf16[512,384]{1,0:T(8,128)(2,1)}, bf16[512,384]{1,0:T(8,128)(2,1)}, u32[]{:S(2)}, u32[]{:S(2)}) collective-permute-start(bf16[512,384]{1,0:T(8,128)(2,1)} %even_attention.1.refs_0_), channel_id=1, source_target_pairs={{0,2},{1,3},{2,4},{3,5},{4,6},{5,7},{6,0},{7,1},{8,10},{9,11},{10,... | collective-permute-start | bytes 1179656 | tf_op jit(solution)/shard_map/ppermute | solution.py:63
  114.0 30.9 %collective-permute-start.25 = (bf16[576,768]{1,0:T(8,128)(2,1)}, bf16[576,768]{1,0:T(8,128)(2,1)S(1)}, u32[]{:S(2)}, u32[]{:S(2)}) collective-permute-start(bf16[576,768]{1,0:T(8,128)(2,1)} %constant_dynamic-update-slice_fusion.2), channel_id=1, source_target_pairs={{0,64},{8,72},{16,80},{24,88},{32,96},{40,104},{48,112},{56,120},{... | collective-permute-start | bytes 2654216 | tf_op jit(solution)/shard_map/ppermute | solution.py:59
  117.0 37.4 %collective-permute-start.26 = (bf16[576,768]{1,0:T(8,128)(2,1)}, bf16[576,768]{1,0:T(8,128)(2,1)S(1)}, u32[]{:S(2)}, u32[]{:S(2)}) collective-permute-start(bf16[576,768]{1,0:T(8,128)(2,1)} %constant_dynamic-update-slice_fusion.2), channel_id=1, source_target_pairs={{0,192},{8,200},{16,208},{24,216},{32,224},{40,232},{48,240},{56,2... | collective-permute-start | bytes 2654216 | tf_op jit(solution)/shard_map/ppermute | solution.py:59
  117.1 22.2 %collective-permute-start.12 = (bf16[192,768]{1,0:T(8,128)(2,1)}, bf16[192,768]{1,0:T(8,128)(2,1)}, u32[]{:S(2)}, u32[]{:S(2)}) collective-permute-start(bf16[192,768]{1,0:T(8,128)(2,1)} %collective-permute-done.10), channel_id=1, source_target_pairs={{0,64},{8,72},{16,80},{24,88},{32,96},{40,104},{48,112},{56,120},{... | collective-permute-start | bytes 884744 | tf_op jit(solution)/shard_map/ppermute | solution.py:59
  119.6 23.7 %collective-permute-start.13 = (bf16[192,768]{1,0:T(8,128)(2,1)}, bf16[192,768]{1,0:T(8,128)(2,1)}, u32[]{:S(2)}, u32[]{:S(2)}) collective-permute-start(bf16[192,768]{1,0:T(8,128)(2,1)} %collective-permute-done.10), channel_id=1, source_target_pairs={{0,192},{8,200},{16,208},{24,216},{32,224},{40,232},{48,240},{56,2... | collective-permute-start | bytes 884744 | tf_op jit(solution)/shard_map/ppermute | solution.py:59
  136.6 8.4 %copy-start.10 = (bf16[4,128,384]{2,1,0:T(8,128)(2,1)S(1)}, bf16[4,128,384]{2,1,0:T(8,128)(2,1)}, u32[]{:S(2)}) copy-start(bf16[4,128,384]{2,1,0:T(8,128)(2,1)} %odd_attention.1) | copy-start | bytes 1179652
  136.6 9.2 %copy-start.34 = (bf16[192,768]{1,0:T(8,128)(2,1)S(1)}, bf16[192,768]{1,0:T(8,128)(2,1)}, u32[]{:S(2)}) copy-start(bf16[192,768]{1,0:T(8,128)(2,1)} %copy-done.33) | copy-start | bytes 884740
  136.6 9.2 %copy-start.36 = (bf16[192,768]{1,0:T(8,128)(2,1)S(1)}, bf16[192,768]{1,0:T(8,128)(2,1)}, u32[]{:S(2)}) copy-start(bf16[192,768]{1,0:T(8,128)(2,1)} %copy-done.35) | copy-start | bytes 884740
  136.6 14.8 %collective-permute-start.5 = (bf16[512,384]{1,0:T(8,128)(2,1)}, bf16[512,384]{1,0:T(8,128)(2,1)S(1)}, u32[]{:S(2)}, u32[]{:S(2)}) collective-permute-start(bf16[512,384]{1,0:T(8,128)(2,1)} %bitcast.16), channel_id=1, source_target_pairs={{0,6},{1,7},{2,0},{3,1},{4,2},{5,3},{6,4},{7,5},{8,14},{9,15},{10,... | collective-permute-start | bytes 1179656 | tf_op jit(solution)/shard_map/ppermute | solution.py:63
  139.3 15.1 %collective-permute-start.7 = (bf16[512,384]{1,0:T(8,128)(2,1)}, bf16[512,384]{1,0:T(8,128)(2,1)S(1)}, u32[]{:S(2)}, u32[]{:S(2)}) collective-permute-start(bf16[512,384]{1,0:T(8,128)(2,1)} %bitcast.17), channel_id=1, source_target_pairs={{0,4},{1,5},{2,6},{3,7},{4,0},{5,1},{6,2},{7,3},{8,12},{9,13},{10,... | collective-permute-start | bytes 1179656 | tf_op jit(solution)/shard_map/ppermute | solution.py:63
  143.2 17.7 %collective-permute-start.16 = (bf16[384,768]{1,0:T(8,128)(2,1)}, bf16[384,768]{1,0:T(8,128)(2,1)S(1)}, u32[]{:S(2)}, u32[]{:S(2)}) collective-permute-start(bf16[384,768]{1,0:T(8,128)(2,1)} %pad_maximum_fusion), channel_id=1, source_target_pairs={{0,64},{8,72},{16,80},{24,88},{32,96},{40,104},{48,112},{56,120},{... | collective-permute-start | bytes 1769480 | tf_op jit(solution)/shard_map/ppermute | solution.py:59
  145.0 13.1 %collective-permute-start.9 = (bf16[512,384]{1,0:T(8,128)(2,1)S(1)}, bf16[512,384]{1,0:T(8,128)(2,1)S(1)}, u32[]{:S(2)}, u32[]{:S(2)}) collective-permute-start(bf16[512,384]{1,0:T(8,128)(2,1)S(1)} %bitcast.18), channel_id=1, source_target_pairs={{0,2},{1,3},{2,4},{3,5},{4,6},{5,7},{6,0},{7,1},{8,10},{9,11},{10,... | collective-permute-start | bytes 1179656 | tf_op jit(solution)/shard_map/ppermute | solution.py:63
  151.4 6.6 %copy-start.26 = (bf16[512,384]{1,0:T(8,128)(2,1)}, bf16[512,384]{1,0:T(8,128)(2,1)S(1)}, u32[]{:S(2)}) copy-start(bf16[512,384]{1,0:T(8,128)(2,1)S(1)} %collective-permute-done.5.refs_3_) | copy-start | bytes 1179652
  151.4 17.0 %collective-permute-start.17 = (bf16[384,768]{1,0:T(8,128)(2,1)}, bf16[384,768]{1,0:T(8,128)(2,1)}, u32[]{:S(2)}, u32[]{:S(2)}) collective-permute-start(bf16[384,768]{1,0:T(8,128)(2,1)} %pad_maximum_fusion), channel_id=1, source_target_pairs={{0,192},{8,200},{16,208},{24,216},{32,224},{40,232},{48,240},{56,2... | collective-permute-start | bytes 1769480 | tf_op jit(solution)/shard_map/ppermute | solution.py:59
  154.4 3.7 %copy-start.28 = (bf16[512,384]{1,0:T(8,128)(2,1)}, bf16[512,384]{1,0:T(8,128)(2,1)S(1)}, u32[]{:S(2)}) copy-start(bf16[512,384]{1,0:T(8,128)(2,1)S(1)} %collective-permute-done.7.refs_5_) | copy-start | bytes 1179652
  154.4 17.0 %collective-permute-start.20 = (bf16[384,768]{1,0:T(8,128)(2,1)}, bf16[384,768]{1,0:T(8,128)(2,1)}, u32[]{:S(2)}, u32[]{:S(2)}) collective-permute-start(bf16[384,768]{1,0:T(8,128)(2,1)} %pad_maximum_fusion.1), channel_id=1, source_target_pairs={{0,64},{8,72},{16,80},{24,88},{32,96},{40,104},{48,112},{56,120},{... | collective-permute-start | bytes 1769480 | tf_op jit(solution)/shard_map/ppermute | solution.py:59
  154.4 20.6 %collective-permute-start.21 = (bf16[384,768]{1,0:T(8,128)(2,1)}, bf16[384,768]{1,0:T(8,128)(2,1)}, u32[]{:S(2)}, u32[]{:S(2)}) collective-permute-start(bf16[384,768]{1,0:T(8,128)(2,1)} %pad_maximum_fusion.1), channel_id=1, source_target_pairs={{0,192},{8,200},{16,208},{24,216},{32,224},{40,232},{48,240},{56,2... | collective-permute-start | bytes 1769480 | tf_op jit(solution)/shard_map/ppermute | solution.py:59
  158.9 17.2 %collective-permute-start.28 = (bf16[288,768]{1,0:T(8,128)(2,1)}, bf16[288,768]{1,0:T(8,128)(2,1)}, u32[]{:S(2)}, u32[]{:S(2)}) collective-permute-start(bf16[288,768]{1,0:T(8,128)(2,1)} %pad_maximum_fusion.3), channel_id=1, source_target_pairs={{0,64},{8,72},{16,80},{24,88},{32,96},{40,104},{48,112},{56,120},{... | collective-permute-start | bytes 1327112 | tf_op jit(solution)/shard_map/ppermute | solution.py:59
  161.7 18.0 %collective-permute-start.27 = (bf16[288,768]{1,0:T(8,128)(2,1)}, bf16[288,768]{1,0:T(8,128)(2,1)}, u32[]{:S(2)}, u32[]{:S(2)}) collective-permute-start(bf16[288,768]{1,0:T(8,128)(2,1)} %pad_maximum_fusion.2), channel_id=1, source_target_pairs={{0,192},{8,200},{16,208},{24,216},{32,224},{40,232},{48,240},{56,2... | collective-permute-start | bytes 1327112 | tf_op jit(solution)/shard_map/ppermute | solution.py:59
  179.7 1.1 copy-start.3
  181.8 1.1 copy-start.8
  185.8 1.1 copy-start.19
  191.8 6.7 %copy-start.4 = (bf16[384,768]{1,0:T(8,128)(2,1)S(1)}, bf16[384,768]{1,0:T(8,128)(2,1)}, u32[]{:S(2)}) copy-start(bf16[384,768]{1,0:T(8,128)(2,1)} %copy-done.2) | copy-start | bytes 1769476
  191.8 6.7 %copy-start.9 = (bf16[384,768]{1,0:T(8,128)(2,1)S(1)}, bf16[384,768]{1,0:T(8,128)(2,1)}, u32[]{:S(2)}) copy-start(bf16[384,768]{1,0:T(8,128)(2,1)} %copy-done.7) | copy-start | bytes 1769476
  191.8 6.7 %copy-start.13 = (bf16[192,768]{1,0:T(8,128)(2,1)S(1)}, bf16[192,768]{1,0:T(8,128)(2,1)}, u32[]{:S(2)}) copy-start(bf16[192,768]{1,0:T(8,128)(2,1)} %copy-done.11) | copy-start | bytes 884740
  191.9 6.7 %copy-start.22 = (bf16[512,384]{1,0:T(8,128)(2,1)S(1)}, bf16[512,384]{1,0:T(8,128)(2,1)}, u32[]{:S(2)}) copy-start(bf16[512,384]{1,0:T(8,128)(2,1)} %copy-done.20) | copy-start | bytes 1179652
  191.9 6.7 %copy-start.25 = (bf16[512,384]{1,0:T(8,128)(2,1)S(1)}, bf16[512,384]{1,0:T(8,128)(2,1)}, u32[]{:S(2)}) copy-start(bf16[512,384]{1,0:T(8,128)(2,1)} %copy-done.23) | copy-start | bytes 1179652
  191.9 6.7 %copy-start.32 = (bf16[512,384]{1,0:T(8,128)(2,1)S(1)}, bf16[512,384]{1,0:T(8,128)(2,1)}, u32[]{:S(2)}) copy-start(bf16[512,384]{1,0:T(8,128)(2,1)} %copy-done.30) | copy-start | bytes 1179652
  197.6 8.1 %collective-permute-start.29 = (bf16[512,768]{1,0:T(8,128)(2,1)S(1)}, bf16[512,768]{1,0:T(8,128)(2,1)}, u32[]{:S(2)}, u32[]{:S(2)}) collective-permute-start(bf16[512,768]{1,0:T(8,128)(2,1)S(1)} %project.3), channel_id=1, source_target_pairs={{0,1},{1,0},{2,3},{3,2},{4,5},{5,4},{6,7},{7,6},{8,9},{9,8},{10,11... | collective-permute-start | bytes 2359304 | tf_op jit(solution)/shard_map/ppermute | solution.py:63
  204.5 1.2 copy-start.1
  205.7 4.2 %copy-start.43 = (bf16[32,768]{1,0:T(8,128)(2,1)S(1)}, bf16[32,768]{1,0:T(8,128)(2,1)}, u32[]{:S(2)}) copy-start(bf16[32,768]{1,0:T(8,128)(2,1)} %param.17) | copy-start | bytes 147460
  205.7 11.0 %copy-start.44 = (bf16[32,768]{1,0:T(8,128)(2,1)S(1)}, bf16[32,768]{1,0:T(8,128)(2,1)}, u32[]{:S(2)}) copy-start(bf16[32,768]{1,0:T(8,128)(2,1)} %param.18) | copy-start | bytes 147460
  209.6 1.4 collective-permute-start.30
  211.6 9.2 %copy-start.37 = (f32[4,1,128]{2,1,0:T(1,128)}, f32[4,1,128]{2,1,0:T(1,128)S(1)}, u32[]{:S(2)}) copy-start(f32[4,1,128]{2,1,0:T(1,128)S(1)} %add.34.s0_ref) | copy-start | bytes 6148
  211.6 6.4 %collective-permute-start.31 = (f32[4,1,128]{2,1,0:T(1,128)S(1)}, f32[4,1,128]{2,1,0:T(1,128)S(1)}, u32[]{:S(2)}, u32[]{:S(2)}) collective-permute-start(f32[4,1,128]{2,1,0:T(1,128)S(1)} %add.34.s0_ref), channel_id=1, source_target_pairs={{0,6},{1,7},{2,0},{3,1},{4,2},{5,3},{6,4},{7,5},{8,14},{9,15},{10,... | collective-permute-start | bytes 6152 | tf_op jit(solution)/shard_map/ppermute | solution.py:63
  215.7 5.1 %collective-permute-start.32 = (f32[4,1,128]{2,1,0:T(1,128)S(1)}, f32[4,1,128]{2,1,0:T(1,128)S(1)}, u32[]{:S(2)}, u32[]{:S(2)}) collective-permute-start(f32[4,1,128]{2,1,0:T(1,128)S(1)} %add.34.s0_ref), channel_id=1, source_target_pairs={{0,4},{1,5},{2,6},{3,7},{4,0},{5,1},{6,2},{7,3},{8,12},{9,13},{10,... | collective-permute-start | bytes 6152 | tf_op jit(solution)/shard_map/ppermute | solution.py:63
  215.7 5.1 %collective-permute-start.33 = (f32[4,1,128]{2,1,0:T(1,128)S(1)}, f32[4,1,128]{2,1,0:T(1,128)S(1)}, u32[]{:S(2)}, u32[]{:S(2)}) collective-permute-start(f32[4,1,128]{2,1,0:T(1,128)S(1)} %add.34.s0_ref), channel_id=1, source_target_pairs={{0,2},{1,3},{2,4},{3,5},{4,6},{5,7},{6,0},{7,1},{8,10},{9,11},{10,... | collective-permute-start | bytes 6152 | tf_op jit(solution)/shard_map/ppermute | solution.py:63
  218.1 2.7 %copy-start.38 = (f32[4,1,128]{2,1,0:T(1,128)}, f32[4,1,128]{2,1,0:T(1,128)S(1)}, u32[]{:S(2)}) copy-start(f32[4,1,128]{2,1,0:T(1,128)S(1)} %collective-permute-done.31.s1_ref) | copy-start | bytes 6148
  (16 other events, 14.0 us)

commit v2 on v0

v2 whole, which is shorter than its diff:
```python
import functools
import math

import jax
import jax.numpy as jnp
from jax import lax
from jax.experimental import pallas as pl
from jax.experimental.pallas import tpu as pltpu
from jax.sharding import PartitionSpec as P

D = 6144
HD = 128
S = 128
FR = 4
X, Y, Z, CORES = 4, 4, 8, 2
ROWS = FR * S
COLS = D // (X * CORES)
HALF = COLS // 2
WB = D // (Y * Z)
GROUP = 16
eps = 1e-06
negative = -1e30
NT = (((1,), (1,)), ((), ()))
HBM = pl.BlockSpec(memory_space=pltpu.HBM)
ROOM = pltpu.CompilerParams(vmem_limit_bytes=56 * 1024 * 1024)


def ring_perm(d):
    n = Y * Z
    return [(i, (i + d) % n) for i in range(n)]


def mp_perm(dx, dc):
    return [
        (x * CORES + c, (x + dx) % X * CORES + (c + dc) % CORES)
        for x in range(X)
        for c in range(CORES)
    ]


def device(x, y, z, c):
    return (y * Z + z) * X * CORES + x * CORES + c


PLACES = [(x, y, z, c) for x in range(X) for y in range(Y) for z in range(Z) for c in range(CORES)]


def weight_perm():
    half = Z // 2
    return [
        (device(x, y, z, c), device(y, x, z % half * CORES + c, z // half)) for x, y, z, c in PLACES
    ]


def spread_perm(shift):
    return [(device(x, y, z, c), device((y + shift) % X, x, z, c)) for x, y, z, c in PLACES]


def mp_move(a, dx, dc=0):
    return lax.ppermute(a, "mp", mp_perm(dx, dc))


def clip_index(frame_counts, frame_ids):
    ends = jnp.cumsum(frame_counts)
    return jnp.sum((ends[None, :] <= frame_ids[:, None]).astype(jnp.int32), axis=1)


def cost(flops, nbytes):
    return pl.CostEstimate(flops=flops, bytes_accessed=nbytes, transcendentals=0)


def pack_kv_kernel(k_ref, v_ref, r3_ref, r1_ref, l3_ref, l1_ref):
    for which, ref in enumerate((k_ref, v_ref)):
        r3_ref[which] = ref[1:]
        r1_ref[which] = ref[:1]
        l3_ref[which] = ref[: FR - 1]
        l1_ref[which] = ref[FR - 1 :]


def pack_kv(keys, values):
    sizes = (FR - 1, 1, FR - 1, 1)
    return pl.pallas_call(
        pack_kv_kernel,
        grid=(3,),
        in_specs=[pl.BlockSpec((FR, S, HD), lambda j: (0, 0, 2 * j + 1))] * 2,
        out_specs=[pl.BlockSpec((2, n, S, HD), lambda j: (0, 0, 0, j)) for n in sizes],
        out_shape=[jax.ShapeDtypeStruct((2, n, S, HALF), jnp.bfloat16) for n in sizes],
        compiler_params=ROOM,
        cost_estimate=cost(0, 6 * ROWS * HALF * 2),
        name="pack_kv",
    )(keys.reshape(FR, S, COLS), values.reshape(FR, S, COLS))


def softmax_weights(scores):
    highest = jnp.max(scores, axis=-1, keepdims=True)
    raised = jnp.exp(scores - highest)
    inverse = 1.0 / jnp.sum(raised, axis=-1, keepdims=True)
    return (raised * inverse).astype(jnp.bfloat16)


EVEN_FRAMES = 2


def even_kernel(info_ref, q_ref, k_ref, v_ref, o_ref):
    base = pl.program_id(0) * EVEN_FRAMES
    lane = lax.broadcasted_iota(jnp.int32, (S, S), 1)
    row = lax.broadcasted_iota(jnp.int32, (S, HD), 0)
    pieces = [(f, h) for f in range(EVEN_FRAMES) for h in range(3)]

    def take(ref, f, h):
        return ref[f * S : (f + 1) * S, 2 * h * HD : (2 * h + 1) * HD]

    scores = []
    for f, h in pieces:
        raw = lax.dot_general(
            take(q_ref, f, h), take(k_ref, f, h), NT, preferred_element_type=jnp.float32
        ) * (1.0 / math.sqrt(HD))
        scores.append(jnp.where(lane < info_ref[FR + base + f], raw, negative))
    weights = softmax_weights(jnp.concatenate(scores, axis=0))
    for i, (f, h) in enumerate(pieces):
        out = jnp.dot(
            weights[i * S : (i + 1) * S], take(v_ref, f, h), preferred_element_type=jnp.float32
        )
        out = jnp.where(row < info_ref[FR + base + f], out, 0.0).astype(jnp.bfloat16)
        o_ref[f * S : (f + 1) * S, h * HD : (h + 1) * HD] = out


def even_attention(info, queries, keys, values):
    block = pl.BlockSpec((EVEN_FRAMES * S, COLS), lambda f, g: (f, 0))
    return pl.pallas_call(
        even_kernel,
        grid_spec=pltpu.PrefetchScalarGridSpec(
            num_scalar_prefetch=1,
            grid=(FR // EVEN_FRAMES,),
            in_specs=[block] * 3,
            out_specs=pl.BlockSpec((EVEN_FRAMES * S, HALF), lambda f, g: (f, 0)),
        ),
        out_shape=jax.ShapeDtypeStruct((ROWS, HALF), jnp.bfloat16),
        compiler_params=ROOM,
        cost_estimate=cost(FR * 3 * 4 * S * S * HD, 4 * ROWS * COLS * 2),
        name="even_attention",
    )(info, queries, keys, values)


WINDOW = 18
BATCH = 2


def odd_kernel(info_ref, clip_ref, q_ref, k_ref, v_ref, *refs):
    far_refs, o_ref = refs[:-1], refs[-1]
    keys_wide = WINDOW * GROUP
    query_cell = lax.broadcasted_iota(jnp.int32, (GROUP, keys_wide), 0)
    key_cell = lax.rem(lax.broadcasted_iota(jnp.int32, (GROUP, keys_wide), 1), GROUP)
    same_cell = query_cell == key_cell
    allowed = [same_cell & (clip_ref[...] == info_ref[f]) for f in range(FR)]
    cell = lax.broadcasted_iota(jnp.int32, (GROUP, HD), 0)
    pieces = [(b, h) for b in range(BATCH) for h in range(3)]

    def window(own_ref, which, b, h):
        rows = slice(b * GROUP, (b + 1) * GROUP)
        wide = slice((2 * h + 1) * HD, (2 * h + 2) * HD)
        at = slice(h * HD, (h + 1) * HD)
        parts = [own_ref[:, rows, wide]]
        parts += [r[which, :, rows, at] for r in far_refs]
        return jnp.concatenate([p.reshape(-1, HD) for p in parts], axis=0)

    scores = []
    for b, h in pieces:
        q = q_ref[:, b * GROUP : (b + 1) * GROUP, (2 * h + 1) * HD : (2 * h + 2) * HD]
        raw = lax.dot_general(
            q.reshape(FR * GROUP, HD), window(k_ref, 0, b, h), NT,
            preferred_element_type=jnp.float32,
        ) * (1.0 / math.sqrt(HD))
        for f in range(FR):
            scores.append(jnp.where(allowed[f], raw[f * GROUP : (f + 1) * GROUP], negative))
    weights = softmax_weights(jnp.concatenate(scores, axis=0))
    n = FR * GROUP
    for i, (b, h) in enumerate(pieces):
        out = jnp.dot(
            weights[i * n : (i + 1) * n], window(v_ref, 1, b, h),
            preferred_element_type=jnp.float32,
        )
        first = (pl.program_id(0) * BATCH + b) * GROUP
        for f in range(FR):
            part = out[f * GROUP : (f + 1) * GROUP]
            part = jnp.where(first + cell < info_ref[FR + f], part, 0.0)
            o_ref[f, b * GROUP : (b + 1) * GROUP, h * HD : (h + 1) * HD] = part.astype(
                jnp.bfloat16
            )


def odd_attention(info, key_clips, queries, keys, values, others):
    def frames(a):
        return a.reshape(FR, S, COLS)

    step = GROUP * BATCH
    own = pl.BlockSpec((FR, step, COLS), lambda i, g: (0, i, 0))

    def other(n):
        return pl.BlockSpec((2, n, step, HALF), lambda i, g: (0, 0, i, 0))

    out = pl.pallas_call(
        odd_kernel,
        grid_spec=pltpu.PrefetchScalarGridSpec(
            num_scalar_prefetch=1,
            grid=(S // step,),
            in_specs=[
                pl.BlockSpec((1, WINDOW * GROUP), lambda i, g: (0, 0)),
                own, own, own, *[other(a.shape[1]) for a in others],
            ],
            out_specs=pl.BlockSpec((FR, step, HALF), lambda i, g: (0, i, 0)),
        ),
        out_shape=jax.ShapeDtypeStruct((FR, S, HALF), jnp.bfloat16),
        compiler_params=ROOM,
        cost_estimate=cost(ROWS * 3 * 4 * WINDOW * GROUP * HD, 10 * ROWS * COLS * 2),
        name="odd_attention",
    )(info, key_clips, frames(queries), frames(keys), frames(values), *others)
    return out.reshape(ROWS, HALF)


def project_kernel(shifts, info_ref, *refs):
    own_refs, other_even, other_odd = refs[: 2 * X], refs[2 * X], refs[2 * X + 1 : 3 * X + 1]
    w_ref = refs[3 * X + 1]
    n = len(shifts)
    o_refs, (a_buf, w_buf, a_sem, w_sem) = refs[3 * X + 2 : 3 * X + 2 + n], refs[3 * X + 2 + n :]
    x, y, core = info_ref[2 * FR], info_ref[2 * FR + 1], info_ref[2 * FR + 2]
    half = Z // 2
    w_copies = [
        pltpu.make_async_copy(
            w_ref.at[CORES * i + c], w_buf.at[i, :, c * COLS : (c + 1) * COLS], w_sem.at[i]
        )
        for i in range(half)
        for c in range(CORES)
    ]
    for copy in w_copies:
        copy.start()
    for i, d in enumerate(shifts):
        slot = lax.rem(x - y - d + 2 * X, X)
        for r in range(X):
            sources = [own_refs[2 * r], own_refs[2 * r + 1]]
            sources += [other_even.at[r * ROWS : (r + 1) * ROWS], other_odd[r]]

            @pl.when(slot == r)
            def _(sources=sources, i=i):
                for k, source in enumerate(sources):
                    side = core if k < 2 else 1 - core
                    for h in range(3):
                        at = pl.multiple_of(side * COLS + (2 * h + k % 2) * HD, HD)
                        pltpu.make_async_copy(
                            source.at[:, h * HD : (h + 1) * HD],
                            a_buf.at[i, :, pl.ds(at, HD)],
                            a_sem.at[i],
                        ).start()
    for copy in w_copies:
        copy.wait()
    for i in range(n):
        pltpu.make_async_copy(a_buf.at[i], a_buf.at[i], a_sem.at[i]).wait()
        total = lax.dot_general(
            a_buf[i], w_buf[...].reshape(COLS, 2 * COLS), NT, preferred_element_type=jnp.float32
        )
        o_refs[i][...] = total.astype(o_refs[i].dtype)


def project(info, operands, shifts, out_type):
    n = len(shifts)
    return pl.pallas_call(
        functools.partial(project_kernel, shifts),
        grid_spec=pltpu.PrefetchScalarGridSpec(
            num_scalar_prefetch=1,
            grid=(1,),
            in_specs=[HBM] * len(operands),
            out_specs=[pl.BlockSpec((ROWS, COLS), lambda i, p: (0, 0))] * n,
            scratch_shapes=[
                pltpu.VMEM((n, ROWS, 2 * COLS), jnp.bfloat16),
                pltpu.VMEM((Z // 2, WB, 2 * COLS), jnp.bfloat16),
                pltpu.SemaphoreType.DMA((n,)),
                pltpu.SemaphoreType.DMA((Z // 2,)),
            ],
        ),
        out_shape=[jax.ShapeDtypeStruct((ROWS, COLS), out_type)] * n,
        compiler_params=ROOM,
        cost_estimate=cost(4 * n * ROWS * COLS * COLS, 4 * 1024 * 1024),
        name="project",
    )(info, *operands)


TAIL_FRAMES = 2


def table_row(table_ref, clip):
    lane = lax.broadcasted_iota(jnp.int32, (8, table_ref.shape[0]), 1)
    hot = jnp.where(lane == clip, 1.0, 0.0).astype(jnp.bfloat16)
    return jnp.dot(hot, table_ref[...], preferred_element_type=jnp.float32)[:1]


def update_kernel(
    info_ref, own_ref, p0_ref, p1_ref, p2_ref, residual_ref, gate_ref, u_ref, sq_ref
):
    for f in range(TAIL_FRAMES):
        rows = slice(f * S, (f + 1) * S)
        gate = table_row(gate_ref, info_ref[pl.program_id(0) * TAIL_FRAMES + f])
        folded = None
        for j in range(COLS // HD):
            at = slice(j * HD, (j + 1) * HD)
            total = own_ref[rows, at]
            for part_ref in (p0_ref, p1_ref, p2_ref):
                total = total + part_ref[rows, at].astype(jnp.float32)
            combined = residual_ref[rows, at].astype(jnp.float32) + gate[:, at] * total
            updated = combined.astype(jnp.bfloat16)
            u_ref[rows, at] = updated
            wide = updated.astype(jnp.float32)
            folded = wide * wide if folded is None else folded + wide * wide
        sq_ref[f] = jnp.sum(folded.T, axis=0, keepdims=True)


def update(info, own, parts, residual, gate):
    block = pl.BlockSpec((TAIL_FRAMES * S, COLS), lambda f, g: (f, 0))
    return pl.pallas_call(
        update_kernel,
        grid_spec=pltpu.PrefetchScalarGridSpec(
            num_scalar_prefetch=1,
            grid=(FR // TAIL_FRAMES,),
            in_specs=[block] * 5 + [pl.BlockSpec(gate.shape, lambda f, g: (0, 0))],
            out_specs=[block, pl.BlockSpec((TAIL_FRAMES, 1, S), lambda f, g: (f, 0, 0))],
        ),
        out_shape=[
            jax.ShapeDtypeStruct((ROWS, COLS), jnp.bfloat16),
            jax.ShapeDtypeStruct((FR, 1, S), jnp.float32),
        ],
        compiler_params=ROOM,
        cost_estimate=cost(0, ROWS * COLS * 14),
        name="update",
    )(info, own, *parts, residual, gate)


def norm_kernel(info_ref, u_ref, s0_ref, s1_ref, s2_ref, s3_ref, scale_ref, shift_ref, o_ref):
    for f in range(TAIL_FRAMES):
        rows = slice(f * S, (f + 1) * S)
        clip = info_ref[pl.program_id(0) * TAIL_FRAMES + f]
        scale, shift = table_row(scale_ref, clip), table_row(shift_ref, clip)
        total = s0_ref[f] + s1_ref[f] + s2_ref[f] + s3_ref[f]
        inverse = lax.rsqrt(total * (1.0 / D) + eps)
        inverse = jnp.broadcast_to(inverse, (S, S)).T
        for j in range(COLS // HD):
            at = slice(j * HD, (j + 1) * HD)
            wide = u_ref[rows, at].astype(jnp.float32)
            normed = wide * inverse * (1.0 + scale[:, at]) + shift[:, at]
            o_ref[rows, at] = normed.astype(jnp.bfloat16)


def norm(info, updated, sums, scale, shift):
    block = pl.BlockSpec((TAIL_FRAMES * S, COLS), lambda f, g: (f, 0))
    table = pl.BlockSpec(scale.shape, lambda f, g: (0, 0))
    lane = pl.BlockSpec((TAIL_FRAMES, 1, S), lambda f, g: (f, 0, 0))
    return pl.pallas_call(
        norm_kernel,
        grid_spec=pltpu.PrefetchScalarGridSpec(
            num_scalar_prefetch=1,
            grid=(FR // TAIL_FRAMES,),
            in_specs=[block, lane, lane, lane, lane, table, table],
            out_specs=block,
        ),
        out_shape=jax.ShapeDtypeStruct((ROWS, COLS), jnp.bfloat16),
        compiler_params=ROOM,
        cost_estimate=cost(0, ROWS * COLS * 4),
        name="norm",
    )(info, updated, *sums, scale, shift)


def gather_weight(own):
    groups = [[y * Z + z for z in range(Z)] for y in range(Y)]
    return lax.all_gather(own, "seq", axis=0, tiled=False, axis_index_groups=groups)


def spread(a):
    return [lax.ppermute(a, ("seq", "mp"), spread_perm(r)) for r in range(X)]


def gather_x(a):
    return [a, mp_move(a, -1), mp_move(a, 2), mp_move(a, 1)]


def seq_move(a, dy):
    perm = [(y * Z + z, (y + dy) % Y * Z + z) for y in range(Y) for z in range(Z)]
    return lax.ppermute(a, "seq", perm)


def local(
    queries,
    keys,
    values,
    residual,
    out_weight,
    gate,
    mod_scale,
    mod_shift,
    frame_counts,
    patch_counts,
):
    s = lax.axis_index("seq")
    m = lax.axis_index("mp")
    x, core, y = m // CORES, m % CORES, s // Z

    barrier = lax.optimization_barrier
    own_weight = lax.ppermute(out_weight.T, ("seq", "mp"), weight_perm())
    packed = pack_kv(keys, values)
    packed, queries = barrier((packed, queries))
    right3, right1, left3, left1 = packed
    right3 = lax.ppermute(right3, "seq", ring_perm(1))
    left3 = lax.ppermute(left3, "seq", ring_perm(-1))
    right1 = lax.ppermute(right1, "seq", ring_perm(1))
    left1 = lax.ppermute(left1, "seq", ring_perm(-1))

    first = s * FR
    own_clips = clip_index(frame_counts, first + jnp.arange(FR, dtype=jnp.int32))
    clip_ids = jnp.arange(frame_counts.shape[0], dtype=jnp.int32)
    hot = own_clips[:, None] == clip_ids[None, :]
    own_grid = jnp.sum(jnp.where(hot, patch_counts[None, :], 0), axis=1)
    info = jnp.concatenate([own_clips, own_grid, jnp.stack([x, y, core]).astype(jnp.int32)])
    rel = [0, 1, 2, 3, -3, -2, -1, -4, 4, 5, 6, 7, -7, -6, -5, 8, 9, 10]
    rel = [r for r in rel for _ in range(GROUP)]
    key_ids = first + jnp.array(rel, dtype=jnp.int32)
    inside = (key_ids >= 0) & (key_ids < FR * Y * Z)
    key_clips = jnp.where(inside, clip_index(frame_counts, key_ids), -1)[None, :]

    even = even_attention(info, queries, keys, values)
    right3, left3, right1, left1, even, own_weight = barrier(
        (right3, left3, right1, left1, even, own_weight)
    )
    right6 = lax.ppermute(right3, "seq", ring_perm(1))
    left6 = lax.ppermute(left3, "seq", ring_perm(-1))
    weights = gather_weight(own_weight)
    even = spread(even)
    others = (right3, right1, left3, left1, right6, left6)
    odd = odd_attention(info, key_clips, queries, keys, values, others)
    odd, even = barrier((odd, even))
    odd = spread(odd)
    other_even = mp_move(jnp.concatenate(even, axis=0), 0, 1)
    other_odd = [mp_move(a, 0, 1) for a in odd]
    own_parts = [a for pair in zip(even, odd) for a in pair]
    operands = [*own_parts, other_even, *other_odd, weights]

    (far,) = project(info, operands, (2,), jnp.bfloat16)
    far, info = barrier((far, info))
    far = seq_move(far, 2)
    up, down = project(info, operands, (1, -1), jnp.bfloat16)
    up, down, info = barrier((up, down, info))
    up, down = seq_move(up, 1), seq_move(down, -1)
    (own,) = project(info, operands, (0,), jnp.float32)

    updated, squares = update(info, own, (far, up, down), residual, gate)
    squares = squares + mp_move(squares, 0, 1)
    normed = norm(info, updated, gather_x(squares), mod_scale, mod_shift)
    return updated, normed


def solution(mesh):
    in_specs = (
        P("seq", "mp"),
        P("seq", "mp"),
        P("seq", "mp"),
        P("seq", "mp"),
        P("mp", "seq"),
        P(None, "mp"),
        P(None, "mp"),
        P(None, "mp"),
        P(),
        P(),
    )
    out_specs = (P("seq", "mp"), P("seq", "mp"))
    return jax.shard_map(local, mesh=mesh, in_specs=in_specs, out_specs=out_specs, check_vma=False)
```

time: 244 us -> 196 us (0.80)
  waiting for transfers between devices: 147 us -> 83.4 us
  Pallas kernels: 0 us -> 38.8 us
  starting transfers between devices: 32.8 us -> 50.1 us
  matrix products: 16.7 us -> 0 us
  blocking collectives: 12.8 us -> 0 us
  local copies, waits for them, and re-layouts: 15.4 us -> 6.92 us
    ppermute x0 -> x27, waiting for transfers between devices: none -> 83.4 us  [the longest x8 28.9 us: spread(): return [lax.ppermute(a, ('seq', 'mp'), spread_perm(r)) for r in range(X)]]
    reduce_scatter x1 -> x0, waiting for transfers between devices: 72.5 us -> none  [local(): lax.psum_scatter(partial_terms, 'mp', scatter_dimension=1, tiled=True)]
    all_to_all x4 -> x0, waiting for transfers between devices: 50.9 us -> none  [the longest x1 14.4 us: local(): lax.all_to_all(v_time, 'seq', split_axis=1, concat_axis=0, tiled=True)]
    ppermute x0 -> x27, starting transfers between devices: none -> 50.1 us  [the longest x8 19.7 us: spread(): return [lax.ppermute(a, ('seq', 'mp'), spread_perm(r)) for r in range(X)]]
    pallas_call x0 -> x8, Pallas kernels: none -> 38.8 us  [the longest x3 18.5 us: project(): pl.pallas_call(functools.partial(project_kernel, shifts), grid_spec=pltpu...]
    all_to_all x4 -> x0, starting transfers between devices: 32.6 us -> none  [the longest x1 11.7 us: local(): lax.all_to_all(q_time, 'seq', split_axis=1, concat_axis=0, tiled=True)]
    all_gather x1, waiting for transfers between devices: 22.7 us -> 0.01 us  [gather_weight(): lax.all_gather(own, 'seq', axis=0, tiled=False, axis_index_groups=groups)]
    dot_general x8 -> x0, matrix products: 16.2 us -> none  [the longest x1 11.6 us: local(): jnp.dot(attended, lax.all_gather(out_weight, 'seq', axis=1, tiled=True),...]
  transfers between devices with their start and end apart: 6 -> 28, of which waited for: 6 -> 15; matrix products, arithmetic and copies ran while one was open for 9% -> 2% of each run, Pallas kernels for 0% -> 12%
where the time goes in v2:
time: 196 us
  waiting for transfers between devices  83.4 us (43%)
  starting transfers between devices  50.1 us (26%)
  Pallas kernels  38.8 us (20%)
  between operations  14.5 us (7%)
  local copies, waits for them, and re-layouts  6.92 us (4%)
  other arithmetic  2.12 us (1%)
    ppermute x8, waiting for transfers between devices, spread(): return [lax.ppermute(a, ('seq', 'mp'), spread_perm(r)) for r in range(X)]  28.9 us
    ppermute x3, waiting for transfers between devices, seq_move(): return lax.ppermute(a, 'seq', perm)  20.7 us
    ppermute x8, starting transfers between devices, spread(): return [lax.ppermute(a, ('seq', 'mp'), spread_perm(r)) for r in range(X)]  19.7 us
    pallas_call x3, Pallas kernels, project(): pl.pallas_call(functools.partial(project_kernel, shifts), grid_spec=pltpu...  18.5 us
    ppermute x1, waiting for transfers between devices, local(): right1 = lax.ppermute(right1, 'seq', ring_perm(1))  13.8 us
    ppermute x1, waiting for transfers between devices, local(): right6 = lax.ppermute(right3, 'seq', ring_perm(1))  10.5 us
    ppermute x9, waiting for transfers between devices, mp_move(): return lax.ppermute(a, 'mp', mp_perm(dx, dc))  6.6 us
    ppermute x9, starting transfers between devices, mp_move(): return lax.ppermute(a, 'mp', mp_perm(dx, dc))  6.18 us
  transfers between devices with their start and end apart: 28, of which 15 were waited for; matrix products, arithmetic and copies ran while one was open for 2% of the time, Pallas kernels for 12%

profile of v2, /device:TPU:8, one launch (start us, length us, event | category | flops | bytes accessed | tf_op | source)
XLA Modules:
  0.0 195.9 jit_solution(18005056755796574290)
XLA Ops:
  7.2 0.0 all-gather.3.cloned.1.call-start
  7.2 0.0 copy-start.25
  7.2 3.3 %pack_kv.1 = (bf16[2,3,128,384]{3,2,1,0:T(8,128)(2,1)}, bf16[2,1,128,384]{3,2,1,0:T(8,128)(2,1)}, bf16[2,3,128,384]{3,2,1,0:T(8,128)(2,1)}, bf16[2,1,128,384]{3,2,1,0:T(8,128)(2,1)}) custom-call(bf16[4,128,768]{2,1,0:T(8,128)(2,1)} %bitcast.13, bf16[4,128,768]{2,1,0:T(8,128)(2,1)} %bitcast.15), custom_call_target="tpu_custom_call" | custom-call | bytes 2359296 | tf_op jit(solution)/shard_map/pack_kv/pallas_call | solution.py:82
  10.5 1.9 collective-permute-start
  12.4 3.9 %collective-permute-start.1 = (bf16[2,3,128,384]{3,2,1,0:T(8,128)(2,1)}, bf16[2,3,128,384]{3,2,1,0:T(8,128)(2,1)S(1)}, u32[]{:S(2)}, u32[]{:S(2)}) collective-permute-start(bf16[2,3,128,384]{3,2,1,0:T(8,128)(2,1)} %get-tuple-element.37), channel_id=1, source_target_pairs={{0,248},{8,0},{16,8},{24,16},{32,24},{40,32},{48,40},{56,48},{64,5... | collective-permute-start | bytes 1769480 | tf_op jit(solution)/shard_map/ppermute | solution.py:410
  16.3 5.8 %collective-permute-start.4 = (bf16[192,768]{1,0:T(8,128)(2,1)}, bf16[192,768]{1,0:T(8,128)(2,1)S(1)}, u32[]{:S(2)}, u32[]{:S(2)}) collective-permute-start(bf16[192,768]{1,0:T(8,128)(2,1)} %bitcast.23), channel_id=1, source_target_pairs={{0,0},{1,8},{8,16},{9,24},{16,32},{17,40},{24,48},{25,56},{32,1},{... | collective-permute-start | bytes 884744 | tf_op jit(solution)/shard_map/ppermute | solution.py:405
  22.2 0.1 collective-permute-start.2
  22.3 4.1 %collective-permute-start.3 = (bf16[2,1,128,384]{3,2,1,0:T(8,128)(2,1)}, bf16[2,1,128,384]{3,2,1,0:T(8,128)(2,1)S(1)}, u32[]{:S(2)}, u32[]{:S(2)}) collective-permute-start(bf16[2,1,128,384]{3,2,1,0:T(8,128)(2,1)} %get-tuple-element.39), channel_id=1, source_target_pairs={{0,248},{8,0},{16,8},{24,16},{32,24},{40,32},{48,40},{56,48},{64,5... | collective-permute-start | bytes 589832 | tf_op jit(solution)/shard_map/ppermute | solution.py:412
  26.4 0.7 copy.15
  27.1 0.1 reduce-window.8
  27.2 0.1 reduce
  27.3 0.2 convert_reduce_fusion.1
  27.5 0.8 select_reduce_fusion
  28.3 0.7 concatenate.6.info_ref
  29.0 3.8 %even_attention.1 = bf16[512,384]{1,0:T(8,128)(2,1)} custom-call(s32[11]{0:T(128)} %concatenate.6.info_ref, bf16[512,768]{1,0:T(8,128)(2,1)} %q_ref, bf16[512,768]{1,0:T(8,128)(2,1)} %k_ref.1, bf16[512,768]{1,0:T(8,128)(2,1)} %v_ref.1), custom_call_target="tpu_custom_call" | custom-call | flops 100663296 | bytes 3145728 | tf_op jit(solution)/shard_map/even_attention/pallas_call | solution.py:130
  32.8 13.8 %collective-permute-done.2.refs_1_ = bf16[2,1,128,384]{3,2,1,0:T(8,128)(2,1)S(1)} collective-permute-done((bf16[2,1,128,384]{3,2,1,0:T(8,128)(2,1)}, bf16[2,1,128,384]{3,2,1,0:T(8,128)(2,1)S(1)}, u32[]{:S(2)}, u32[]{:S(2)}) %collective-permute-start.2) | collective-permute-done | bytes 196640 | tf_op jit(solution)/shard_map/ppermute | solution.py:411
  46.7 0.0 copy-start.16
  46.7 0.7 copy-done.21
  47.4 0.0 all-gather.3.cloned.1.call-update
  47.4 0.1 collective-permute-start.5
  47.5 4.1 %collective-permute-start.6 = (bf16[2,3,128,384]{3,2,1,0:T(8,128)(2,1)S(1)}, bf16[2,3,128,384]{3,2,1,0:T(8,128)(2,1)S(1)}, u32[]{:S(2)}, u32[]{:S(2)}) collective-permute-start(bf16[2,3,128,384]{3,2,1,0:T(8,128)(2,1)S(1)} %collective-permute-done.1.refs_2_), channel_id=1, source_target_pairs={{0,248},{8,0},{16,8},{24,16},{32,24},{40,32},{48,40},{56,48},{64,5... | collective-permute-start | bytes 1769480 | tf_op jit(solution)/shard_map/ppermute | solution.py:431
  51.6 5.8 %collective-permute-start.9 = (bf16[512,384]{1,0:T(8,128)(2,1)}, bf16[512,384]{1,0:T(8,128)(2,1)S(1)}, u32[]{:S(2)}, u32[]{:S(2)}) collective-permute-start(bf16[512,384]{1,0:T(8,128)(2,1)} %even_attention.1), channel_id=1, source_target_pairs={{0,4},{1,5},{8,12},{9,13},{16,20},{17,21},{24,28},{25,29},{32,36},... | collective-permute-start | bytes 1179656 | tf_op jit(solution)/shard_map/ppermute | solution.py:376
  57.5 10.5 %collective-permute-done.5.refs_4_ = bf16[2,3,128,384]{3,2,1,0:T(8,128)(2,1)S(1)} collective-permute-done((bf16[2,3,128,384]{3,2,1,0:T(8,128)(2,1)S(1)}, bf16[2,3,128,384]{3,2,1,0:T(8,128)(2,1)S(1)}, u32[]{:S(2)}, u32[]{:S(2)}) %collective-permute-start.5) | collective-permute-done | bytes 589856 | tf_op jit(solution)/shard_map/ppermute | solution.py:430
  68.0 1.9 collective-permute-start.7
  69.9 0.1 convert_reduce_fusion
  70.0 0.6 broadcast_in_dim.29.clip_ref
  70.6 2.8 %collective-permute-done.6.refs_5_ = bf16[2,3,128,384]{3,2,1,0:T(8,128)(2,1)S(1)} collective-permute-done((bf16[2,3,128,384]{3,2,1,0:T(8,128)(2,1)S(1)}, bf16[2,3,128,384]{3,2,1,0:T(8,128)(2,1)S(1)}, u32[]{:S(2)}, u32[]{:S(2)}) %collective-permute-start.6) | collective-permute-done | bytes 589856 | tf_op jit(solution)/shard_map/ppermute | solution.py:431
  73.5 0.8 copy-done.19
  74.3 6.1 %odd_attention.1 = bf16[4,128,384]{2,1,0:T(8,128)(2,1)} custom-call(s32[11]{0:T(128)} %concatenate.6.info_ref, s32[1,288]{1,0:T(1,128)} %broadcast_in_dim.29.clip_ref, bf16[4,128,768]{2,1,0:T(8,128)(2,1)} %bitcast.17, bf16[4,128,768]{2,1,0:T(8,128)(2,1)} %bitcast.14, bf16[4,128,768]{2,1,0:T(8,128)(2,1)} %bitcast.16, bf16[2,3,128,384]{3,2,1,0:T(8,128)(2,1)} %copy-done.16, ...), custom_call_target="tpu_custom_call" | custom-call | flops 226492416 | bytes 7864320 | tf_op jit(solution)/shard_map/odd_attention/pallas_call | solution.py:202
  80.4 2.5 %collective-permute-done.7.refs_0_ = bf16[512,384]{1,0:T(8,128)(2,1)S(1)} collective-permute-done((bf16[512,384]{1,0:T(8,128)(2,1)}, bf16[512,384]{1,0:T(8,128)(2,1)S(1)}, u32[]{:S(2)}, u32[]{:S(2)}) %collective-permute-start.7) | collective-permute-done | bytes 393248 | tf_op jit(solution)/shard_map/ppermute | solution.py:376
  83.0 0.2 pad_maximum_fusion
  83.1 0.1 collective-permute-start.15
  83.2 0.1 collective-permute-start.14
  83.3 8.0 %collective-permute-start.13 = (bf16[512,384]{1,0:T(8,128)(2,1)S(1)}, bf16[512,384]{1,0:T(8,128)(2,1)S(1)}, u32[]{:S(2)}, u32[]{:S(2)}) collective-permute-start(bf16[512,384]{1,0:T(8,128)(2,1)S(1)} %bitcast.19), channel_id=1, source_target_pairs={{0,4},{1,5},{8,12},{9,13},{16,20},{17,21},{24,28},{25,29},{32,36},... | collective-permute-start | bytes 1179656 | tf_op jit(solution)/shard_map/ppermute | solution.py:376
  91.4 1.9 collective-permute-start.12
  93.3 1.9 collective-permute-start.11
  95.3 0.3 collective-permute-start.19
  95.6 13.1 %collective-permute-done.13.refs_5_ = bf16[512,384]{1,0:T(8,128)(2,1)S(1)} collective-permute-done((bf16[512,384]{1,0:T(8,128)(2,1)S(1)}, bf16[512,384]{1,0:T(8,128)(2,1)S(1)}, u32[]{:S(2)}, u32[]{:S(2)}) %collective-permute-start.13) | collective-permute-done | bytes 393248 | tf_op jit(solution)/shard_map/ppermute | solution.py:376
  108.7 5.5 %collective-permute-done.12.refs_3_ = bf16[512,384]{1,0:T(8,128)(2,1)S(1)} collective-permute-done((bf16[512,384]{1,0:T(8,128)(2,1)S(1)}, bf16[512,384]{1,0:T(8,128)(2,1)S(1)}, u32[]{:S(2)}, u32[]{:S(2)}) %collective-permute-start.12) | collective-permute-done | bytes 393248 | tf_op jit(solution)/shard_map/ppermute | solution.py:376
  114.1 7.8 %collective-permute-done.11.refs_1_ = bf16[512,384]{1,0:T(8,128)(2,1)S(1)} collective-permute-done((bf16[512,384]{1,0:T(8,128)(2,1)S(1)}, bf16[512,384]{1,0:T(8,128)(2,1)S(1)}, u32[]{:S(2)}, u32[]{:S(2)}) %collective-permute-start.11) | collective-permute-done | bytes 393248 | tf_op jit(solution)/shard_map/ppermute | solution.py:376
  122.0 1.7 collective-permute-done.16.refs_9_
  123.7 0.7 copy-done.12
  124.5 1.1 copy-done
  125.6 5.2 %project.3 = bf16[512,768]{1,0:T(8,128)(2,1)} custom-call(s32[11]{0:T(128)} %concatenate.6.info_ref, bf16[512,384]{1,0:T(8,128)(2,1)} %copy-done.4, bf16[512,384]{1,0:T(8,128)(2,1)} %copy-done.8, bf16[512,384]{1,0:T(8,128)(2,1)} %copy-done.3, bf16[512,384]{1,0:T(8,128)(2,1)} %copy-done.7, bf16[512,384]{1,0:T(8,128)(2,1)} %copy-done.2, ...), custom_call_target="tpu_custom_call" | custom-call | flops 1207959552 | bytes 4194304 | tf_op jit(solution)/shard_map/project/pallas_call | solution.py:266
  130.8 2.0 %collective-permute-start.20 = (bf16[512,768]{1,0:T(8,128)(2,1)}, bf16[512,768]{1,0:T(8,128)(2,1)S(1)}, u32[]{:S(2)}, u32[]{:S(2)}) collective-permute-start(bf16[512,768]{1,0:T(8,128)(2,1)} %project.3), channel_id=1, source_target_pairs={{0,128},{8,136},{16,144},{24,152},{32,160},{40,168},{48,176},{56,1... | collective-permute-start | bytes 2359304 | tf_op jit(solution)/shard_map/ppermute | solution.py:385
  132.8 7.9 %project.4 = (bf16[512,768]{1,0:T(8,128)(2,1)}, bf16[512,768]{1,0:T(8,128)(2,1)}) custom-call(s32[11]{0:T(128)} %concatenate.6.info_ref, bf16[512,384]{1,0:T(8,128)(2,1)} %copy-done.4, bf16[512,384]{1,0:T(8,128)(2,1)} %copy-done.8, bf16[512,384]{1,0:T(8,128)(2,1)} %copy-done.3, bf16[512,384]{1,0:T(8,128)(2,1)} %copy-done.7, bf16[512,384]{1,0:T(8,128)(2,1)} %copy-done.2, ...), custom_call_target="tpu_custom_call" | custom-call | flops 2415919104 | bytes 4194304 | tf_op jit(solution)/shard_map/project/pallas_call | solution.py:266
  140.7 0.1 collective-permute-start.21
  140.8 2.0 %collective-permute-start.22 = (bf16[512,768]{1,0:T(8,128)(2,1)}, bf16[512,768]{1,0:T(8,128)(2,1)S(1)}, u32[]{:S(2)}, u32[]{:S(2)}) collective-permute-start(bf16[512,768]{1,0:T(8,128)(2,1)} %get-tuple-element.57), channel_id=1, source_target_pairs={{0,192},{8,200},{16,208},{24,216},{32,224},{40,232},{48,240},{56,2... | collective-permute-start | bytes 2359304 | tf_op jit(solution)/shard_map/ppermute | solution.py:385
  142.8 5.5 %project.5.own_ref = f32[512,768]{1,0:T(8,128)} custom-call(s32[11]{0:T(128)} %concatenate.6.info_ref, bf16[512,384]{1,0:T(8,128)(2,1)} %copy-done.4, bf16[512,384]{1,0:T(8,128)(2,1)} %copy-done.8, bf16[512,384]{1,0:T(8,128)(2,1)} %copy-done.3, bf16[512,384]{1,0:T(8,128)(2,1)} %copy-done.7, bf16[512,384]{1,0:T(8,128)(2,1)} %copy-done.2, ...), custom_call_target="tpu_custom_call" | custom-call | flops 1207959552 | bytes 4194304 | tf_op jit(solution)/shard_map/project/pallas_call | solution.py:266
  148.3 4.7 %collective-permute-done.20.p0_ref = bf16[512,768]{1,0:T(8,128)(2,1)S(1)} collective-permute-done((bf16[512,768]{1,0:T(8,128)(2,1)}, bf16[512,768]{1,0:T(8,128)(2,1)S(1)}, u32[]{:S(2)}, u32[]{:S(2)}) %collective-permute-start.20) | collective-permute-done | bytes 786464 | tf_op jit(solution)/shard_map/ppermute | solution.py:385
  153.0 14.4 %collective-permute-done.21.p1_ref = bf16[512,768]{1,0:T(8,128)(2,1)S(1)} collective-permute-done((bf16[512,768]{1,0:T(8,128)(2,1)}, bf16[512,768]{1,0:T(8,128)(2,1)S(1)}, u32[]{:S(2)}, u32[]{:S(2)}) %collective-permute-start.21) | collective-permute-done | bytes 786464 | tf_op jit(solution)/shard_map/ppermute | solution.py:385
  167.5 1.5 collective-permute-done.22.p2_ref
  169.0 0.9 copy-done.15
  169.9 4.1 %update.1 = (bf16[512,768]{1,0:T(8,128)(2,1)}, f32[4,1,128]{2,1,0:T(1,128)}) custom-call(s32[11]{0:T(128)} %concatenate.6.info_ref, f32[512,768]{1,0:T(8,128)} %project.5.own_ref, bf16[512,768]{1,0:T(8,128)(2,1)} %copy-done.13, bf16[512,768]{1,0:T(8,128)(2,1)} %copy-done.14, bf16[512,768]{1,0:T(8,128)(2,1)} %copy-done.15, bf16[512,768]{1,0:T(8,128)(2,1)} %residual_ref.1, ...), custom_call_target="tpu_custom_call" | custom-call | bytes 5505024 | tf_op jit(solution)/shard_map/update/pallas_call | solution.py:318
  174.1 0.0 collective-permute-start.23
  174.1 1.4 collective-permute-done.23
  175.4 0.7 add.30.s0_ref
  176.1 2.5 %collective-permute-start.26 = (f32[4,1,128]{2,1,0:T(1,128)S(1)}, f32[4,1,128]{2,1,0:T(1,128)S(1)}, u32[]{:S(2)}, u32[]{:S(2)}) collective-permute-start(f32[4,1,128]{2,1,0:T(1,128)S(1)} %add.30.s0_ref), channel_id=1, source_target_pairs={{0,2},{1,3},{2,4},{3,5},{4,6},{5,7},{6,0},{7,1},{8,10},{9,11},{10,... | collective-permute-start | bytes 6152 | tf_op jit(solution)/shard_map/ppermute | solution.py:60
  178.6 3.3 %collective-permute-start.25 = (f32[4,1,128]{2,1,0:T(1,128)S(1)}, f32[4,1,128]{2,1,0:T(1,128)S(1)}, u32[]{:S(2)}, u32[]{:S(2)}) collective-permute-start(f32[4,1,128]{2,1,0:T(1,128)S(1)} %add.30.s0_ref), channel_id=1, source_target_pairs={{0,4},{1,5},{2,6},{3,7},{4,0},{5,1},{6,2},{7,3},{8,12},{9,13},{10,... | collective-permute-start | bytes 6152 | tf_op jit(solution)/shard_map/ppermute | solution.py:60
  181.9 0.1 collective-permute-done.26.s3_ref
  182.0 1.7 collective-permute-done.25.s2_ref
  183.7 1.8 collective-permute-done.24.s1_ref
  185.5 0.6 copy-done.28
  186.0 3.0 %norm.1 = bf16[512,768]{1,0:T(8,128)(2,1)} custom-call(s32[11]{0:T(128)} %concatenate.6.info_ref, bf16[512,768]{1,0:T(8,128)(2,1)} %get-tuple-element.29.u_ref, f32[4,1,128]{2,1,0:T(1,128)} %copy-done.24, f32[4,1,128]{2,1,0:T(1,128)} %copy-done.28, f32[4,1,128]{2,1,0:T(1,128)} %copy-done.27, f32[4,1,128]{2,1,0:T(1,128)} %copy-done.26, ...), custom_call_target="tpu_custom_call" | custom-call | bytes 1572864 | tf_op jit(solution)/shard_map/norm/pallas_call | solution.py:355
  (72 shorter events, 0.2 us)
Async XLA Ops:
  7.2 117.3 %all-gather.3.cloned.1.call-start = ((), (), s32[]{:S(2)}) async-start(), calls=%async_computation | async-start | bytes 2654208 | tf_op jit(solution)/shard_map/all_gather | solution.py:372
  7.2 62.7 %copy-start.25 = (s32[288]{0:T(512)S(1)}, s32[288]{0:T(512)}, u32[]{:S(2)}) copy-start(s32[288]{0:T(512)} %constant.57.clone) | copy-start | bytes 3460
  10.5 36.2 %collective-permute-start = (bf16[2,3,128,384]{3,2,1,0:T(8,128)(2,1)}, bf16[2,3,128,384]{3,2,1,0:T(8,128)(2,1)S(1)}, u32[]{:S(2)}, u32[]{:S(2)}) collective-permute-start(bf16[2,3,128,384]{3,2,1,0:T(8,128)(2,1)} %get-tuple-element.36), channel_id=1, source_target_pairs={{0,8},{8,16},{16,24},{24,32},{32,40},{40,48},{48,56},{56,64},{64,7... | collective-permute-start | bytes 1769480 | tf_op jit(solution)/shard_map/ppermute | solution.py:409
  12.4 34.3 %collective-permute-start.1 = (bf16[2,3,128,384]{3,2,1,0:T(8,128)(2,1)}, bf16[2,3,128,384]{3,2,1,0:T(8,128)(2,1)S(1)}, u32[]{:S(2)}, u32[]{:S(2)}) collective-permute-start(bf16[2,3,128,384]{3,2,1,0:T(8,128)(2,1)} %get-tuple-element.37), channel_id=1, source_target_pairs={{0,248},{8,0},{16,8},{24,16},{32,24},{40,32},{48,40},{56,48},{64,5... | collective-permute-start | bytes 1769480 | tf_op jit(solution)/shard_map/ppermute | solution.py:410
  16.3 30.3 %collective-permute-start.4 = (bf16[192,768]{1,0:T(8,128)(2,1)}, bf16[192,768]{1,0:T(8,128)(2,1)S(1)}, u32[]{:S(2)}, u32[]{:S(2)}) collective-permute-start(bf16[192,768]{1,0:T(8,128)(2,1)} %bitcast.23), channel_id=1, source_target_pairs={{0,0},{1,8},{8,16},{9,24},{16,32},{17,40},{24,48},{25,56},{32,1},{... | collective-permute-start | bytes 884744 | tf_op jit(solution)/shard_map/ppermute | solution.py:405
  22.2 24.5 %collective-permute-start.2 = (bf16[2,1,128,384]{3,2,1,0:T(8,128)(2,1)}, bf16[2,1,128,384]{3,2,1,0:T(8,128)(2,1)S(1)}, u32[]{:S(2)}, u32[]{:S(2)}) collective-permute-start(bf16[2,1,128,384]{3,2,1,0:T(8,128)(2,1)} %get-tuple-element.38), channel_id=1, source_target_pairs={{0,8},{8,16},{16,24},{24,32},{32,40},{40,48},{48,56},{56,64},{64,7... | collective-permute-start | bytes 589832 | tf_op jit(solution)/shard_map/ppermute | solution.py:411
  22.3 24.4 %collective-permute-start.3 = (bf16[2,1,128,384]{3,2,1,0:T(8,128)(2,1)}, bf16[2,1,128,384]{3,2,1,0:T(8,128)(2,1)S(1)}, u32[]{:S(2)}, u32[]{:S(2)}) collective-permute-start(bf16[2,1,128,384]{3,2,1,0:T(8,128)(2,1)} %get-tuple-element.39), channel_id=1, source_target_pairs={{0,248},{8,0},{16,8},{24,16},{32,24},{40,32},{48,40},{56,48},{64,5... | collective-permute-start | bytes 589832 | tf_op jit(solution)/shard_map/ppermute | solution.py:412
  46.6 26.8 %copy-start.22 = (bf16[2,1,128,384]{3,2,1,0:T(8,128)(2,1)}, bf16[2,1,128,384]{3,2,1,0:T(8,128)(2,1)S(1)}, u32[]{:S(2)}) copy-start(bf16[2,1,128,384]{3,2,1,0:T(8,128)(2,1)S(1)} %collective-permute-done.2.refs_1_) | copy-start | bytes 589828
  46.6 26.8 %copy-start.23 = (bf16[2,1,128,384]{3,2,1,0:T(8,128)(2,1)}, bf16[2,1,128,384]{3,2,1,0:T(8,128)(2,1)S(1)}, u32[]{:S(2)}) copy-start(bf16[2,1,128,384]{3,2,1,0:T(8,128)(2,1)S(1)} %collective-permute-done.3.refs_3_) | copy-start | bytes 589828
  46.6 0.8 copy-start.21
  46.7 26.8 %copy-start.16 = (bf16[2,3,128,384]{3,2,1,0:T(8,128)(2,1)}, bf16[2,3,128,384]{3,2,1,0:T(8,128)(2,1)S(1)}, u32[]{:S(2)}) copy-start(bf16[2,3,128,384]{3,2,1,0:T(8,128)(2,1)S(1)} %collective-permute-done.refs_0_) | copy-start | bytes 1769476
  46.7 26.8 %copy-start.17 = (bf16[2,3,128,384]{3,2,1,0:T(8,128)(2,1)}, bf16[2,3,128,384]{3,2,1,0:T(8,128)(2,1)S(1)}, u32[]{:S(2)}) copy-start(bf16[2,3,128,384]{3,2,1,0:T(8,128)(2,1)S(1)} %collective-permute-done.1.refs_2_) | copy-start | bytes 1769476
  47.4 20.6 %collective-permute-start.5 = (bf16[2,3,128,384]{3,2,1,0:T(8,128)(2,1)S(1)}, bf16[2,3,128,384]{3,2,1,0:T(8,128)(2,1)S(1)}, u32[]{:S(2)}, u32[]{:S(2)}) collective-permute-start(bf16[2,3,128,384]{3,2,1,0:T(8,128)(2,1)S(1)} %collective-permute-done.refs_0_), channel_id=1, source_target_pairs={{0,8},{8,16},{16,24},{24,32},{32,40},{40,48},{48,56},{56,64},{64,7... | collective-permute-start | bytes 1769480 | tf_op jit(solution)/shard_map/ppermute | solution.py:430
  47.5 25.9 %collective-permute-start.6 = (bf16[2,3,128,384]{3,2,1,0:T(8,128)(2,1)S(1)}, bf16[2,3,128,384]{3,2,1,0:T(8,128)(2,1)S(1)}, u32[]{:S(2)}, u32[]{:S(2)}) collective-permute-start(bf16[2,3,128,384]{3,2,1,0:T(8,128)(2,1)S(1)} %collective-permute-done.1.refs_2_), channel_id=1, source_target_pairs={{0,248},{8,0},{16,8},{24,16},{32,24},{40,32},{48,40},{56,48},{64,5... | collective-permute-start | bytes 1769480 | tf_op jit(solution)/shard_map/ppermute | solution.py:431
  51.6 28.8 %collective-permute-start.10 = (bf16[512,384]{1,0:T(8,128)(2,1)}, bf16[512,384]{1,0:T(8,128)(2,1)S(1)}, u32[]{:S(2)}, u32[]{:S(2)}) collective-permute-start(bf16[512,384]{1,0:T(8,128)(2,1)} %even_attention.1), channel_id=1, source_target_pairs={{0,6},{1,7},{8,14},{9,15},{16,22},{17,23},{24,30},{25,31},{32,38},... | collective-permute-start | bytes 1179656 | tf_op jit(solution)/shard_map/ppermute | solution.py:376
  51.6 28.8 %collective-permute-start.9 = (bf16[512,384]{1,0:T(8,128)(2,1)}, bf16[512,384]{1,0:T(8,128)(2,1)S(1)}, u32[]{:S(2)}, u32[]{:S(2)}) collective-permute-start(bf16[512,384]{1,0:T(8,128)(2,1)} %even_attention.1), channel_id=1, source_target_pairs={{0,4},{1,5},{8,12},{9,13},{16,20},{17,21},{24,28},{25,29},{32,36},... | collective-permute-start | bytes 1179656 | tf_op jit(solution)/shard_map/ppermute | solution.py:376
  57.5 23.0 %collective-permute-start.8 = (bf16[512,384]{1,0:T(8,128)(2,1)}, bf16[512,384]{1,0:T(8,128)(2,1)S(1)}, u32[]{:S(2)}, u32[]{:S(2)}) collective-permute-start(bf16[512,384]{1,0:T(8,128)(2,1)} %even_attention.1), channel_id=1, source_target_pairs={{0,2},{1,3},{8,10},{9,11},{16,18},{17,19},{24,26},{25,27},{32,34},... | collective-permute-start | bytes 1179656 | tf_op jit(solution)/shard_map/ppermute | solution.py:376
  68.0 5.5 %copy-start.18 = (bf16[2,3,128,384]{3,2,1,0:T(8,128)(2,1)}, bf16[2,3,128,384]{3,2,1,0:T(8,128)(2,1)S(1)}, u32[]{:S(2)}) copy-start(bf16[2,3,128,384]{3,2,1,0:T(8,128)(2,1)S(1)} %collective-permute-done.5.refs_4_) | copy-start | bytes 1769476
  68.0 15.0 %collective-permute-start.7 = (bf16[512,384]{1,0:T(8,128)(2,1)}, bf16[512,384]{1,0:T(8,128)(2,1)S(1)}, u32[]{:S(2)}, u32[]{:S(2)}) collective-permute-start(bf16[512,384]{1,0:T(8,128)(2,1)} %even_attention.1), channel_id=1, source_target_pairs={{0,0},{1,1},{8,8},{9,9},{16,16},{17,17},{24,24},{25,25},{32,32},{3... | collective-permute-start | bytes 1179656 | tf_op jit(solution)/shard_map/ppermute | solution.py:376
  73.4 0.8 copy-start.19
  80.4 2.8 %copy-start.20 = (bf16[4,128,384]{2,1,0:T(8,128)(2,1)S(1)}, bf16[4,128,384]{2,1,0:T(8,128)(2,1)}, u32[]{:S(2)}) copy-start(bf16[4,128,384]{2,1,0:T(8,128)(2,1)} %odd_attention.1) | copy-start | bytes 1179652
  80.4 44.0 %copy-start.1 = (bf16[512,384]{1,0:T(8,128)(2,1)}, bf16[512,384]{1,0:T(8,128)(2,1)S(1)}, u32[]{:S(2)}) copy-start(bf16[512,384]{1,0:T(8,128)(2,1)S(1)} %collective-permute-done.10.refs_6_) | copy-start | bytes 1179652
  80.4 44.0 %copy-start.2 = (bf16[512,384]{1,0:T(8,128)(2,1)}, bf16[512,384]{1,0:T(8,128)(2,1)S(1)}, u32[]{:S(2)}) copy-start(bf16[512,384]{1,0:T(8,128)(2,1)S(1)} %collective-permute-done.9.refs_4_) | copy-start | bytes 1179652
  80.4 44.0 %copy-start.3 = (bf16[512,384]{1,0:T(8,128)(2,1)}, bf16[512,384]{1,0:T(8,128)(2,1)S(1)}, u32[]{:S(2)}) copy-start(bf16[512,384]{1,0:T(8,128)(2,1)S(1)} %collective-permute-done.8.refs_2_) | copy-start | bytes 1179652
  83.0 41.5 %copy-start.4 = (bf16[512,384]{1,0:T(8,128)(2,1)}, bf16[512,384]{1,0:T(8,128)(2,1)S(1)}, u32[]{:S(2)}) copy-start(bf16[512,384]{1,0:T(8,128)(2,1)S(1)} %collective-permute-done.7.refs_0_) | copy-start | bytes 1179652
  83.1 41.3 %collective-permute-start.15 = (bf16[2048,384]{1,0:T(8,128)(2,1)S(1)}, bf16[2048,384]{1,0:T(8,128)(2,1)S(1)}, u32[]{:S(2)}, u32[]{:S(2)}) collective-permute-start(bf16[2048,384]{1,0:T(8,128)(2,1)S(1)} %pad_maximum_fusion), channel_id=1, source_target_pairs={{0,1},{1,0},{2,3},{3,2},{4,5},{5,4},{6,7},{7,6},{8,9},{9,8},{10,11... | collective-permute-start | bytes 4718600 | tf_op jit(solution)/shard_map/ppermute | solution.py:60
  83.2 12.0 %collective-permute-start.14 = (bf16[512,384]{1,0:T(8,128)(2,1)S(1)}, bf16[512,384]{1,0:T(8,128)(2,1)S(1)}, u32[]{:S(2)}, u32[]{:S(2)}) collective-permute-start(bf16[512,384]{1,0:T(8,128)(2,1)S(1)} %bitcast.18), channel_id=1, source_target_pairs={{0,6},{1,7},{8,14},{9,15},{16,22},{17,23},{24,30},{25,31},{32,38},... | collective-permute-start | bytes 1179656 | tf_op jit(solution)/shard_map/ppermute | solution.py:376
  83.3 25.3 %collective-permute-start.13 = (bf16[512,384]{1,0:T(8,128)(2,1)S(1)}, bf16[512,384]{1,0:T(8,128)(2,1)S(1)}, u32[]{:S(2)}, u32[]{:S(2)}) collective-permute-start(bf16[512,384]{1,0:T(8,128)(2,1)S(1)} %bitcast.19), channel_id=1, source_target_pairs={{0,4},{1,5},{8,12},{9,13},{16,20},{17,21},{24,28},{25,29},{32,36},... | collective-permute-start | bytes 1179656 | tf_op jit(solution)/shard_map/ppermute | solution.py:376
  91.4 22.8 %collective-permute-start.12 = (bf16[512,384]{1,0:T(8,128)(2,1)S(1)}, bf16[512,384]{1,0:T(8,128)(2,1)S(1)}, u32[]{:S(2)}, u32[]{:S(2)}) collective-permute-start(bf16[512,384]{1,0:T(8,128)(2,1)S(1)} %bitcast.20), channel_id=1, source_target_pairs={{0,2},{1,3},{8,10},{9,11},{16,18},{17,19},{24,26},{25,27},{32,34},... | collective-permute-start | bytes 1179656 | tf_op jit(solution)/shard_map/ppermute | solution.py:376
  93.3 28.6 %collective-permute-start.11 = (bf16[512,384]{1,0:T(8,128)(2,1)S(1)}, bf16[512,384]{1,0:T(8,128)(2,1)S(1)}, u32[]{:S(2)}, u32[]{:S(2)}) collective-permute-start(bf16[512,384]{1,0:T(8,128)(2,1)S(1)} %bitcast.21), channel_id=1, source_target_pairs={{0,0},{1,1},{8,8},{9,9},{16,16},{17,17},{24,24},{25,25},{32,32},{3... | collective-permute-start | bytes 1179656 | tf_op jit(solution)/shard_map/ppermute | solution.py:376
  95.2 29.2 %copy-start.5 = (bf16[512,384]{1,0:T(8,128)(2,1)}, bf16[512,384]{1,0:T(8,128)(2,1)S(1)}, u32[]{:S(2)}) copy-start(bf16[512,384]{1,0:T(8,128)(2,1)S(1)} %collective-permute-done.14.refs_7_) | copy-start | bytes 1179652
  95.3 26.7 %collective-permute-start.19 = (bf16[512,384]{1,0:T(8,128)(2,1)S(1)}, bf16[512,384]{1,0:T(8,128)(2,1)S(1)}, u32[]{:S(2)}, u32[]{:S(2)}) collective-permute-start(bf16[512,384]{1,0:T(8,128)(2,1)S(1)} %collective-permute-done.14.refs_7_), channel_id=1, source_target_pairs={{0,1},{1,0},{2,3},{3,2},{4,5},{5,4},{6,7},{7,6},{8,9},{9,8},{10,11... | collective-permute-start | bytes 1179656 | tf_op jit(solution)/shard_map/ppermute | solution.py:60
  108.7 13.3 %copy-start.6 = (bf16[512,384]{1,0:T(8,128)(2,1)}, bf16[512,384]{1,0:T(8,128)(2,1)S(1)}, u32[]{:S(2)}) copy-start(bf16[512,384]{1,0:T(8,128)(2,1)S(1)} %collective-permute-done.13.refs_5_) | copy-start | bytes 1179652
  108.7 13.3 %collective-permute-start.18 = (bf16[512,384]{1,0:T(8,128)(2,1)S(1)}, bf16[512,384]{1,0:T(8,128)(2,1)S(1)}, u32[]{:S(2)}, u32[]{:S(2)}) collective-permute-start(bf16[512,384]{1,0:T(8,128)(2,1)S(1)} %collective-permute-done.13.refs_5_), channel_id=1, source_target_pairs={{0,1},{1,0},{2,3},{3,2},{4,5},{5,4},{6,7},{7,6},{8,9},{9,8},{10,11... | collective-permute-start | bytes 1179656 | tf_op jit(solution)/shard_map/ppermute | solution.py:60
  114.1 9.5 %copy-start.7 = (bf16[512,384]{1,0:T(8,128)(2,1)}, bf16[512,384]{1,0:T(8,128)(2,1)S(1)}, u32[]{:S(2)}) copy-start(bf16[512,384]{1,0:T(8,128)(2,1)S(1)} %collective-permute-done.12.refs_3_) | copy-start | bytes 1179652
  114.1 7.8 %collective-permute-start.17 = (bf16[512,384]{1,0:T(8,128)(2,1)S(1)}, bf16[512,384]{1,0:T(8,128)(2,1)S(1)}, u32[]{:S(2)}, u32[]{:S(2)}) collective-permute-start(bf16[512,384]{1,0:T(8,128)(2,1)S(1)} %collective-permute-done.12.refs_3_), channel_id=1, source_target_pairs={{0,1},{1,0},{2,3},{3,2},{4,5},{5,4},{6,7},{7,6},{8,9},{9,8},{10,11... | collective-permute-start | bytes 1179656 | tf_op jit(solution)/shard_map/ppermute | solution.py:60
  121.9 1.7 copy-start.8
  121.9 1.7 collective-permute-start.16
  121.9 1.7 copy-start.9
  122.0 1.7 copy-start.10
  122.0 1.7 copy-start.11
  123.7 0.7 copy-start.12
  124.4 1.2 copy-start
  130.8 22.2 %collective-permute-start.20 = (bf16[512,768]{1,0:T(8,128)(2,1)}, bf16[512,768]{1,0:T(8,128)(2,1)S(1)}, u32[]{:S(2)}, u32[]{:S(2)}) collective-permute-start(bf16[512,768]{1,0:T(8,128)(2,1)} %project.3), channel_id=1, source_target_pairs={{0,128},{8,136},{16,144},{24,152},{32,160},{40,168},{48,176},{56,1... | collective-permute-start | bytes 2359304 | tf_op jit(solution)/shard_map/ppermute | solution.py:385
  140.7 26.8 %collective-permute-start.21 = (bf16[512,768]{1,0:T(8,128)(2,1)}, bf16[512,768]{1,0:T(8,128)(2,1)S(1)}, u32[]{:S(2)}, u32[]{:S(2)}) collective-permute-start(bf16[512,768]{1,0:T(8,128)(2,1)} %get-tuple-element.56), channel_id=1, source_target_pairs={{0,64},{8,72},{16,80},{24,88},{32,96},{40,104},{48,112},{56,120},{... | collective-permute-start | bytes 2359304 | tf_op jit(solution)/shard_map/ppermute | solution.py:385
  140.8 28.2 %collective-permute-start.22 = (bf16[512,768]{1,0:T(8,128)(2,1)}, bf16[512,768]{1,0:T(8,128)(2,1)S(1)}, u32[]{:S(2)}, u32[]{:S(2)}) collective-permute-start(bf16[512,768]{1,0:T(8,128)(2,1)} %get-tuple-element.57), channel_id=1, source_target_pairs={{0,192},{8,200},{16,208},{24,216},{32,224},{40,232},{48,240},{56,2... | collective-permute-start | bytes 2359304 | tf_op jit(solution)/shard_map/ppermute | solution.py:385
  153.0 16.0 %copy-start.13 = (bf16[512,768]{1,0:T(8,128)(2,1)}, bf16[512,768]{1,0:T(8,128)(2,1)S(1)}, u32[]{:S(2)}) copy-start(bf16[512,768]{1,0:T(8,128)(2,1)S(1)} %collective-permute-done.20.p0_ref) | copy-start | bytes 2359300
  167.5 1.5 copy-start.14
  169.0 0.9 copy-start.15
  174.1 1.4 collective-permute-start.23
  176.1 9.4 %copy-start.24 = (f32[4,1,128]{2,1,0:T(1,128)}, f32[4,1,128]{2,1,0:T(1,128)S(1)}, u32[]{:S(2)}) copy-start(f32[4,1,128]{2,1,0:T(1,128)S(1)} %add.30.s0_ref) | copy-start | bytes 6148
  176.1 5.9 %collective-permute-start.26 = (f32[4,1,128]{2,1,0:T(1,128)S(1)}, f32[4,1,128]{2,1,0:T(1,128)S(1)}, u32[]{:S(2)}, u32[]{:S(2)}) collective-permute-start(f32[4,1,128]{2,1,0:T(1,128)S(1)} %add.30.s0_ref), channel_id=1, source_target_pairs={{0,2},{1,3},{2,4},{3,5},{4,6},{5,7},{6,0},{7,1},{8,10},{9,11},{10,... | collective-permute-start | bytes 6152 | tf_op jit(solution)/shard_map/ppermute | solution.py:60
  178.6 5.1 %collective-permute-start.25 = (f32[4,1,128]{2,1,0:T(1,128)S(1)}, f32[4,1,128]{2,1,0:T(1,128)S(1)}, u32[]{:S(2)}, u32[]{:S(2)}) collective-permute-start(f32[4,1,128]{2,1,0:T(1,128)S(1)} %add.30.s0_ref), channel_id=1, source_target_pairs={{0,4},{1,5},{2,6},{3,7},{4,0},{5,1},{6,2},{7,3},{8,12},{9,13},{10,... | collective-permute-start | bytes 6152 | tf_op jit(solution)/shard_map/ppermute | solution.py:60
  181.9 3.6 %collective-permute-start.24 = (f32[4,1,128]{2,1,0:T(1,128)S(1)}, f32[4,1,128]{2,1,0:T(1,128)S(1)}, u32[]{:S(2)}, u32[]{:S(2)}) collective-permute-start(f32[4,1,128]{2,1,0:T(1,128)S(1)} %add.30.s0_ref), channel_id=1, source_target_pairs={{0,6},{1,7},{2,0},{3,1},{4,2},{5,3},{6,4},{7,5},{8,14},{9,15},{10,... | collective-permute-start | bytes 6152 | tf_op jit(solution)/shard_map/ppermute | solution.py:60
  182.0 3.5 %copy-start.26 = (f32[4,1,128]{2,1,0:T(1,128)}, f32[4,1,128]{2,1,0:T(1,128)S(1)}, u32[]{:S(2)}) copy-start(f32[4,1,128]{2,1,0:T(1,128)S(1)} %collective-permute-done.26.s3_ref) | copy-start | bytes 6148
  183.7 1.8 copy-start.27
  185.4 0.6 copy-start.28
Sparse Core Ops, SparseCore 0:
  47.5 43.4 all-gather.2

commit v3 on v2

--- a/solution.py
+++ b/solution.py
@@ -23,6 +23,7 @@
 NT = (((1,), (1,)), ((), ()))
 HBM = pl.BlockSpec(memory_space=pltpu.HBM)
 ROOM = pltpu.CompilerParams(vmem_limit_bytes=56 * 1024 * 1024)
+TIGHT = pltpu.CompilerParams(vmem_limit_bytes=20 * 1024 * 1024)
 
 
 def ring_perm(d):
@@ -219,10 +220,10 @@
 
 
 def project_kernel(shifts, info_ref, *refs):
-    own_refs, other_even, other_odd = refs[: 2 * X], refs[2 * X], refs[2 * X + 1 : 3 * X + 1]
-    w_ref = refs[3 * X + 1]
+    own_refs, other_even, other_odd = refs[: 2 * X], refs[2 * X : 3 * X], refs[3 * X : 4 * X]
+    w_ref = refs[4 * X]
     n = len(shifts)
-    o_refs, (a_buf, w_buf, a_sem, w_sem) = refs[3 * X + 2 : 3 * X + 2 + n], refs[3 * X + 2 + n :]
+    o_refs, (a_buf, w_buf, a_sem, w_sem) = refs[4 * X + 1 : 4 * X + 1 + n], refs[4 * X + 1 + n :]
     x, y, core = info_ref[2 * FR], info_ref[2 * FR + 1], info_ref[2 * FR + 2]
     half = Z // 2
     w_copies = [
@@ -238,7 +239,7 @@
         slot = lax.rem(x - y - d + 2 * X, X)
         for r in range(X):
             sources = [own_refs[2 * r], own_refs[2 * r + 1]]
-            sources += [other_even.at[r * ROWS : (r + 1) * ROWS], other_odd[r]]
+            sources += [other_even[r], other_odd[r]]
 
             @pl.when(slot == r)
             def _(sources=sources, i=i):
@@ -327,7 +328,7 @@
             jax.ShapeDtypeStruct((ROWS, COLS), jnp.bfloat16),
             jax.ShapeDtypeStruct((FR, 1, S), jnp.float32),
         ],
-        compiler_params=ROOM,
+        compiler_params=TIGHT,
         cost_estimate=cost(0, ROWS * COLS * 14),
         name="update",
     )(info, own, *parts, residual, gate)
@@ -372,8 +373,8 @@
     return lax.all_gather(own, "seq", axis=0, tiled=False, axis_index_groups=groups)
 
 
-def spread(a):
-    return [lax.ppermute(a, ("seq", "mp"), spread_perm(r)) for r in range(X)]
+def spread(a, shift):
+    return lax.ppermute(a, ("seq", "mp"), spread_perm(shift))
 
 
 def gather_x(a):
@@ -430,15 +431,17 @@
     right6 = lax.ppermute(right3, "seq", ring_perm(1))
     left6 = lax.ppermute(left3, "seq", ring_perm(-1))
     weights = gather_weight(own_weight)
-    even = spread(even)
+    early = [spread(even, r) for r in range(1, X)]
     others = (right3, right1, left3, left1, right6, left6)
     odd = odd_attention(info, key_clips, queries, keys, values, others)
     odd, even = barrier((odd, even))
-    odd = spread(odd)
-    other_even = mp_move(jnp.concatenate(even, axis=0), 0, 1)
+    odd = [spread(odd, r) for r in range(X)]
+    early, _ = barrier((early, odd[X - 1]))
+    even = [spread(even, 0)] + early
+    other_even = [mp_move(a, 0, 1) for a in even]
     other_odd = [mp_move(a, 0, 1) for a in odd]
     own_parts = [a for pair in zip(even, odd) for a in pair]
-    operands = [*own_parts, other_even, *other_odd, weights]
+    operands = [*own_parts, *other_even, *other_odd, weights]
 
     (far,) = project(info, operands, (2,), jnp.bfloat16)
     far, info = barrier((far, info))

time: 196 us -> 188 us (0.959)
  waiting for transfers between devices: 83.4 us -> 75.7 us
  starting transfers between devices: 50.1 us -> 52.1 us
    ppermute x8, waiting for transfers between devices: 28.9 us -> 17.9 us  [spread(): return lax.ppermute(a, ('seq', 'mp'), spread_perm(shift))]
    ppermute x9 -> x12, starting transfers between devices: 6.18 us -> 9.83 us  [mp_move(): return lax.ppermute(a, 'mp', mp_perm(dx, dc))]
    ppermute x1, waiting for transfers between devices: 2.82 us -> 5.21 us  [local(): left6 = lax.ppermute(left3, 'seq', ring_perm(-1))]
    unnamed x58 -> x64, local copies, waits for them, and re-layouts: 4.92 us -> 4.31 us
    ppermute x9 -> x12, waiting for transfers between devices: 6.6 us -> 7.09 us  [mp_move(): return lax.ppermute(a, 'mp', mp_perm(dx, dc))]
  transfers between devices with their start and end apart: 28 -> 31, of which waited for: 15 -> 16; matrix products, arithmetic and copies ran while one was open for 2% -> 2% of each run, Pallas kernels for 12% -> 13%
where the time goes in v3:
time: 188 us; the launch traced here: 187 us
  waiting for transfers between devices  75.7 us (40%)
  starting transfers between devices  52.1 us (28%)
  Pallas kernels  37.1 us (20%)
  between operations  14.4 us (8%)
  local copies, waits for them, and re-layouts  6.26 us (3%)
    ppermute x3, waiting for transfers between devices, seq_move(): return lax.ppermute(a, 'seq', perm)  21.7 us
    ppermute x8, starting transfers between devices, spread(): return lax.ppermute(a, ('seq', 'mp'), spread_perm(shift))  19.1 us
    pallas_call x3, Pallas kernels, project(): pl.pallas_call(functools.partial(project_kernel, shifts), grid_spec=pltpu...  18.6 us
    ppermute x8, waiting for transfers between devices, spread(): return lax.ppermute(a, ('seq', 'mp'), spread_perm(shift))  17.9 us
    ppermute x1, waiting for transfers between devices, local(): right1 = lax.ppermute(right1, 'seq', ring_perm(1))  13.9 us
    ppermute x12, starting transfers between devices, mp_move(): return lax.ppermute(a, 'mp', mp_perm(dx, dc))  9.83 us
    ppermute x1, waiting for transfers between devices, local(): right6 = lax.ppermute(right3, 'seq', ring_perm(1))  9.81 us
    ppermute x12, waiting for transfers between devices, mp_move(): return lax.ppermute(a, 'mp', mp_perm(dx, dc))  7.09 us
  transfers between devices with their start and end apart: 31, of which 16 were waited for; matrix products, arithmetic and copies ran while one was open for 2% of the time, Pallas kernels for 13%

profile of v3, /device:TPU:8, one launch (start us, length us, event | category | flops | bytes accessed | tf_op | source)
XLA Modules:
  0.0 186.8 jit_solution(16018188242300263692)
XLA Ops:
  7.2 0.0 all-gather.3.cloned.1.call-start
  7.2 3.3 %pack_kv.1 = (bf16[2,3,128,384]{3,2,1,0:T(8,128)(2,1)}, bf16[2,1,128,384]{3,2,1,0:T(8,128)(2,1)}, bf16[2,3,128,384]{3,2,1,0:T(8,128)(2,1)}, bf16[2,1,128,384]{3,2,1,0:T(8,128)(2,1)}) custom-call(bf16[4,128,768]{2,1,0:T(8,128)(2,1)} %bitcast.13, bf16[4,128,768]{2,1,0:T(8,128)(2,1)} %bitcast.15), custom_call_target="tpu_custom_call" | custom-call | bytes 2359296 | tf_op jit(solution)/shard_map/pack_kv/pallas_call | solution.py:83
  10.5 1.9 %collective-permute-start = (bf16[2,3,128,384]{3,2,1,0:T(8,128)(2,1)}, bf16[2,3,128,384]{3,2,1,0:T(8,128)(2,1)S(1)}, u32[]{:S(2)}, u32[]{:S(2)}) collective-permute-start(bf16[2,3,128,384]{3,2,1,0:T(8,128)(2,1)} %get-tuple-element.36), channel_id=1, source_target_pairs={{0,8},{8,16},{16,24},{24,32},{32,40},{40,48},{48,56},{56,64},{64,7... | collective-permute-start | bytes 1769480 | tf_op jit(solution)/shard_map/ppermute | solution.py:410
  12.4 3.9 %collective-permute-start.1 = (bf16[2,3,128,384]{3,2,1,0:T(8,128)(2,1)}, bf16[2,3,128,384]{3,2,1,0:T(8,128)(2,1)S(1)}, u32[]{:S(2)}, u32[]{:S(2)}) collective-permute-start(bf16[2,3,128,384]{3,2,1,0:T(8,128)(2,1)} %get-tuple-element.37), channel_id=1, source_target_pairs={{0,248},{8,0},{16,8},{24,16},{32,24},{40,32},{48,40},{56,48},{64,5... | collective-permute-start | bytes 1769480 | tf_op jit(solution)/shard_map/ppermute | solution.py:411
  16.3 5.8 %collective-permute-start.4 = (bf16[192,768]{1,0:T(8,128)(2,1)}, bf16[192,768]{1,0:T(8,128)(2,1)S(1)}, u32[]{:S(2)}, u32[]{:S(2)}) collective-permute-start(bf16[192,768]{1,0:T(8,128)(2,1)} %bitcast.23), channel_id=1, source_target_pairs={{0,0},{1,8},{8,16},{9,24},{16,32},{17,40},{24,48},{25,56},{32,1},{... | collective-permute-start | bytes 884744 | tf_op jit(solution)/shard_map/ppermute | solution.py:406
  22.2 0.1 collective-permute-start.2
  22.3 4.1 %collective-permute-start.3 = (bf16[2,1,128,384]{3,2,1,0:T(8,128)(2,1)}, bf16[2,1,128,384]{3,2,1,0:T(8,128)(2,1)S(1)}, u32[]{:S(2)}, u32[]{:S(2)}) collective-permute-start(bf16[2,1,128,384]{3,2,1,0:T(8,128)(2,1)} %get-tuple-element.39), channel_id=1, source_target_pairs={{0,248},{8,0},{16,8},{24,16},{32,24},{40,32},{48,40},{56,48},{64,5... | collective-permute-start | bytes 589832 | tf_op jit(solution)/shard_map/ppermute | solution.py:413
  26.4 0.7 copy.15
  27.1 0.1 reduce-window.8
  27.2 0.1 reduce
  27.3 0.2 convert_reduce_fusion.1
  27.5 0.8 select_reduce_fusion
  28.3 0.6 concatenate.3.info_ref
  29.0 3.8 %even_attention.1 = bf16[512,384]{1,0:T(8,128)(2,1)} custom-call(s32[11]{0:T(128)} %concatenate.3.info_ref, bf16[512,768]{1,0:T(8,128)(2,1)} %q_ref, bf16[512,768]{1,0:T(8,128)(2,1)} %k_ref.1, bf16[512,768]{1,0:T(8,128)(2,1)} %v_ref.1), custom_call_target="tpu_custom_call" | custom-call | flops 100663296 | bytes 3145728 | tf_op jit(solution)/shard_map/even_attention/pallas_call | solution.py:131
  32.7 13.9 %collective-permute-done.2.refs_1_ = bf16[2,1,128,384]{3,2,1,0:T(8,128)(2,1)S(1)} collective-permute-done((bf16[2,1,128,384]{3,2,1,0:T(8,128)(2,1)}, bf16[2,1,128,384]{3,2,1,0:T(8,128)(2,1)S(1)}, u32[]{:S(2)}, u32[]{:S(2)}) %collective-permute-start.2) | collective-permute-done | bytes 196640 | tf_op jit(solution)/shard_map/ppermute | solution.py:412
  46.7 0.7 copy-done.24
  47.4 0.0 all-gather.3.cloned.1.call-update
  47.4 0.1 collective-permute-start.5
  47.5 4.1 %collective-permute-start.6 = (bf16[2,3,128,384]{3,2,1,0:T(8,128)(2,1)S(1)}, bf16[2,3,128,384]{3,2,1,0:T(8,128)(2,1)S(1)}, u32[]{:S(2)}, u32[]{:S(2)}) collective-permute-start(bf16[2,3,128,384]{3,2,1,0:T(8,128)(2,1)S(1)} %collective-permute-done.1.refs_2_), channel_id=1, source_target_pairs={{0,248},{8,0},{16,8},{24,16},{32,24},{40,32},{48,40},{56,48},{64,5... | collective-permute-start | bytes 1769480 | tf_op jit(solution)/shard_map/ppermute | solution.py:432
  51.6 0.1 convert_reduce_fusion
  51.7 0.6 broadcast_in_dim.29.clip_ref
  52.3 5.8 %collective-permute-start.10 = (bf16[512,384]{1,0:T(8,128)(2,1)}, bf16[512,384]{1,0:T(8,128)(2,1)S(1)}, u32[]{:S(2)}, u32[]{:S(2)}) collective-permute-start(bf16[512,384]{1,0:T(8,128)(2,1)} %even_attention.1), channel_id=1, source_target_pairs={{0,4},{1,5},{8,12},{9,13},{16,20},{17,21},{24,28},{25,29},{32,36},... | collective-permute-start | bytes 1179656 | tf_op jit(solution)/shard_map/ppermute | solution.py:377
  58.2 9.8 %collective-permute-done.5.refs_4_ = bf16[2,3,128,384]{3,2,1,0:T(8,128)(2,1)S(1)} collective-permute-done((bf16[2,3,128,384]{3,2,1,0:T(8,128)(2,1)S(1)}, bf16[2,3,128,384]{3,2,1,0:T(8,128)(2,1)S(1)}, u32[]{:S(2)}, u32[]{:S(2)}) %collective-permute-start.5) | collective-permute-done | bytes 589856 | tf_op jit(solution)/shard_map/ppermute | solution.py:431
  68.0 5.2 %collective-permute-done.6.refs_5_ = bf16[2,3,128,384]{3,2,1,0:T(8,128)(2,1)S(1)} collective-permute-done((bf16[2,3,128,384]{3,2,1,0:T(8,128)(2,1)S(1)}, bf16[2,3,128,384]{3,2,1,0:T(8,128)(2,1)S(1)}, u32[]{:S(2)}, u32[]{:S(2)}) %collective-permute-start.6) | collective-permute-done | bytes 589856 | tf_op jit(solution)/shard_map/ppermute | solution.py:432
  73.2 0.8 copy-done.22
  74.0 6.3 %odd_attention.1 = bf16[4,128,384]{2,1,0:T(8,128)(2,1)} custom-call(s32[11]{0:T(128)} %concatenate.3.info_ref, s32[1,288]{1,0:T(1,128)} %broadcast_in_dim.29.clip_ref, bf16[4,128,768]{2,1,0:T(8,128)(2,1)} %bitcast.17, bf16[4,128,768]{2,1,0:T(8,128)(2,1)} %bitcast.14, bf16[4,128,768]{2,1,0:T(8,128)(2,1)} %bitcast.16, bf16[2,3,128,384]{3,2,1,0:T(8,128)(2,1)} %copy-done.19, ...), custom_call_target="tpu_custom_call" | custom-call | flops 226492416 | bytes 7864320 | tf_op jit(solution)/shard_map/odd_attention/pallas_call | solution.py:203
  80.3 1.9 %collective-permute-start.7 = (bf16[512,384]{1,0:T(8,128)(2,1)S(1)}, bf16[512,384]{1,0:T(8,128)(2,1)S(1)}, u32[]{:S(2)}, u32[]{:S(2)}) collective-permute-start(bf16[512,384]{1,0:T(8,128)(2,1)S(1)} %copy-done.23), channel_id=1, source_target_pairs={{0,0},{1,1},{8,8},{9,9},{16,16},{17,17},{24,24},{25,25},{32,32},{3... | collective-permute-start | bytes 1179656 | tf_op jit(solution)/shard_map/ppermute | solution.py:377
  82.2 0.1 collective-permute-start.14
  82.3 0.1 collective-permute-start.13
  82.4 3.4 %collective-permute-start.12 = (bf16[512,384]{1,0:T(8,128)(2,1)}, bf16[512,384]{1,0:T(8,128)(2,1)S(1)}, u32[]{:S(2)}, u32[]{:S(2)}) collective-permute-start(bf16[512,384]{1,0:T(8,128)(2,1)} %bitcast.20), channel_id=1, source_target_pairs={{0,6},{1,7},{8,14},{9,15},{16,22},{17,23},{24,30},{25,31},{32,38},... | collective-permute-start | bytes 1179656 | tf_op jit(solution)/shard_map/ppermute | solution.py:377
  85.9 7.8 %collective-permute-start.8 = (bf16[512,384]{1,0:T(8,128)(2,1)}, bf16[512,384]{1,0:T(8,128)(2,1)S(1)}, u32[]{:S(2)}, u32[]{:S(2)}) collective-permute-start(bf16[512,384]{1,0:T(8,128)(2,1)} %bitcast.21), channel_id=1, source_target_pairs={{0,0},{1,1},{8,8},{9,9},{16,16},{17,17},{24,24},{25,25},{32,32},{3... | collective-permute-start | bytes 1179656 | tf_op jit(solution)/shard_map/ppermute | solution.py:377
  93.6 4.8 %collective-permute-done.7.refs_0_ = bf16[512,384]{1,0:T(8,128)(2,1)S(1)} collective-permute-done((bf16[512,384]{1,0:T(8,128)(2,1)S(1)}, bf16[512,384]{1,0:T(8,128)(2,1)S(1)}, u32[]{:S(2)}, u32[]{:S(2)}) %collective-permute-start.7) | collective-permute-done | bytes 393248 | tf_op jit(solution)/shard_map/ppermute | solution.py:377
  98.5 0.5 collective-permute-start.21
  99.0 3.3 %collective-permute-done.13.refs_3_ = bf16[512,384]{1,0:T(8,128)(2,1)S(1)} collective-permute-done((bf16[512,384]{1,0:T(8,128)(2,1)}, bf16[512,384]{1,0:T(8,128)(2,1)S(1)}, u32[]{:S(2)}, u32[]{:S(2)}) %collective-permute-start.13) | collective-permute-done | bytes 393248 | tf_op jit(solution)/shard_map/ppermute | solution.py:377
  102.3 2.0 %collective-permute-start.20 = (bf16[512,384]{1,0:T(8,128)(2,1)S(1)}, bf16[512,384]{1,0:T(8,128)(2,1)S(1)}, u32[]{:S(2)}, u32[]{:S(2)}) collective-permute-start(bf16[512,384]{1,0:T(8,128)(2,1)S(1)} %collective-permute-done.13.refs_3_), channel_id=1, source_target_pairs={{0,1},{1,0},{2,3},{3,2},{4,5},{5,4},{6,7},{7,6},{8,9},{9,8},{10,11... | collective-permute-start | bytes 1179656 | tf_op jit(solution)/shard_map/ppermute | solution.py:61
  104.3 0.1 collective-permute-start.16
  104.4 9.8 %collective-permute-done.8.refs_1_ = bf16[512,384]{1,0:T(8,128)(2,1)S(1)} collective-permute-done((bf16[512,384]{1,0:T(8,128)(2,1)}, bf16[512,384]{1,0:T(8,128)(2,1)S(1)}, u32[]{:S(2)}, u32[]{:S(2)}) %collective-permute-start.8) | collective-permute-done | bytes 393248 | tf_op jit(solution)/shard_map/ppermute | solution.py:377
  114.2 0.5 collective-permute-start.18
  114.7 0.1 collective-permute-start.22
  114.8 0.4 collective-permute-start.19
  115.2 0.7 collective-permute-done.17.refs_10_
  115.9 0.6 collective-permute-done.18.refs_11_
  116.5 1.1 collective-permute-done.22.refs_15_
  117.6 0.7 copy-done.18
  118.4 5.2 %project.3 = bf16[512,768]{1,0:T(8,128)(2,1)} custom-call(s32[11]{0:T(128)} %concatenate.3.info_ref, bf16[512,384]{1,0:T(8,128)(2,1)} %copy-done.7, bf16[512,384]{1,0:T(8,128)(2,1)} %copy-done.11, bf16[512,384]{1,0:T(8,128)(2,1)} %copy-done.6, bf16[512,384]{1,0:T(8,128)(2,1)} %copy-done.9, bf16[512,384]{1,0:T(8,128)(2,1)} %copy-done.5, ...), custom_call_target="tpu_custom_call" | custom-call | flops 1207959552 | bytes 4194304 | tf_op jit(solution)/shard_map/project/pallas_call | solution.py:267
  123.7 1.0 collective-permute-start.23
  124.6 7.9 %project.4 = (bf16[512,768]{1,0:T(8,128)(2,1)}, bf16[512,768]{1,0:T(8,128)(2,1)}) custom-call(s32[11]{0:T(128)} %concatenate.3.info_ref, bf16[512,384]{1,0:T(8,128)(2,1)} %copy-done.7, bf16[512,384]{1,0:T(8,128)(2,1)} %copy-done.11, bf16[512,384]{1,0:T(8,128)(2,1)} %copy-done.6, bf16[512,384]{1,0:T(8,128)(2,1)} %copy-done.9, bf16[512,384]{1,0:T(8,128)(2,1)} %copy-done.5, ...), custom_call_target="tpu_custom_call" | custom-call | flops 2415919104 | bytes 4194304 | tf_op jit(solution)/shard_map/project/pallas_call | solution.py:267
  132.6 0.1 collective-permute-start.24
  132.7 2.0 %collective-permute-start.25 = (bf16[512,768]{1,0:T(8,128)(2,1)}, bf16[512,768]{1,0:T(8,128)(2,1)S(1)}, u32[]{:S(2)}, u32[]{:S(2)}) collective-permute-start(bf16[512,768]{1,0:T(8,128)(2,1)} %get-tuple-element.57), channel_id=1, source_target_pairs={{0,192},{8,200},{16,208},{24,216},{32,224},{40,232},{48,240},{56,2... | collective-permute-start | bytes 2359304 | tf_op jit(solution)/shard_map/ppermute | solution.py:386
  134.7 5.5 %project.5.own_ref = f32[512,768]{1,0:T(8,128)} custom-call(s32[11]{0:T(128)} %concatenate.3.info_ref, bf16[512,384]{1,0:T(8,128)(2,1)} %copy-done.7, bf16[512,384]{1,0:T(8,128)(2,1)} %copy-done.11, bf16[512,384]{1,0:T(8,128)(2,1)} %copy-done.6, bf16[512,384]{1,0:T(8,128)(2,1)} %copy-done.9, bf16[512,384]{1,0:T(8,128)(2,1)} %copy-done.5, ...), custom_call_target="tpu_custom_call" | custom-call | flops 1207959552 | bytes 4194304 | tf_op jit(solution)/shard_map/project/pallas_call | solution.py:267
  140.2 5.7 %collective-permute-done.23.p0_ref = bf16[512,768]{1,0:T(8,128)(2,1)S(1)} collective-permute-done((bf16[512,768]{1,0:T(8,128)(2,1)}, bf16[512,768]{1,0:T(8,128)(2,1)S(1)}, u32[]{:S(2)}, u32[]{:S(2)}) %collective-permute-start.23) | collective-permute-done | bytes 786464 | tf_op jit(solution)/shard_map/ppermute | solution.py:386
  145.9 12.6 %collective-permute-done.24.p1_ref = bf16[512,768]{1,0:T(8,128)(2,1)S(1)} collective-permute-done((bf16[512,768]{1,0:T(8,128)(2,1)}, bf16[512,768]{1,0:T(8,128)(2,1)S(1)}, u32[]{:S(2)}, u32[]{:S(2)}) %collective-permute-start.24) | collective-permute-done | bytes 786464 | tf_op jit(solution)/shard_map/ppermute | solution.py:386
  158.5 3.4 %collective-permute-done.25.p2_ref = bf16[512,768]{1,0:T(8,128)(2,1)S(1)} collective-permute-done((bf16[512,768]{1,0:T(8,128)(2,1)}, bf16[512,768]{1,0:T(8,128)(2,1)S(1)}, u32[]{:S(2)}, u32[]{:S(2)}) %collective-permute-start.25) | collective-permute-done | bytes 786464 | tf_op jit(solution)/shard_map/ppermute | solution.py:386
  161.9 1.4 copy-done
  163.3 2.2 %update.1 = (bf16[512,768]{1,0:T(8,128)(2,1)}, f32[4,1,128]{2,1,0:T(1,128)S(1)}) custom-call(s32[11]{0:T(128)S(1)} %copy-done.3, f32[512,768]{1,0:T(8,128)S(1)} %copy-done, bf16[512,768]{1,0:T(8,128)(2,1)S(1)} %collective-permute-done.23.p0_ref, bf16[512,768]{1,0:T(8,128)(2,1)S(1)} %collective-permute-done.24.p1_ref, ...), custom_call_target="tpu_custom_call" | custom-call | bytes 5505024 | tf_op jit(solution)/shard_map/update/pallas_call | solution.py:319
  165.5 0.0 collective-permute-start.26
  165.5 1.1 collective-permute-done.26
  166.6 2.7 %collective-permute-start.29 = (f32[4,1,128]{2,1,0:T(1,128)S(1)}, f32[4,1,128]{2,1,0:T(1,128)S(1)}, u32[]{:S(2)}, u32[]{:S(2)}) collective-permute-start(f32[4,1,128]{2,1,0:T(1,128)S(1)} %add.30.s0_ref), channel_id=1, source_target_pairs={{0,2},{1,3},{2,4},{3,5},{4,6},{5,7},{6,0},{7,1},{8,10},{9,11},{10,... | collective-permute-start | bytes 6152 | tf_op jit(solution)/shard_map/ppermute | solution.py:61
  169.3 3.5 %collective-permute-start.28 = (f32[4,1,128]{2,1,0:T(1,128)S(1)}, f32[4,1,128]{2,1,0:T(1,128)S(1)}, u32[]{:S(2)}, u32[]{:S(2)}) collective-permute-start(f32[4,1,128]{2,1,0:T(1,128)S(1)} %add.30.s0_ref), channel_id=1, source_target_pairs={{0,4},{1,5},{2,6},{3,7},{4,0},{5,1},{6,2},{7,3},{8,12},{9,13},{10,... | collective-permute-start | bytes 6152 | tf_op jit(solution)/shard_map/ppermute | solution.py:61
  172.8 0.1 collective-permute-done.29.s3_ref
  172.9 1.5 collective-permute-done.28.s2_ref
  174.4 2.0 %collective-permute-done.27.s1_ref = f32[4,1,128]{2,1,0:T(1,128)S(1)} collective-permute-done((f32[4,1,128]{2,1,0:T(1,128)S(1)}, f32[4,1,128]{2,1,0:T(1,128)S(1)}, u32[]{:S(2)}, u32[]{:S(2)}) %collective-permute-start.27) | collective-permute-done | bytes 2080 | tf_op jit(solution)/shard_map/ppermute | solution.py:61
  176.4 0.6 copy-done.31
  177.0 3.0 %norm.1 = bf16[512,768]{1,0:T(8,128)(2,1)} custom-call(s32[11]{0:T(128)} %concatenate.3.info_ref, bf16[512,768]{1,0:T(8,128)(2,1)} %get-tuple-element.29.u_ref, f32[4,1,128]{2,1,0:T(1,128)} %copy-done.27, f32[4,1,128]{2,1,0:T(1,128)} %copy-done.31, f32[4,1,128]{2,1,0:T(1,128)} %copy-done.30, f32[4,1,128]{2,1,0:T(1,128)} %copy-done.29, ...), custom_call_target="tpu_custom_call" | custom-call | bytes 1572864 | tf_op jit(solution)/shard_map/norm/pallas_call | solution.py:356
  (83 shorter events, 0.2 us)
Async XLA Ops:
  7.2 111.2 %all-gather.3.cloned.1.call-start = ((), (), s32[]{:S(2)}) async-start(), calls=%async_computation | async-start | bytes 2654208 | tf_op jit(solution)/shard_map/all_gather | solution.py:373
  7.2 44.4 %copy-start.28 = (s32[288]{0:T(512)S(1)}, s32[288]{0:T(512)}, u32[]{:S(2)}) copy-start(s32[288]{0:T(512)} %constant.57.clone) | copy-start | bytes 3460
  10.5 36.2 %collective-permute-start = (bf16[2,3,128,384]{3,2,1,0:T(8,128)(2,1)}, bf16[2,3,128,384]{3,2,1,0:T(8,128)(2,1)S(1)}, u32[]{:S(2)}, u32[]{:S(2)}) collective-permute-start(bf16[2,3,128,384]{3,2,1,0:T(8,128)(2,1)} %get-tuple-element.36), channel_id=1, source_target_pairs={{0,8},{8,16},{16,24},{24,32},{32,40},{40,48},{48,56},{56,64},{64,7... | collective-permute-start | bytes 1769480 | tf_op jit(solution)/shard_map/ppermute | solution.py:410
  12.4 34.3 %collective-permute-start.1 = (bf16[2,3,128,384]{3,2,1,0:T(8,128)(2,1)}, bf16[2,3,128,384]{3,2,1,0:T(8,128)(2,1)S(1)}, u32[]{:S(2)}, u32[]{:S(2)}) collective-permute-start(bf16[2,3,128,384]{3,2,1,0:T(8,128)(2,1)} %get-tuple-element.37), channel_id=1, source_target_pairs={{0,248},{8,0},{16,8},{24,16},{32,24},{40,32},{48,40},{56,48},{64,5... | collective-permute-start | bytes 1769480 | tf_op jit(solution)/shard_map/ppermute | solution.py:411
  16.3 30.3 %collective-permute-start.4 = (bf16[192,768]{1,0:T(8,128)(2,1)}, bf16[192,768]{1,0:T(8,128)(2,1)S(1)}, u32[]{:S(2)}, u32[]{:S(2)}) collective-permute-start(bf16[192,768]{1,0:T(8,128)(2,1)} %bitcast.23), channel_id=1, source_target_pairs={{0,0},{1,8},{8,16},{9,24},{16,32},{17,40},{24,48},{25,56},{32,1},{... | collective-permute-start | bytes 884744 | tf_op jit(solution)/shard_map/ppermute | solution.py:406
  22.2 24.5 %collective-permute-start.2 = (bf16[2,1,128,384]{3,2,1,0:T(8,128)(2,1)}, bf16[2,1,128,384]{3,2,1,0:T(8,128)(2,1)S(1)}, u32[]{:S(2)}, u32[]{:S(2)}) collective-permute-start(bf16[2,1,128,384]{3,2,1,0:T(8,128)(2,1)} %get-tuple-element.38), channel_id=1, source_target_pairs={{0,8},{8,16},{16,24},{24,32},{32,40},{40,48},{48,56},{56,64},{64,7... | collective-permute-start | bytes 589832 | tf_op jit(solution)/shard_map/ppermute | solution.py:412
  22.3 24.4 %collective-permute-start.3 = (bf16[2,1,128,384]{3,2,1,0:T(8,128)(2,1)}, bf16[2,1,128,384]{3,2,1,0:T(8,128)(2,1)S(1)}, u32[]{:S(2)}, u32[]{:S(2)}) collective-permute-start(bf16[2,1,128,384]{3,2,1,0:T(8,128)(2,1)} %get-tuple-element.39), channel_id=1, source_target_pairs={{0,248},{8,0},{16,8},{24,16},{32,24},{40,32},{48,40},{56,48},{64,5... | collective-permute-start | bytes 589832 | tf_op jit(solution)/shard_map/ppermute | solution.py:413
  46.6 26.6 %copy-start.25 = (bf16[2,1,128,384]{3,2,1,0:T(8,128)(2,1)}, bf16[2,1,128,384]{3,2,1,0:T(8,128)(2,1)S(1)}, u32[]{:S(2)}) copy-start(bf16[2,1,128,384]{3,2,1,0:T(8,128)(2,1)S(1)} %collective-permute-done.2.refs_1_) | copy-start | bytes 589828
  46.6 26.6 %copy-start.26 = (bf16[2,1,128,384]{3,2,1,0:T(8,128)(2,1)}, bf16[2,1,128,384]{3,2,1,0:T(8,128)(2,1)S(1)}, u32[]{:S(2)}) copy-start(bf16[2,1,128,384]{3,2,1,0:T(8,128)(2,1)S(1)} %collective-permute-done.3.refs_3_) | copy-start | bytes 589828
  46.6 0.7 copy-start.24
  46.7 26.5 %copy-start.19 = (bf16[2,3,128,384]{3,2,1,0:T(8,128)(2,1)}, bf16[2,3,128,384]{3,2,1,0:T(8,128)(2,1)S(1)}, u32[]{:S(2)}) copy-start(bf16[2,3,128,384]{3,2,1,0:T(8,128)(2,1)S(1)} %collective-permute-done.refs_0_) | copy-start | bytes 1769476
  46.7 26.5 %copy-start.20 = (bf16[2,3,128,384]{3,2,1,0:T(8,128)(2,1)}, bf16[2,3,128,384]{3,2,1,0:T(8,128)(2,1)S(1)}, u32[]{:S(2)}) copy-start(bf16[2,3,128,384]{3,2,1,0:T(8,128)(2,1)S(1)} %collective-permute-done.1.refs_2_) | copy-start | bytes 1769476
  47.4 20.6 %collective-permute-start.5 = (bf16[2,3,128,384]{3,2,1,0:T(8,128)(2,1)S(1)}, bf16[2,3,128,384]{3,2,1,0:T(8,128)(2,1)S(1)}, u32[]{:S(2)}, u32[]{:S(2)}) collective-permute-start(bf16[2,3,128,384]{3,2,1,0:T(8,128)(2,1)S(1)} %collective-permute-done.refs_0_), channel_id=1, source_target_pairs={{0,8},{8,16},{16,24},{24,32},{32,40},{40,48},{48,56},{56,64},{64,7... | collective-permute-start | bytes 1769480 | tf_op jit(solution)/shard_map/ppermute | solution.py:431
  47.5 25.7 %collective-permute-start.6 = (bf16[2,3,128,384]{3,2,1,0:T(8,128)(2,1)S(1)}, bf16[2,3,128,384]{3,2,1,0:T(8,128)(2,1)S(1)}, u32[]{:S(2)}, u32[]{:S(2)}) collective-permute-start(bf16[2,3,128,384]{3,2,1,0:T(8,128)(2,1)S(1)} %collective-permute-done.1.refs_2_), channel_id=1, source_target_pairs={{0,248},{8,0},{16,8},{24,16},{32,24},{40,32},{48,40},{56,48},{64,5... | collective-permute-start | bytes 1769480 | tf_op jit(solution)/shard_map/ppermute | solution.py:432
  51.6 30.7 %collective-permute-start.11 = (bf16[512,384]{1,0:T(8,128)(2,1)}, bf16[512,384]{1,0:T(8,128)(2,1)S(1)}, u32[]{:S(2)}, u32[]{:S(2)}) collective-permute-start(bf16[512,384]{1,0:T(8,128)(2,1)} %even_attention.1), channel_id=1, source_target_pairs={{0,6},{1,7},{8,14},{9,15},{16,22},{17,23},{24,30},{25,31},{32,38},... | collective-permute-start | bytes 1179656 | tf_op jit(solution)/shard_map/ppermute | solution.py:377
  52.3 30.1 %collective-permute-start.10 = (bf16[512,384]{1,0:T(8,128)(2,1)}, bf16[512,384]{1,0:T(8,128)(2,1)S(1)}, u32[]{:S(2)}, u32[]{:S(2)}) collective-permute-start(bf16[512,384]{1,0:T(8,128)(2,1)} %even_attention.1), channel_id=1, source_target_pairs={{0,4},{1,5},{8,12},{9,13},{16,20},{17,21},{24,28},{25,29},{32,36},... | collective-permute-start | bytes 1179656 | tf_op jit(solution)/shard_map/ppermute | solution.py:377
  58.2 27.7 %collective-permute-start.9 = (bf16[512,384]{1,0:T(8,128)(2,1)}, bf16[512,384]{1,0:T(8,128)(2,1)S(1)}, u32[]{:S(2)}, u32[]{:S(2)}) collective-permute-start(bf16[512,384]{1,0:T(8,128)(2,1)} %even_attention.1), channel_id=1, source_target_pairs={{0,2},{1,3},{8,10},{9,11},{16,18},{17,19},{24,26},{25,27},{32,34},... | collective-permute-start | bytes 1179656 | tf_op jit(solution)/shard_map/ppermute | solution.py:377
  68.0 5.2 %copy-start.21 = (bf16[2,3,128,384]{3,2,1,0:T(8,128)(2,1)}, bf16[2,3,128,384]{3,2,1,0:T(8,128)(2,1)S(1)}, u32[]{:S(2)}) copy-start(bf16[2,3,128,384]{3,2,1,0:T(8,128)(2,1)S(1)} %collective-permute-done.5.refs_4_) | copy-start | bytes 1769476
  73.2 0.8 copy-start.22
  74.0 6.3 %copy-start.23 = (bf16[512,384]{1,0:T(8,128)(2,1)S(1)}, bf16[512,384]{1,0:T(8,128)(2,1)}, u32[]{:S(2)}) copy-start(bf16[512,384]{1,0:T(8,128)(2,1)} %even_attention.1) | copy-start | bytes 1179652
  80.3 18.2 %collective-permute-start.7 = (bf16[512,384]{1,0:T(8,128)(2,1)S(1)}, bf16[512,384]{1,0:T(8,128)(2,1)S(1)}, u32[]{:S(2)}, u32[]{:S(2)}) collective-permute-start(bf16[512,384]{1,0:T(8,128)(2,1)S(1)} %copy-done.23), channel_id=1, source_target_pairs={{0,0},{1,1},{8,8},{9,9},{16,16},{17,17},{24,24},{25,25},{32,32},{3... | collective-permute-start | bytes 1179656 | tf_op jit(solution)/shard_map/ppermute | solution.py:377
  82.2 16.3 %collective-permute-start.14 = (bf16[512,384]{1,0:T(8,128)(2,1)}, bf16[512,384]{1,0:T(8,128)(2,1)S(1)}, u32[]{:S(2)}, u32[]{:S(2)}) collective-permute-start(bf16[512,384]{1,0:T(8,128)(2,1)} %bitcast.18), channel_id=1, source_target_pairs={{0,4},{1,5},{8,12},{9,13},{16,20},{17,21},{24,28},{25,29},{32,36},... | collective-permute-start | bytes 1179656 | tf_op jit(solution)/shard_map/ppermute | solution.py:377
  82.3 36.1 %copy-start.4 = (bf16[512,384]{1,0:T(8,128)(2,1)}, bf16[512,384]{1,0:T(8,128)(2,1)S(1)}, u32[]{:S(2)}) copy-start(bf16[512,384]{1,0:T(8,128)(2,1)S(1)} %collective-permute-done.11.refs_6_) | copy-start | bytes 1179652
  82.3 19.9 %collective-permute-start.13 = (bf16[512,384]{1,0:T(8,128)(2,1)}, bf16[512,384]{1,0:T(8,128)(2,1)S(1)}, u32[]{:S(2)}, u32[]{:S(2)}) collective-permute-start(bf16[512,384]{1,0:T(8,128)(2,1)} %bitcast.19), channel_id=1, source_target_pairs={{0,2},{1,3},{8,10},{9,11},{16,18},{17,19},{24,26},{25,27},{32,34},... | collective-permute-start | bytes 1179656 | tf_op jit(solution)/shard_map/ppermute | solution.py:377
  82.4 36.0 %copy-start.5 = (bf16[512,384]{1,0:T(8,128)(2,1)}, bf16[512,384]{1,0:T(8,128)(2,1)S(1)}, u32[]{:S(2)}) copy-start(bf16[512,384]{1,0:T(8,128)(2,1)S(1)} %collective-permute-done.10.refs_4_) | copy-start | bytes 1179652
  82.4 21.8 %collective-permute-start.12 = (bf16[512,384]{1,0:T(8,128)(2,1)}, bf16[512,384]{1,0:T(8,128)(2,1)S(1)}, u32[]{:S(2)}, u32[]{:S(2)}) collective-permute-start(bf16[512,384]{1,0:T(8,128)(2,1)} %bitcast.20), channel_id=1, source_target_pairs={{0,6},{1,7},{8,14},{9,15},{16,22},{17,23},{24,30},{25,31},{32,38},... | collective-permute-start | bytes 1179656 | tf_op jit(solution)/shard_map/ppermute | solution.py:377
  85.9 32.5 %copy-start.6 = (bf16[512,384]{1,0:T(8,128)(2,1)}, bf16[512,384]{1,0:T(8,128)(2,1)S(1)}, u32[]{:S(2)}) copy-start(bf16[512,384]{1,0:T(8,128)(2,1)S(1)} %collective-permute-done.9.refs_2_) | copy-start | bytes 1179652
  85.9 28.3 %collective-permute-start.8 = (bf16[512,384]{1,0:T(8,128)(2,1)}, bf16[512,384]{1,0:T(8,128)(2,1)S(1)}, u32[]{:S(2)}, u32[]{:S(2)}) collective-permute-start(bf16[512,384]{1,0:T(8,128)(2,1)} %bitcast.21), channel_id=1, source_target_pairs={{0,0},{1,1},{8,8},{9,9},{16,16},{17,17},{24,24},{25,25},{32,32},{3... | collective-permute-start | bytes 1179656 | tf_op jit(solution)/shard_map/ppermute | solution.py:377
  98.5 19.9 %copy-start.7 = (bf16[512,384]{1,0:T(8,128)(2,1)}, bf16[512,384]{1,0:T(8,128)(2,1)S(1)}, u32[]{:S(2)}) copy-start(bf16[512,384]{1,0:T(8,128)(2,1)S(1)} %collective-permute-done.7.refs_0_) | copy-start | bytes 1179652
  98.5 15.7 %collective-permute-start.15 = (bf16[512,384]{1,0:T(8,128)(2,1)S(1)}, bf16[512,384]{1,0:T(8,128)(2,1)S(1)}, u32[]{:S(2)}, u32[]{:S(2)}) collective-permute-start(bf16[512,384]{1,0:T(8,128)(2,1)S(1)} %collective-permute-done.7.refs_0_), channel_id=1, source_target_pairs={{0,1},{1,0},{2,3},{3,2},{4,5},{5,4},{6,7},{7,6},{8,9},{9,8},{10,11... | collective-permute-start | bytes 1179656 | tf_op jit(solution)/shard_map/ppermute | solution.py:61
  98.5 19.9 %copy-start.8 = (bf16[512,384]{1,0:T(8,128)(2,1)}, bf16[512,384]{1,0:T(8,128)(2,1)S(1)}, u32[]{:S(2)}) copy-start(bf16[512,384]{1,0:T(8,128)(2,1)S(1)} %collective-permute-done.14.refs_5_) | copy-start | bytes 1179652
  98.5 16.2 %collective-permute-start.21 = (bf16[512,384]{1,0:T(8,128)(2,1)S(1)}, bf16[512,384]{1,0:T(8,128)(2,1)S(1)}, u32[]{:S(2)}, u32[]{:S(2)}) collective-permute-start(bf16[512,384]{1,0:T(8,128)(2,1)S(1)} %collective-permute-done.14.refs_5_), channel_id=1, source_target_pairs={{0,1},{1,0},{2,3},{3,2},{4,5},{5,4},{6,7},{7,6},{8,9},{9,8},{10,11... | collective-permute-start | bytes 1179656 | tf_op jit(solution)/shard_map/ppermute | solution.py:61
  102.2 16.2 %copy-start.9 = (bf16[512,384]{1,0:T(8,128)(2,1)}, bf16[512,384]{1,0:T(8,128)(2,1)S(1)}, u32[]{:S(2)}) copy-start(bf16[512,384]{1,0:T(8,128)(2,1)S(1)} %collective-permute-done.13.refs_3_) | copy-start | bytes 1179652
  102.3 12.5 %collective-permute-start.20 = (bf16[512,384]{1,0:T(8,128)(2,1)S(1)}, bf16[512,384]{1,0:T(8,128)(2,1)S(1)}, u32[]{:S(2)}, u32[]{:S(2)}) collective-permute-start(bf16[512,384]{1,0:T(8,128)(2,1)S(1)} %collective-permute-done.13.refs_3_), channel_id=1, source_target_pairs={{0,1},{1,0},{2,3},{3,2},{4,5},{5,4},{6,7},{7,6},{8,9},{9,8},{10,11... | collective-permute-start | bytes 1179656 | tf_op jit(solution)/shard_map/ppermute | solution.py:61
  104.3 14.2 %copy-start.10 = (bf16[512,384]{1,0:T(8,128)(2,1)}, bf16[512,384]{1,0:T(8,128)(2,1)S(1)}, u32[]{:S(2)}) copy-start(bf16[512,384]{1,0:T(8,128)(2,1)S(1)} %collective-permute-done.12.refs_7_) | copy-start | bytes 1179652
  104.3 10.9 %collective-permute-start.16 = (bf16[512,384]{1,0:T(8,128)(2,1)S(1)}, bf16[512,384]{1,0:T(8,128)(2,1)S(1)}, u32[]{:S(2)}, u32[]{:S(2)}) collective-permute-start(bf16[512,384]{1,0:T(8,128)(2,1)S(1)} %collective-permute-done.9.refs_2_), channel_id=1, source_target_pairs={{0,1},{1,0},{2,3},{3,2},{4,5},{5,4},{6,7},{7,6},{8,9},{9,8},{10,11... | collective-permute-start | bytes 1179656 | tf_op jit(solution)/shard_map/ppermute | solution.py:61
  114.2 4.3 %copy-start.11 = (bf16[512,384]{1,0:T(8,128)(2,1)}, bf16[512,384]{1,0:T(8,128)(2,1)S(1)}, u32[]{:S(2)}) copy-start(bf16[512,384]{1,0:T(8,128)(2,1)S(1)} %collective-permute-done.8.refs_1_) | copy-start | bytes 1179652
  114.2 1.7 collective-permute-start.17
  114.2 4.3 %copy-start.12 = (bf16[512,384]{1,0:T(8,128)(2,1)}, bf16[512,384]{1,0:T(8,128)(2,1)S(1)}, u32[]{:S(2)}) copy-start(bf16[512,384]{1,0:T(8,128)(2,1)S(1)} %collective-permute-done.15.refs_8_) | copy-start | bytes 1179652
  114.2 2.3 %collective-permute-start.18 = (bf16[512,384]{1,0:T(8,128)(2,1)S(1)}, bf16[512,384]{1,0:T(8,128)(2,1)S(1)}, u32[]{:S(2)}, u32[]{:S(2)}) collective-permute-start(bf16[512,384]{1,0:T(8,128)(2,1)S(1)} %collective-permute-done.11.refs_6_), channel_id=1, source_target_pairs={{0,1},{1,0},{2,3},{3,2},{4,5},{5,4},{6,7},{7,6},{8,9},{9,8},{10,11... | collective-permute-start | bytes 1179656 | tf_op jit(solution)/shard_map/ppermute | solution.py:61
  114.7 2.9 %copy-start.13 = (bf16[512,384]{1,0:T(8,128)(2,1)}, bf16[512,384]{1,0:T(8,128)(2,1)S(1)}, u32[]{:S(2)}) copy-start(bf16[512,384]{1,0:T(8,128)(2,1)S(1)} %collective-permute-done.21.refs_14_) | copy-start | bytes 1179652
  114.7 2.9 %collective-permute-start.22 = (bf16[512,384]{1,0:T(8,128)(2,1)S(1)}, bf16[512,384]{1,0:T(8,128)(2,1)S(1)}, u32[]{:S(2)}, u32[]{:S(2)}) collective-permute-start(bf16[512,384]{1,0:T(8,128)(2,1)S(1)} %collective-permute-done.12.refs_7_), channel_id=1, source_target_pairs={{0,1},{1,0},{2,3},{3,2},{4,5},{5,4},{6,7},{7,6},{8,9},{9,8},{10,11... | collective-permute-start | bytes 1179656 | tf_op jit(solution)/shard_map/ppermute | solution.py:61
  114.8 2.8 %copy-start.14 = (bf16[512,384]{1,0:T(8,128)(2,1)}, bf16[512,384]{1,0:T(8,128)(2,1)S(1)}, u32[]{:S(2)}) copy-start(bf16[512,384]{1,0:T(8,128)(2,1)S(1)} %collective-permute-done.20.refs_13_) | copy-start | bytes 1179652
  114.8 3.6 %collective-permute-start.19 = (bf16[512,384]{1,0:T(8,128)(2,1)S(1)}, bf16[512,384]{1,0:T(8,128)(2,1)}, u32[]{:S(2)}, u32[]{:S(2)}) collective-permute-start(bf16[512,384]{1,0:T(8,128)(2,1)S(1)} %collective-permute-done.8.refs_1_), channel_id=1, source_target_pairs={{0,1},{1,0},{2,3},{3,2},{4,5},{5,4},{6,7},{7,6},{8,9},{9,8},{10,11... | collective-permute-start | bytes 1179656 | tf_op jit(solution)/shard_map/ppermute | solution.py:61
  115.2 2.4 %copy-start.15 = (bf16[512,384]{1,0:T(8,128)(2,1)}, bf16[512,384]{1,0:T(8,128)(2,1)S(1)}, u32[]{:S(2)}) copy-start(bf16[512,384]{1,0:T(8,128)(2,1)S(1)} %collective-permute-done.16.refs_9_) | copy-start | bytes 1179652
  115.9 1.7 copy-start.16
  116.5 1.1 copy-start.17
  117.6 0.7 copy-start.18
  123.7 22.2 %collective-permute-start.23 = (bf16[512,768]{1,0:T(8,128)(2,1)}, bf16[512,768]{1,0:T(8,128)(2,1)S(1)}, u32[]{:S(2)}, u32[]{:S(2)}) collective-permute-start(bf16[512,768]{1,0:T(8,128)(2,1)} %project.3), channel_id=1, source_target_pairs={{0,128},{8,136},{16,144},{24,152},{32,160},{40,168},{48,176},{56,1... | collective-permute-start | bytes 2359304 | tf_op jit(solution)/shard_map/ppermute | solution.py:386
  132.5 29.3 %copy-start.1 = (bf16[512,768]{1,0:T(8,128)(2,1)S(1)}, bf16[512,768]{1,0:T(8,128)(2,1)}, u32[]{:S(2)}) copy-start(bf16[512,768]{1,0:T(8,128)(2,1)} %residual_ref.1) | copy-start | bytes 2359300
  132.6 29.3 %copy-start.2 = (bf16[32,768]{1,0:T(8,128)(2,1)S(1)}, bf16[32,768]{1,0:T(8,128)(2,1)}, u32[]{:S(2)}) copy-start(bf16[32,768]{1,0:T(8,128)(2,1)} %gate_ref.1) | copy-start | bytes 147460
  132.6 29.3 %copy-start.3 = (s32[11]{0:T(128)S(1)}, s32[11]{0:T(128)}, u32[]{:S(2)}) copy-start(s32[11]{0:T(128)} %concatenate.3.info_ref) | copy-start | bytes 136
  132.6 26.0 %collective-permute-start.24 = (bf16[512,768]{1,0:T(8,128)(2,1)}, bf16[512,768]{1,0:T(8,128)(2,1)S(1)}, u32[]{:S(2)}, u32[]{:S(2)}) collective-permute-start(bf16[512,768]{1,0:T(8,128)(2,1)} %get-tuple-element.56), channel_id=1, source_target_pairs={{0,64},{8,72},{16,80},{24,88},{32,96},{40,104},{48,112},{56,120},{... | collective-permute-start | bytes 2359304 | tf_op jit(solution)/shard_map/ppermute | solution.py:386
  132.7 29.2 %collective-permute-start.25 = (bf16[512,768]{1,0:T(8,128)(2,1)}, bf16[512,768]{1,0:T(8,128)(2,1)S(1)}, u32[]{:S(2)}, u32[]{:S(2)}) collective-permute-start(bf16[512,768]{1,0:T(8,128)(2,1)} %get-tuple-element.57), channel_id=1, source_target_pairs={{0,192},{8,200},{16,208},{24,216},{32,224},{40,232},{48,240},{56,2... | collective-permute-start | bytes 2359304 | tf_op jit(solution)/shard_map/ppermute | solution.py:386
  161.9 1.4 copy-start
  165.5 1.2 collective-permute-start.26
  166.6 9.8 %copy-start.27 = (f32[4,1,128]{2,1,0:T(1,128)}, f32[4,1,128]{2,1,0:T(1,128)S(1)}, u32[]{:S(2)}) copy-start(f32[4,1,128]{2,1,0:T(1,128)S(1)} %add.30.s0_ref) | copy-start | bytes 6148
  166.6 6.3 %collective-permute-start.29 = (f32[4,1,128]{2,1,0:T(1,128)S(1)}, f32[4,1,128]{2,1,0:T(1,128)S(1)}, u32[]{:S(2)}, u32[]{:S(2)}) collective-permute-start(f32[4,1,128]{2,1,0:T(1,128)S(1)} %add.30.s0_ref), channel_id=1, source_target_pairs={{0,2},{1,3},{2,4},{3,5},{4,6},{5,7},{6,0},{7,1},{8,10},{9,11},{10,... | collective-permute-start | bytes 6152 | tf_op jit(solution)/shard_map/ppermute | solution.py:61
  169.3 5.1 %collective-permute-start.28 = (f32[4,1,128]{2,1,0:T(1,128)S(1)}, f32[4,1,128]{2,1,0:T(1,128)S(1)}, u32[]{:S(2)}, u32[]{:S(2)}) collective-permute-start(f32[4,1,128]{2,1,0:T(1,128)S(1)} %add.30.s0_ref), channel_id=1, source_target_pairs={{0,4},{1,5},{2,6},{3,7},{4,0},{5,1},{6,2},{7,3},{8,12},{9,13},{10,... | collective-permute-start | bytes 6152 | tf_op jit(solution)/shard_map/ppermute | solution.py:61
  172.8 3.6 %collective-permute-start.27 = (f32[4,1,128]{2,1,0:T(1,128)S(1)}, f32[4,1,128]{2,1,0:T(1,128)S(1)}, u32[]{:S(2)}, u32[]{:S(2)}) collective-permute-start(f32[4,1,128]{2,1,0:T(1,128)S(1)} %add.30.s0_ref), channel_id=1, source_target_pairs={{0,6},{1,7},{2,0},{3,1},{4,2},{5,3},{6,4},{7,5},{8,14},{9,15},{10,... | collective-permute-start | bytes 6152 | tf_op jit(solution)/shard_map/ppermute | solution.py:61
  172.9 3.5 %copy-start.29 = (f32[4,1,128]{2,1,0:T(1,128)}, f32[4,1,128]{2,1,0:T(1,128)S(1)}, u32[]{:S(2)}) copy-start(f32[4,1,128]{2,1,0:T(1,128)S(1)} %collective-permute-done.29.s3_ref) | copy-start | bytes 6148
  174.4 2.0 %copy-start.30 = (f32[4,1,128]{2,1,0:T(1,128)}, f32[4,1,128]{2,1,0:T(1,128)S(1)}, u32[]{:S(2)}) copy-start(f32[4,1,128]{2,1,0:T(1,128)S(1)} %collective-permute-done.28.s2_ref) | copy-start | bytes 6148
  176.4 0.6 copy-start.31
Sparse Core Ops, SparseCore 0:
  47.5 43.4 all-gather.2

commit v4 on v3

--- a/solution.py
+++ b/solution.py
@@ -23,6 +23,7 @@
 NT = (((1,), (1,)), ((), ()))
 HBM = pl.BlockSpec(memory_space=pltpu.HBM)
 ROOM = pltpu.CompilerParams(vmem_limit_bytes=56 * 1024 * 1024)
+MIDDLE = pltpu.CompilerParams(vmem_limit_bytes=52 * 1024 * 1024)
 TIGHT = pltpu.CompilerParams(vmem_limit_bytes=20 * 1024 * 1024)
 
 
@@ -70,26 +71,30 @@
     return pl.CostEstimate(flops=flops, bytes_accessed=nbytes, transcendentals=0)
 
 
-def pack_kv_kernel(k_ref, v_ref, r3_ref, r1_ref, l3_ref, l1_ref):
-    for which, ref in enumerate((k_ref, v_ref)):
-        r3_ref[which] = ref[1:]
-        r1_ref[which] = ref[:1]
-        l3_ref[which] = ref[: FR - 1]
-        l1_ref[which] = ref[FR - 1 :]
+def pack_kv_kernel(*refs):
+    r3_ref, r1_ref, l3_ref, l1_ref = refs[6:]
+    for i, ref in enumerate(refs[:6]):
+        which, at = i // 3, slice(i % 3 * HD, (i % 3 + 1) * HD)
+        r3_ref[which, :, :, at] = ref[1:]
+        r1_ref[which, :, :, at] = ref[:1]
+        l3_ref[which, :, :, at] = ref[: FR - 1]
+        l1_ref[which, :, :, at] = ref[FR - 1 :]
 
 
 def pack_kv(keys, values):
     sizes = (FR - 1, 1, FR - 1, 1)
+    heads = [pl.BlockSpec((FR, S, HD), lambda i, j=j: (0, 0, 2 * j + 1)) for j in range(3)]
+    keys, values = keys.reshape(FR, S, COLS), values.reshape(FR, S, COLS)
     return pl.pallas_call(
         pack_kv_kernel,
-        grid=(3,),
-        in_specs=[pl.BlockSpec((FR, S, HD), lambda j: (0, 0, 2 * j + 1))] * 2,
-        out_specs=[pl.BlockSpec((2, n, S, HD), lambda j: (0, 0, 0, j)) for n in sizes],
+        grid=(1,),
+        in_specs=heads * 2,
+        out_specs=[pl.BlockSpec((2, n, S, HALF), lambda i: (0, 0, 0, 0)) for n in sizes],
         out_shape=[jax.ShapeDtypeStruct((2, n, S, HALF), jnp.bfloat16) for n in sizes],
         compiler_params=ROOM,
         cost_estimate=cost(0, 6 * ROWS * HALF * 2),
         name="pack_kv",
-    )(keys.reshape(FR, S, COLS), values.reshape(FR, S, COLS))
+    )(keys, keys, keys, values, values, values)
 
 
 def softmax_weights(scores):
@@ -212,7 +217,7 @@
             out_specs=pl.BlockSpec((FR, step, HALF), lambda i, g: (0, i, 0)),
         ),
         out_shape=jax.ShapeDtypeStruct((FR, S, HALF), jnp.bfloat16),
-        compiler_params=ROOM,
+        compiler_params=TIGHT,
         cost_estimate=cost(ROWS * 3 * 4 * WINDOW * GROUP * HD, 10 * ROWS * COLS * 2),
         name="odd_attention",
     )(info, key_clips, frames(queries), frames(keys), frames(values), *others)
@@ -279,7 +284,7 @@
             ],
         ),
         out_shape=[jax.ShapeDtypeStruct((ROWS, COLS), out_type)] * n,
-        compiler_params=ROOM,
+        compiler_params=MIDDLE,
         cost_estimate=cost(4 * n * ROWS * COLS * COLS, 4 * 1024 * 1024),
         name="project",
     )(info, *operands)
@@ -362,7 +367,7 @@
             out_specs=block,
         ),
         out_shape=jax.ShapeDtypeStruct((ROWS, COLS), jnp.bfloat16),
-        compiler_params=ROOM,
+        compiler_params=TIGHT,
         cost_estimate=cost(0, ROWS * COLS * 4),
         name="norm",
     )(info, updated, *sums, scale, shift)

time: 188 us -> 183 us (0.973)
  Pallas kernels: 37.1 us -> 32.2 us
  waiting for transfers between devices: 75.7 us -> 78.6 us
    ppermute x3, starting transfers between devices: 3.06 us -> 5.96 us  [seq_move(): return lax.ppermute(a, 'seq', perm)]
    ppermute x12, starting transfers between devices: 9.83 us -> 7.38 us  [mp_move(): return lax.ppermute(a, 'mp', mp_perm(dx, dc))]
    unnamed x64 -> x52, local copies, waits for them, and re-layouts: 4.31 us -> 4.05 us
  transfers between devices with their start and end apart: 31 -> 31, of which waited for: 16 -> 16; matrix products, arithmetic and copies ran while one was open for 2% -> 1% of each run, Pallas kernels for 13% -> 11%
where the time goes in v4:
time: 183 us
  waiting for transfers between devices  78.6 us (43%)
  starting transfers between devices  52.6 us (29%)
  Pallas kernels  32.2 us (18%)
  between operations  14.4 us (8%)
  local copies, waits for them, and re-layouts  4.74 us (3%)
    ppermute x3, waiting for transfers between devices, seq_move(): return lax.ppermute(a, 'seq', perm)  22.1 us
    ppermute x8, starting transfers between devices, spread(): return lax.ppermute(a, ('seq', 'mp'), spread_perm(shift))  19.1 us
    ppermute x8, waiting for transfers between devices, spread(): return lax.ppermute(a, ('seq', 'mp'), spread_perm(shift))  18.2 us
    pallas_call x3, Pallas kernels, project(): pl.pallas_call(functools.partial(project_kernel, shifts), grid_spec=pltpu...  17 us
    ppermute x1, waiting for transfers between devices, local(): right1 = lax.ppermute(right1, 'seq', ring_perm(1))  15.1 us
    ppermute x1, waiting for transfers between devices, local(): right6 = lax.ppermute(right3, 'seq', ring_perm(1))  10.6 us
    ppermute x12, starting transfers between devices, mp_move(): return lax.ppermute(a, 'mp', mp_perm(dx, dc))  7.38 us
    ppermute x12, waiting for transfers between devices, mp_move(): return lax.ppermute(a, 'mp', mp_perm(dx, dc))  7.11 us
  transfers between devices with their start and end apart: 31, of which 16 were waited for; matrix products, arithmetic and copies ran while one was open for 1% of the time, Pallas kernels for 11%

profile of v4, /device:TPU:8, one launch (start us, length us, event | category | flops | bytes accessed | tf_op | source)
XLA Modules:
  0.0 183.1 jit_solution(17035674711853288826)
XLA Ops:
  7.2 0.0 all-gather.3.cloned.1.call-start
  7.2 2.6 %pack_kv.1 = (bf16[2,3,128,384]{3,2,1,0:T(8,128)(2,1)}, bf16[2,1,128,384]{3,2,1,0:T(8,128)(2,1)}, bf16[2,3,128,384]{3,2,1,0:T(8,128)(2,1)}, bf16[2,1,128,384]{3,2,1,0:T(8,128)(2,1)}) custom-call(bf16[4,128,768]{2,1,0:T(8,128)(2,1)} %bitcast.10, bf16[4,128,768]{2,1,0:T(8,128)(2,1)} %bitcast.11, bf16[4,128,768]{2,1,0:T(8,128)(2,1)} %bitcast.12, ...), custom_call_target="tpu_custom_call" | custom-call | bytes 2359296 | tf_op jit(solution)/shard_map/pack_kv/pallas_call | solution.py:88
  9.9 0.0 copy-start.3
  9.9 2.0 %collective-permute-start = (bf16[2,3,128,384]{3,2,1,0:T(8,128)(2,1)}, bf16[2,3,128,384]{3,2,1,0:T(8,128)(2,1)}, u32[]{:S(2)}, u32[]{:S(2)}) collective-permute-start(bf16[2,3,128,384]{3,2,1,0:T(8,128)(2,1)} %get-tuple-element.36), channel_id=1, source_target_pairs={{0,8},{8,16},{16,24},{24,32},{32,40},{40,48},{48,56},{56,64},{64,7... | collective-permute-start | bytes 1769480 | tf_op jit(solution)/shard_map/ppermute | solution.py:415
  11.9 3.9 %collective-permute-start.1 = (bf16[2,3,128,384]{3,2,1,0:T(8,128)(2,1)}, bf16[2,3,128,384]{3,2,1,0:T(8,128)(2,1)}, u32[]{:S(2)}, u32[]{:S(2)}) collective-permute-start(bf16[2,3,128,384]{3,2,1,0:T(8,128)(2,1)} %get-tuple-element.37), channel_id=1, source_target_pairs={{0,248},{8,0},{16,8},{24,16},{32,24},{40,32},{48,40},{56,48},{64,5... | collective-permute-start | bytes 1769480 | tf_op jit(solution)/shard_map/ppermute | solution.py:416
  15.8 5.8 %collective-permute-start.4 = (bf16[192,768]{1,0:T(8,128)(2,1)S(1)}, bf16[192,768]{1,0:T(8,128)(2,1)S(1)}, u32[]{:S(2)}, u32[]{:S(2)}) collective-permute-start(bf16[192,768]{1,0:T(8,128)(2,1)S(1)} %bitcast.27), channel_id=1, source_target_pairs={{0,0},{1,8},{8,16},{9,24},{16,32},{17,40},{24,48},{25,56},{32,1},{... | collective-permute-start | bytes 884744 | tf_op jit(solution)/shard_map/ppermute | solution.py:411
  21.6 0.1 collective-permute-start.2
  21.7 4.1 %collective-permute-start.3 = (bf16[2,1,128,384]{3,2,1,0:T(8,128)(2,1)}, bf16[2,1,128,384]{3,2,1,0:T(8,128)(2,1)S(1)}, u32[]{:S(2)}, u32[]{:S(2)}) collective-permute-start(bf16[2,1,128,384]{3,2,1,0:T(8,128)(2,1)} %get-tuple-element.39), channel_id=1, source_target_pairs={{0,248},{8,0},{16,8},{24,16},{32,24},{40,32},{48,40},{56,48},{64,5... | collective-permute-start | bytes 589832 | tf_op jit(solution)/shard_map/ppermute | solution.py:418
  25.8 0.1 copy.15
  25.9 0.1 reduce-window.8
  26.0 0.1 reduce
  26.1 0.2 convert_reduce_fusion.1
  26.3 0.2 select_reduce_fusion
  26.5 0.6 concatenate.3.info_ref
  27.1 3.9 %even_attention.1 = bf16[512,384]{1,0:T(8,128)(2,1)} custom-call(s32[11]{0:T(128)} %concatenate.3.info_ref, bf16[512,768]{1,0:T(8,128)(2,1)} %q_ref, bf16[512,768]{1,0:T(8,128)(2,1)} %k_ref.1, bf16[512,768]{1,0:T(8,128)(2,1)} %v_ref.1), custom_call_target="tpu_custom_call" | custom-call | flops 100663296 | bytes 3145728 | tf_op jit(solution)/shard_map/even_attention/pallas_call | solution.py:136
  31.0 15.1 %collective-permute-done.2.refs_1_ = bf16[2,1,128,384]{3,2,1,0:T(8,128)(2,1)S(1)} collective-permute-done((bf16[2,1,128,384]{3,2,1,0:T(8,128)(2,1)}, bf16[2,1,128,384]{3,2,1,0:T(8,128)(2,1)S(1)}, u32[]{:S(2)}, u32[]{:S(2)}) %collective-permute-start.2) | collective-permute-done | bytes 196640 | tf_op jit(solution)/shard_map/ppermute | solution.py:417
  46.1 0.7 copy-done.21
  46.8 0.0 all-gather.3.cloned.1.call-update
  46.8 0.1 collective-permute-start.5
  46.9 4.1 %collective-permute-start.6 = (bf16[2,3,128,384]{3,2,1,0:T(8,128)(2,1)}, bf16[2,3,128,384]{3,2,1,0:T(8,128)(2,1)S(1)}, u32[]{:S(2)}, u32[]{:S(2)}) collective-permute-start(bf16[2,3,128,384]{3,2,1,0:T(8,128)(2,1)} %collective-permute-done.1.refs_2_), channel_id=1, source_target_pairs={{0,248},{8,0},{16,8},{24,16},{32,24},{40,32},{48,40},{56,48},{64,5... | collective-permute-start | bytes 1769480 | tf_op jit(solution)/shard_map/ppermute | solution.py:437
  51.0 0.1 convert_reduce_fusion
  51.2 5.9 %collective-permute-start.10 = (bf16[512,384]{1,0:T(8,128)(2,1)}, bf16[512,384]{1,0:T(8,128)(2,1)S(1)}, u32[]{:S(2)}, u32[]{:S(2)}) collective-permute-start(bf16[512,384]{1,0:T(8,128)(2,1)} %even_attention.1), channel_id=1, source_target_pairs={{0,4},{1,5},{8,12},{9,13},{16,20},{17,21},{24,28},{25,29},{32,36},... | collective-permute-start | bytes 1179656 | tf_op jit(solution)/shard_map/ppermute | solution.py:382
  57.1 10.6 %collective-permute-done.5.refs_4_ = bf16[2,3,128,384]{3,2,1,0:T(8,128)(2,1)S(1)} collective-permute-done((bf16[2,3,128,384]{3,2,1,0:T(8,128)(2,1)}, bf16[2,3,128,384]{3,2,1,0:T(8,128)(2,1)S(1)}, u32[]{:S(2)}, u32[]{:S(2)}) %collective-permute-start.5) | collective-permute-done | bytes 589856 | tf_op jit(solution)/shard_map/ppermute | solution.py:436
  67.7 5.4 %collective-permute-done.6.refs_5_ = bf16[2,3,128,384]{3,2,1,0:T(8,128)(2,1)S(1)} collective-permute-done((bf16[2,3,128,384]{3,2,1,0:T(8,128)(2,1)}, bf16[2,3,128,384]{3,2,1,0:T(8,128)(2,1)S(1)}, u32[]{:S(2)}, u32[]{:S(2)}) %collective-permute-start.6) | collective-permute-done | bytes 589856 | tf_op jit(solution)/shard_map/ppermute | solution.py:437
  73.2 4.7 %odd_attention.1 = bf16[4,128,384]{2,1,0:T(8,128)(2,1)S(1)} custom-call(s32[11]{0:T(128)S(1)} %copy-done.9, s32[1,288]{1,0:T(1,128)S(1)} %broadcast_in_dim.29.clip_ref, bf16[4,128,768]{2,1,0:T(8,128)(2,1)S(1)} %bitcast.18, bf16[4,128,768]{2,1,0:T(8,128)(2,1)S(1)} %bitcast.13, bf16[4,128,768]{2,1,0:T(8,128)(2,1)S(1)} %bitcast.17, ...), custom_call_target="tpu_custom_call" | custom-call | flops 226492416 | bytes 7864320 | tf_op jit(solution)/shard_map/odd_attention/pallas_call | solution.py:208
  77.9 1.9 %collective-permute-start.7 = (bf16[512,384]{1,0:T(8,128)(2,1)S(1)}, bf16[512,384]{1,0:T(8,128)(2,1)S(1)}, u32[]{:S(2)}, u32[]{:S(2)}) collective-permute-start(bf16[512,384]{1,0:T(8,128)(2,1)S(1)} %copy-done.20), channel_id=1, source_target_pairs={{0,0},{1,1},{8,8},{9,9},{16,16},{17,17},{24,24},{25,25},{32,32},{3... | collective-permute-start | bytes 1179656 | tf_op jit(solution)/shard_map/ppermute | solution.py:382
  79.8 0.1 collective-permute-start.14
  79.9 0.1 collective-permute-start.13
  80.0 3.5 %collective-permute-start.12 = (bf16[512,384]{1,0:T(8,128)(2,1)S(1)}, bf16[512,384]{1,0:T(8,128)(2,1)S(1)}, u32[]{:S(2)}, u32[]{:S(2)}) collective-permute-start(bf16[512,384]{1,0:T(8,128)(2,1)S(1)} %bitcast.21), channel_id=1, source_target_pairs={{0,6},{1,7},{8,14},{9,15},{16,22},{17,23},{24,30},{25,31},{32,38},... | collective-permute-start | bytes 1179656 | tf_op jit(solution)/shard_map/ppermute | solution.py:382
  83.5 7.6 %collective-permute-start.8 = (bf16[512,384]{1,0:T(8,128)(2,1)S(1)}, bf16[512,384]{1,0:T(8,128)(2,1)S(1)}, u32[]{:S(2)}, u32[]{:S(2)}) collective-permute-start(bf16[512,384]{1,0:T(8,128)(2,1)S(1)} %bitcast.22), channel_id=1, source_target_pairs={{0,0},{1,1},{8,8},{9,9},{16,16},{17,17},{24,24},{25,25},{32,32},{3... | collective-permute-start | bytes 1179656 | tf_op jit(solution)/shard_map/ppermute | solution.py:382
  91.1 3.5 %collective-permute-done.7.refs_0_ = bf16[512,384]{1,0:T(8,128)(2,1)S(1)} collective-permute-done((bf16[512,384]{1,0:T(8,128)(2,1)S(1)}, bf16[512,384]{1,0:T(8,128)(2,1)S(1)}, u32[]{:S(2)}, u32[]{:S(2)}) %collective-permute-start.7) | collective-permute-done | bytes 393248 | tf_op jit(solution)/shard_map/ppermute | solution.py:382
  94.6 0.6 collective-permute-done.14.refs_5_
  95.2 0.0 collective-permute-start.21
  95.2 4.1 %collective-permute-done.13.refs_3_ = bf16[512,384]{1,0:T(8,128)(2,1)S(1)} collective-permute-done((bf16[512,384]{1,0:T(8,128)(2,1)S(1)}, bf16[512,384]{1,0:T(8,128)(2,1)S(1)}, u32[]{:S(2)}, u32[]{:S(2)}) %collective-permute-start.13) | collective-permute-done | bytes 393248 | tf_op jit(solution)/shard_map/ppermute | solution.py:382
  99.3 2.4 %collective-permute-start.20 = (bf16[512,384]{1,0:T(8,128)(2,1)S(1)}, bf16[512,384]{1,0:T(8,128)(2,1)S(1)}, u32[]{:S(2)}, u32[]{:S(2)}) collective-permute-start(bf16[512,384]{1,0:T(8,128)(2,1)S(1)} %collective-permute-done.13.refs_3_), channel_id=1, source_target_pairs={{0,1},{1,0},{2,3},{3,2},{4,5},{5,4},{6,7},{7,6},{8,9},{9,8},{10,11... | collective-permute-start | bytes 1179656 | tf_op jit(solution)/shard_map/ppermute | solution.py:62
  101.7 0.1 collective-permute-start.16
  101.8 10.0 %collective-permute-done.8.refs_1_ = bf16[512,384]{1,0:T(8,128)(2,1)S(1)} collective-permute-done((bf16[512,384]{1,0:T(8,128)(2,1)S(1)}, bf16[512,384]{1,0:T(8,128)(2,1)S(1)}, u32[]{:S(2)}, u32[]{:S(2)}) %collective-permute-start.8) | collective-permute-done | bytes 393248 | tf_op jit(solution)/shard_map/ppermute | solution.py:382
  111.8 0.5 collective-permute-start.18
  112.3 0.1 collective-permute-start.22
  112.4 0.4 collective-permute-start.19
  112.8 0.7 collective-permute-done.17.refs_10_
  113.5 0.6 collective-permute-done.18.refs_11_
  114.1 1.1 collective-permute-done.22.refs_15_
  115.2 0.7 copy-done.19
  116.0 4.7 %project.3 = bf16[512,768]{1,0:T(8,128)(2,1)} custom-call(s32[11]{0:T(128)S(1)} %copy-done.9, bf16[512,384]{1,0:T(8,128)(2,1)S(1)} %collective-permute-done.7.refs_0_, bf16[512,384]{1,0:T(8,128)(2,1)S(1)} %collective-permute-done.8.refs_1_, bf16[512,384]{1,0:T(8,128)(2,1)S(1)} %collective-permute-done.9.refs_2_, ...), custom_call_target="tpu_custom_call" | custom-call | flops 1207959552 | bytes 4194304 | tf_op jit(solution)/shard_map/project/pallas_call | solution.py:272
  120.7 1.9 %collective-permute-start.23 = (bf16[512,768]{1,0:T(8,128)(2,1)}, bf16[512,768]{1,0:T(8,128)(2,1)S(1)}, u32[]{:S(2)}, u32[]{:S(2)}) collective-permute-start(bf16[512,768]{1,0:T(8,128)(2,1)} %project.3), channel_id=1, source_target_pairs={{0,128},{8,136},{16,144},{24,152},{32,160},{40,168},{48,176},{56,1... | collective-permute-start | bytes 2359304 | tf_op jit(solution)/shard_map/ppermute | solution.py:391
  122.6 7.1 %project.4 = (bf16[512,768]{1,0:T(8,128)(2,1)}, bf16[512,768]{1,0:T(8,128)(2,1)}) custom-call(s32[11]{0:T(128)S(1)} %copy-done.9, bf16[512,384]{1,0:T(8,128)(2,1)S(1)} %collective-permute-done.7.refs_0_, bf16[512,384]{1,0:T(8,128)(2,1)S(1)} %collective-permute-done.8.refs_1_, bf16[512,384]{1,0:T(8,128)(2,1)S(1)} %collective-permute-done.9.refs_2_, ...), custom_call_target="tpu_custom_call" | custom-call | flops 2415919104 | bytes 4194304 | tf_op jit(solution)/shard_map/project/pallas_call | solution.py:272
  129.7 0.0 copy-start.4
  129.7 0.0 copy-start.6
  129.7 1.7 collective-permute-start.24
  131.4 2.3 %collective-permute-start.25 = (bf16[512,768]{1,0:T(8,128)(2,1)}, bf16[512,768]{1,0:T(8,128)(2,1)S(1)}, u32[]{:S(2)}, u32[]{:S(2)}) collective-permute-start(bf16[512,768]{1,0:T(8,128)(2,1)} %get-tuple-element.57), channel_id=1, source_target_pairs={{0,192},{8,200},{16,208},{24,216},{32,224},{40,232},{48,240},{56,2... | collective-permute-start | bytes 2359304 | tf_op jit(solution)/shard_map/ppermute | solution.py:391
  133.8 5.2 %project.5.own_ref = f32[512,768]{1,0:T(8,128)} custom-call(s32[11]{0:T(128)S(1)} %copy-done.9, bf16[512,384]{1,0:T(8,128)(2,1)S(1)} %collective-permute-done.7.refs_0_, bf16[512,384]{1,0:T(8,128)(2,1)S(1)} %collective-permute-done.8.refs_1_, bf16[512,384]{1,0:T(8,128)(2,1)S(1)} %collective-permute-done.9.refs_2_, ...), custom_call_target="tpu_custom_call" | custom-call | flops 1207959552 | bytes 4194304 | tf_op jit(solution)/shard_map/project/pallas_call | solution.py:272
  139.0 4.0 %collective-permute-done.23.p0_ref = bf16[512,768]{1,0:T(8,128)(2,1)S(1)} collective-permute-done((bf16[512,768]{1,0:T(8,128)(2,1)}, bf16[512,768]{1,0:T(8,128)(2,1)S(1)}, u32[]{:S(2)}, u32[]{:S(2)}) %collective-permute-start.23) | collective-permute-done | bytes 786464 | tf_op jit(solution)/shard_map/ppermute | solution.py:391
  143.0 18.1 %collective-permute-done.24.p1_ref = bf16[512,768]{1,0:T(8,128)(2,1)S(1)} collective-permute-done((bf16[512,768]{1,0:T(8,128)(2,1)}, bf16[512,768]{1,0:T(8,128)(2,1)S(1)}, u32[]{:S(2)}, u32[]{:S(2)}) %collective-permute-start.24) | collective-permute-done | bytes 786464 | tf_op jit(solution)/shard_map/ppermute | solution.py:391
  161.1 1.4 copy-done.2
  162.5 2.1 %update.1 = (bf16[512,768]{1,0:T(8,128)(2,1)}, f32[4,1,128]{2,1,0:T(1,128)S(1)}) custom-call(s32[11]{0:T(128)S(1)} %copy-done.9, f32[512,768]{1,0:T(8,128)S(1)} %copy-done.2, bf16[512,768]{1,0:T(8,128)(2,1)S(1)} %collective-permute-done.23.p0_ref, bf16[512,768]{1,0:T(8,128)(2,1)S(1)} %collective-permute-done.24.p1_ref, ...), custom_call_target="tpu_custom_call" | custom-call | bytes 5505024 | tf_op jit(solution)/shard_map/update/pallas_call | solution.py:324
  164.7 1.2 collective-permute-done.26
  165.8 0.3 collective-permute-start.29
  166.1 3.6 %collective-permute-start.28 = (f32[4,1,128]{2,1,0:T(1,128)S(1)}, f32[4,1,128]{2,1,0:T(1,128)S(1)}, u32[]{:S(2)}, u32[]{:S(2)}) collective-permute-start(f32[4,1,128]{2,1,0:T(1,128)S(1)} %add.30.s0_ref), channel_id=1, source_target_pairs={{0,4},{1,5},{2,6},{3,7},{4,0},{5,1},{6,2},{7,3},{8,12},{9,13},{10,... | collective-permute-start | bytes 6152 | tf_op jit(solution)/shard_map/ppermute | solution.py:62
  169.7 0.9 collective-permute-done.29.s3_ref
  170.6 0.7 collective-permute-done.28.s2_ref
  171.3 2.0 %collective-permute-done.27.s1_ref = f32[4,1,128]{2,1,0:T(1,128)S(1)} collective-permute-done((f32[4,1,128]{2,1,0:T(1,128)S(1)}, f32[4,1,128]{2,1,0:T(1,128)S(1)}, u32[]{:S(2)}, u32[]{:S(2)}) %collective-permute-start.27) | collective-permute-done | bytes 2080 | tf_op jit(solution)/shard_map/ppermute | solution.py:62
  173.3 1.1 copy-done.5
  174.4 1.8 norm.1
  (71 shorter events, 0.2 us)
Async XLA Ops:
  7.2 108.8 %all-gather.3.cloned.1.call-start = ((), (), s32[]{:S(2)}) async-start(), calls=%async_computation | async-start | bytes 2654208 | tf_op jit(solution)/shard_map/all_gather | solution.py:378
  7.2 8.6 %copy-start.24 = (bf16[768,192]{0,1:T(8,128)(2,1)S(1)}, bf16[768,192]{0,1:T(8,128)(2,1)}, u32[]{:S(2)}) copy-start(bf16[768,192]{0,1:T(8,128)(2,1)} %param.15) | copy-start | bytes 884740
  7.2 18.6 %copy-start.23 = (s32[32]{0:T(128)S(1)}, s32[32]{0:T(128)}, u32[]{:S(2)}) copy-start(s32[32]{0:T(128)} %param.19) | copy-start | bytes 388
  7.2 19.1 %copy-start.25 = (s32[32]{0:T(128)S(1)}, s32[32]{0:T(128)}, u32[]{:S(2)}) copy-start(s32[32]{0:T(128)} %param.20) | copy-start | bytes 388
  9.8 41.2 %copy-start.22 = (s32[288]{0:T(512)S(1)}, s32[288]{0:T(512)}, u32[]{:S(2)}) copy-start(s32[288]{0:T(512)} %constant.57.clone) | copy-start | bytes 3460
  9.8 63.3 %copy-start = (bf16[512,768]{1,0:T(8,128)(2,1)S(1)}, bf16[512,768]{1,0:T(8,128)(2,1)}, u32[]{:S(2)}) copy-start(bf16[512,768]{1,0:T(8,128)(2,1)} %k_ref.1) | copy-start | bytes 2359300
  9.8 63.3 %copy-start.1 = (bf16[512,768]{1,0:T(8,128)(2,1)S(1)}, bf16[512,768]{1,0:T(8,128)(2,1)}, u32[]{:S(2)}) copy-start(bf16[512,768]{1,0:T(8,128)(2,1)} %v_ref.1) | copy-start | bytes 2359300
  9.9 63.3 %copy-start.3 = (bf16[512,768]{1,0:T(8,128)(2,1)S(1)}, bf16[512,768]{1,0:T(8,128)(2,1)}, u32[]{:S(2)}) copy-start(bf16[512,768]{1,0:T(8,128)(2,1)} %q_ref) | copy-start | bytes 2359300
  9.9 36.2 %collective-permute-start = (bf16[2,3,128,384]{3,2,1,0:T(8,128)(2,1)}, bf16[2,3,128,384]{3,2,1,0:T(8,128)(2,1)}, u32[]{:S(2)}, u32[]{:S(2)}) collective-permute-start(bf16[2,3,128,384]{3,2,1,0:T(8,128)(2,1)} %get-tuple-element.36), channel_id=1, source_target_pairs={{0,8},{8,16},{16,24},{24,32},{32,40},{40,48},{48,56},{56,64},{64,7... | collective-permute-start | bytes 1769480 | tf_op jit(solution)/shard_map/ppermute | solution.py:415
  11.9 34.2 %collective-permute-start.1 = (bf16[2,3,128,384]{3,2,1,0:T(8,128)(2,1)}, bf16[2,3,128,384]{3,2,1,0:T(8,128)(2,1)}, u32[]{:S(2)}, u32[]{:S(2)}) collective-permute-start(bf16[2,3,128,384]{3,2,1,0:T(8,128)(2,1)} %get-tuple-element.37), channel_id=1, source_target_pairs={{0,248},{8,0},{16,8},{24,16},{32,24},{40,32},{48,40},{56,48},{64,5... | collective-permute-start | bytes 1769480 | tf_op jit(solution)/shard_map/ppermute | solution.py:416
  15.8 30.3 %collective-permute-start.4 = (bf16[192,768]{1,0:T(8,128)(2,1)S(1)}, bf16[192,768]{1,0:T(8,128)(2,1)S(1)}, u32[]{:S(2)}, u32[]{:S(2)}) collective-permute-start(bf16[192,768]{1,0:T(8,128)(2,1)S(1)} %bitcast.27), channel_id=1, source_target_pairs={{0,0},{1,8},{8,16},{9,24},{16,32},{17,40},{24,48},{25,56},{32,1},{... | collective-permute-start | bytes 884744 | tf_op jit(solution)/shard_map/ppermute | solution.py:411
  21.6 24.5 %collective-permute-start.2 = (bf16[2,1,128,384]{3,2,1,0:T(8,128)(2,1)}, bf16[2,1,128,384]{3,2,1,0:T(8,128)(2,1)S(1)}, u32[]{:S(2)}, u32[]{:S(2)}) collective-permute-start(bf16[2,1,128,384]{3,2,1,0:T(8,128)(2,1)} %get-tuple-element.38), channel_id=1, source_target_pairs={{0,8},{8,16},{16,24},{24,32},{32,40},{40,48},{48,56},{56,64},{64,7... | collective-permute-start | bytes 589832 | tf_op jit(solution)/shard_map/ppermute | solution.py:417
  21.7 24.4 %collective-permute-start.3 = (bf16[2,1,128,384]{3,2,1,0:T(8,128)(2,1)}, bf16[2,1,128,384]{3,2,1,0:T(8,128)(2,1)S(1)}, u32[]{:S(2)}, u32[]{:S(2)}) collective-permute-start(bf16[2,1,128,384]{3,2,1,0:T(8,128)(2,1)} %get-tuple-element.39), channel_id=1, source_target_pairs={{0,248},{8,0},{16,8},{24,16},{32,24},{40,32},{48,40},{56,48},{64,5... | collective-permute-start | bytes 589832 | tf_op jit(solution)/shard_map/ppermute | solution.py:418
  27.1 46.0 %copy-start.9 = (s32[11]{0:T(128)S(1)}, s32[11]{0:T(128)}, u32[]{:S(2)}) copy-start(s32[11]{0:T(128)} %concatenate.3.info_ref) | copy-start | bytes 136
  46.1 0.7 copy-start.21
  46.8 20.9 %collective-permute-start.5 = (bf16[2,3,128,384]{3,2,1,0:T(8,128)(2,1)}, bf16[2,3,128,384]{3,2,1,0:T(8,128)(2,1)S(1)}, u32[]{:S(2)}, u32[]{:S(2)}) collective-permute-start(bf16[2,3,128,384]{3,2,1,0:T(8,128)(2,1)} %collective-permute-done.refs_0_), channel_id=1, source_target_pairs={{0,8},{8,16},{16,24},{24,32},{32,40},{40,48},{48,56},{56,64},{64,7... | collective-permute-start | bytes 1769480 | tf_op jit(solution)/shard_map/ppermute | solution.py:436
  46.9 26.2 %collective-permute-start.6 = (bf16[2,3,128,384]{3,2,1,0:T(8,128)(2,1)}, bf16[2,3,128,384]{3,2,1,0:T(8,128)(2,1)S(1)}, u32[]{:S(2)}, u32[]{:S(2)}) collective-permute-start(bf16[2,3,128,384]{3,2,1,0:T(8,128)(2,1)} %collective-permute-done.1.refs_2_), channel_id=1, source_target_pairs={{0,248},{8,0},{16,8},{24,16},{32,24},{40,32},{48,40},{56,48},{64,5... | collective-permute-start | bytes 1769480 | tf_op jit(solution)/shard_map/ppermute | solution.py:437
  51.0 28.9 %collective-permute-start.11 = (bf16[512,384]{1,0:T(8,128)(2,1)}, bf16[512,384]{1,0:T(8,128)(2,1)S(1)}, u32[]{:S(2)}, u32[]{:S(2)}) collective-permute-start(bf16[512,384]{1,0:T(8,128)(2,1)} %even_attention.1), channel_id=1, source_target_pairs={{0,6},{1,7},{8,14},{9,15},{16,22},{17,23},{24,30},{25,31},{32,38},... | collective-permute-start | bytes 1179656 | tf_op jit(solution)/shard_map/ppermute | solution.py:382
  51.2 28.8 %collective-permute-start.10 = (bf16[512,384]{1,0:T(8,128)(2,1)}, bf16[512,384]{1,0:T(8,128)(2,1)S(1)}, u32[]{:S(2)}, u32[]{:S(2)}) collective-permute-start(bf16[512,384]{1,0:T(8,128)(2,1)} %even_attention.1), channel_id=1, source_target_pairs={{0,4},{1,5},{8,12},{9,13},{16,20},{17,21},{24,28},{25,29},{32,36},... | collective-permute-start | bytes 1179656 | tf_op jit(solution)/shard_map/ppermute | solution.py:382
  57.1 26.4 %collective-permute-start.9 = (bf16[512,384]{1,0:T(8,128)(2,1)}, bf16[512,384]{1,0:T(8,128)(2,1)S(1)}, u32[]{:S(2)}, u32[]{:S(2)}) collective-permute-start(bf16[512,384]{1,0:T(8,128)(2,1)} %even_attention.1), channel_id=1, source_target_pairs={{0,2},{1,3},{8,10},{9,11},{16,18},{17,19},{24,26},{25,27},{32,34},... | collective-permute-start | bytes 1179656 | tf_op jit(solution)/shard_map/ppermute | solution.py:382
  73.1 4.7 %copy-start.20 = (bf16[512,384]{1,0:T(8,128)(2,1)S(1)}, bf16[512,384]{1,0:T(8,128)(2,1)}, u32[]{:S(2)}) copy-start(bf16[512,384]{1,0:T(8,128)(2,1)} %even_attention.1) | copy-start | bytes 1179652
  77.9 16.7 %collective-permute-start.7 = (bf16[512,384]{1,0:T(8,128)(2,1)S(1)}, bf16[512,384]{1,0:T(8,128)(2,1)S(1)}, u32[]{:S(2)}, u32[]{:S(2)}) collective-permute-start(bf16[512,384]{1,0:T(8,128)(2,1)S(1)} %copy-done.20), channel_id=1, source_target_pairs={{0,0},{1,1},{8,8},{9,9},{16,16},{17,17},{24,24},{25,25},{32,32},{3... | collective-permute-start | bytes 1179656 | tf_op jit(solution)/shard_map/ppermute | solution.py:382
  79.8 15.4 %collective-permute-start.14 = (bf16[512,384]{1,0:T(8,128)(2,1)S(1)}, bf16[512,384]{1,0:T(8,128)(2,1)S(1)}, u32[]{:S(2)}, u32[]{:S(2)}) collective-permute-start(bf16[512,384]{1,0:T(8,128)(2,1)S(1)} %bitcast.19), channel_id=1, source_target_pairs={{0,4},{1,5},{8,12},{9,13},{16,20},{17,21},{24,28},{25,29},{32,36},... | collective-permute-start | bytes 1179656 | tf_op jit(solution)/shard_map/ppermute | solution.py:382
  79.9 33.6 %copy-start.10 = (bf16[512,384]{1,0:T(8,128)(2,1)}, bf16[512,384]{1,0:T(8,128)(2,1)S(1)}, u32[]{:S(2)}) copy-start(bf16[512,384]{1,0:T(8,128)(2,1)S(1)} %collective-permute-done.11.refs_6_) | copy-start | bytes 1179652
  79.9 19.4 %collective-permute-start.13 = (bf16[512,384]{1,0:T(8,128)(2,1)S(1)}, bf16[512,384]{1,0:T(8,128)(2,1)S(1)}, u32[]{:S(2)}, u32[]{:S(2)}) collective-permute-start(bf16[512,384]{1,0:T(8,128)(2,1)S(1)} %bitcast.20), channel_id=1, source_target_pairs={{0,2},{1,3},{8,10},{9,11},{16,18},{17,19},{24,26},{25,27},{32,34},... | collective-permute-start | bytes 1179656 | tf_op jit(solution)/shard_map/ppermute | solution.py:382
  80.0 21.7 %collective-permute-start.12 = (bf16[512,384]{1,0:T(8,128)(2,1)S(1)}, bf16[512,384]{1,0:T(8,128)(2,1)S(1)}, u32[]{:S(2)}, u32[]{:S(2)}) collective-permute-start(bf16[512,384]{1,0:T(8,128)(2,1)S(1)} %bitcast.21), channel_id=1, source_target_pairs={{0,6},{1,7},{8,14},{9,15},{16,22},{17,23},{24,30},{25,31},{32,38},... | collective-permute-start | bytes 1179656 | tf_op jit(solution)/shard_map/ppermute | solution.py:382
  83.5 28.3 %collective-permute-start.8 = (bf16[512,384]{1,0:T(8,128)(2,1)S(1)}, bf16[512,384]{1,0:T(8,128)(2,1)S(1)}, u32[]{:S(2)}, u32[]{:S(2)}) collective-permute-start(bf16[512,384]{1,0:T(8,128)(2,1)S(1)} %bitcast.22), channel_id=1, source_target_pairs={{0,0},{1,1},{8,8},{9,9},{16,16},{17,17},{24,24},{25,25},{32,32},{3... | collective-permute-start | bytes 1179656 | tf_op jit(solution)/shard_map/ppermute | solution.py:382
  94.6 17.2 %collective-permute-start.15 = (bf16[512,384]{1,0:T(8,128)(2,1)S(1)}, bf16[512,384]{1,0:T(8,128)(2,1)S(1)}, u32[]{:S(2)}, u32[]{:S(2)}) collective-permute-start(bf16[512,384]{1,0:T(8,128)(2,1)S(1)} %collective-permute-done.7.refs_0_), channel_id=1, source_target_pairs={{0,1},{1,0},{2,3},{3,2},{4,5},{5,4},{6,7},{7,6},{8,9},{9,8},{10,11... | collective-permute-start | bytes 1179656 | tf_op jit(solution)/shard_map/ppermute | solution.py:62
  95.2 20.8 %copy-start.11 = (bf16[512,384]{1,0:T(8,128)(2,1)}, bf16[512,384]{1,0:T(8,128)(2,1)S(1)}, u32[]{:S(2)}) copy-start(bf16[512,384]{1,0:T(8,128)(2,1)S(1)} %collective-permute-done.14.refs_5_) | copy-start | bytes 1179652
  95.2 17.1 %collective-permute-start.21 = (bf16[512,384]{1,0:T(8,128)(2,1)S(1)}, bf16[512,384]{1,0:T(8,128)(2,1)S(1)}, u32[]{:S(2)}, u32[]{:S(2)}) collective-permute-start(bf16[512,384]{1,0:T(8,128)(2,1)S(1)} %collective-permute-done.14.refs_5_), channel_id=1, source_target_pairs={{0,1},{1,0},{2,3},{3,2},{4,5},{5,4},{6,7},{7,6},{8,9},{9,8},{10,11... | collective-permute-start | bytes 1179656 | tf_op jit(solution)/shard_map/ppermute | solution.py:62
  99.3 13.1 %collective-permute-start.20 = (bf16[512,384]{1,0:T(8,128)(2,1)S(1)}, bf16[512,384]{1,0:T(8,128)(2,1)S(1)}, u32[]{:S(2)}, u32[]{:S(2)}) collective-permute-start(bf16[512,384]{1,0:T(8,128)(2,1)S(1)} %collective-permute-done.13.refs_3_), channel_id=1, source_target_pairs={{0,1},{1,0},{2,3},{3,2},{4,5},{5,4},{6,7},{7,6},{8,9},{9,8},{10,11... | collective-permute-start | bytes 1179656 | tf_op jit(solution)/shard_map/ppermute | solution.py:62
  101.7 14.2 %copy-start.12 = (bf16[512,384]{1,0:T(8,128)(2,1)}, bf16[512,384]{1,0:T(8,128)(2,1)S(1)}, u32[]{:S(2)}) copy-start(bf16[512,384]{1,0:T(8,128)(2,1)S(1)} %collective-permute-done.12.refs_7_) | copy-start | bytes 1179652
  101.7 11.1 %collective-permute-start.16 = (bf16[512,384]{1,0:T(8,128)(2,1)S(1)}, bf16[512,384]{1,0:T(8,128)(2,1)S(1)}, u32[]{:S(2)}, u32[]{:S(2)}) collective-permute-start(bf16[512,384]{1,0:T(8,128)(2,1)S(1)} %collective-permute-done.9.refs_2_), channel_id=1, source_target_pairs={{0,1},{1,0},{2,3},{3,2},{4,5},{5,4},{6,7},{7,6},{8,9},{9,8},{10,11... | collective-permute-start | bytes 1179656 | tf_op jit(solution)/shard_map/ppermute | solution.py:62
  111.8 1.7 collective-permute-start.17
  111.8 4.2 %copy-start.13 = (bf16[512,384]{1,0:T(8,128)(2,1)}, bf16[512,384]{1,0:T(8,128)(2,1)S(1)}, u32[]{:S(2)}) copy-start(bf16[512,384]{1,0:T(8,128)(2,1)S(1)} %collective-permute-done.15.refs_8_) | copy-start | bytes 1179652
  111.8 2.3 %collective-permute-start.18 = (bf16[512,384]{1,0:T(8,128)(2,1)S(1)}, bf16[512,384]{1,0:T(8,128)(2,1)S(1)}, u32[]{:S(2)}, u32[]{:S(2)}) collective-permute-start(bf16[512,384]{1,0:T(8,128)(2,1)S(1)} %collective-permute-done.11.refs_6_), channel_id=1, source_target_pairs={{0,1},{1,0},{2,3},{3,2},{4,5},{5,4},{6,7},{7,6},{8,9},{9,8},{10,11... | collective-permute-start | bytes 1179656 | tf_op jit(solution)/shard_map/ppermute | solution.py:62
  112.3 3.7 %copy-start.14 = (bf16[512,384]{1,0:T(8,128)(2,1)}, bf16[512,384]{1,0:T(8,128)(2,1)S(1)}, u32[]{:S(2)}) copy-start(bf16[512,384]{1,0:T(8,128)(2,1)S(1)} %collective-permute-done.21.refs_14_) | copy-start | bytes 1179652
  112.3 2.9 %collective-permute-start.22 = (bf16[512,384]{1,0:T(8,128)(2,1)S(1)}, bf16[512,384]{1,0:T(8,128)(2,1)S(1)}, u32[]{:S(2)}, u32[]{:S(2)}) collective-permute-start(bf16[512,384]{1,0:T(8,128)(2,1)S(1)} %collective-permute-done.12.refs_7_), channel_id=1, source_target_pairs={{0,1},{1,0},{2,3},{3,2},{4,5},{5,4},{6,7},{7,6},{8,9},{9,8},{10,11... | collective-permute-start | bytes 1179656 | tf_op jit(solution)/shard_map/ppermute | solution.py:62
  112.4 2.8 %copy-start.15 = (bf16[512,384]{1,0:T(8,128)(2,1)}, bf16[512,384]{1,0:T(8,128)(2,1)S(1)}, u32[]{:S(2)}) copy-start(bf16[512,384]{1,0:T(8,128)(2,1)S(1)} %collective-permute-done.20.refs_13_) | copy-start | bytes 1179652
  112.4 3.5 %collective-permute-start.19 = (bf16[512,384]{1,0:T(8,128)(2,1)S(1)}, bf16[512,384]{1,0:T(8,128)(2,1)}, u32[]{:S(2)}, u32[]{:S(2)}) collective-permute-start(bf16[512,384]{1,0:T(8,128)(2,1)S(1)} %collective-permute-done.8.refs_1_), channel_id=1, source_target_pairs={{0,1},{1,0},{2,3},{3,2},{4,5},{5,4},{6,7},{7,6},{8,9},{9,8},{10,11... | collective-permute-start | bytes 1179656 | tf_op jit(solution)/shard_map/ppermute | solution.py:62
  112.8 2.4 %copy-start.16 = (bf16[512,384]{1,0:T(8,128)(2,1)}, bf16[512,384]{1,0:T(8,128)(2,1)S(1)}, u32[]{:S(2)}) copy-start(bf16[512,384]{1,0:T(8,128)(2,1)S(1)} %collective-permute-done.16.refs_9_) | copy-start | bytes 1179652
  113.5 1.7 copy-start.17
  114.1 1.1 copy-start.18
  115.2 0.7 copy-start.19
  120.7 22.2 %collective-permute-start.23 = (bf16[512,768]{1,0:T(8,128)(2,1)}, bf16[512,768]{1,0:T(8,128)(2,1)S(1)}, u32[]{:S(2)}, u32[]{:S(2)}) collective-permute-start(bf16[512,768]{1,0:T(8,128)(2,1)} %project.3), channel_id=1, source_target_pairs={{0,128},{8,136},{16,144},{24,152},{32,160},{40,168},{48,176},{56,1... | collective-permute-start | bytes 2359304 | tf_op jit(solution)/shard_map/ppermute | solution.py:391
  129.7 31.4 %copy-start.4 = (bf16[512,768]{1,0:T(8,128)(2,1)S(1)}, bf16[512,768]{1,0:T(8,128)(2,1)}, u32[]{:S(2)}) copy-start(bf16[512,768]{1,0:T(8,128)(2,1)} %residual_ref.1) | copy-start | bytes 2359300
  129.7 31.4 %copy-start.6 = (bf16[32,768]{1,0:T(8,128)(2,1)S(1)}, bf16[32,768]{1,0:T(8,128)(2,1)}, u32[]{:S(2)}) copy-start(bf16[32,768]{1,0:T(8,128)(2,1)} %gate_ref.1) | copy-start | bytes 147460
  129.7 31.4 %collective-permute-start.24 = (bf16[512,768]{1,0:T(8,128)(2,1)}, bf16[512,768]{1,0:T(8,128)(2,1)S(1)}, u32[]{:S(2)}, u32[]{:S(2)}) collective-permute-start(bf16[512,768]{1,0:T(8,128)(2,1)} %get-tuple-element.56), channel_id=1, source_target_pairs={{0,64},{8,72},{16,80},{24,88},{32,96},{40,104},{48,112},{56,120},{... | collective-permute-start | bytes 2359304 | tf_op jit(solution)/shard_map/ppermute | solution.py:391
  131.4 29.6 %collective-permute-start.25 = (bf16[512,768]{1,0:T(8,128)(2,1)}, bf16[512,768]{1,0:T(8,128)(2,1)S(1)}, u32[]{:S(2)}, u32[]{:S(2)}) collective-permute-start(bf16[512,768]{1,0:T(8,128)(2,1)} %get-tuple-element.57), channel_id=1, source_target_pairs={{0,192},{8,200},{16,208},{24,216},{32,224},{40,232},{48,240},{56,2... | collective-permute-start | bytes 2359304 | tf_op jit(solution)/shard_map/ppermute | solution.py:391
  133.8 39.5 %copy-start.7 = (bf16[32,768]{1,0:T(8,128)(2,1)S(1)}, bf16[32,768]{1,0:T(8,128)(2,1)}, u32[]{:S(2)}) copy-start(bf16[32,768]{1,0:T(8,128)(2,1)} %scale_ref.1) | copy-start | bytes 147460
  133.8 39.5 %copy-start.8 = (bf16[32,768]{1,0:T(8,128)(2,1)S(1)}, bf16[32,768]{1,0:T(8,128)(2,1)}, u32[]{:S(2)}) copy-start(bf16[32,768]{1,0:T(8,128)(2,1)} %shift_ref.1) | copy-start | bytes 147460
  161.1 1.4 copy-start.2
  164.7 1.2 collective-permute-start.26
  165.8 4.8 %collective-permute-start.29 = (f32[4,1,128]{2,1,0:T(1,128)S(1)}, f32[4,1,128]{2,1,0:T(1,128)S(1)}, u32[]{:S(2)}, u32[]{:S(2)}) collective-permute-start(f32[4,1,128]{2,1,0:T(1,128)S(1)} %add.30.s0_ref), channel_id=1, source_target_pairs={{0,2},{1,3},{2,4},{3,5},{4,6},{5,7},{6,0},{7,1},{8,10},{9,11},{10,... | collective-permute-start | bytes 6152 | tf_op jit(solution)/shard_map/ppermute | solution.py:62
  166.1 5.1 %collective-permute-start.28 = (f32[4,1,128]{2,1,0:T(1,128)S(1)}, f32[4,1,128]{2,1,0:T(1,128)S(1)}, u32[]{:S(2)}, u32[]{:S(2)}) collective-permute-start(f32[4,1,128]{2,1,0:T(1,128)S(1)} %add.30.s0_ref), channel_id=1, source_target_pairs={{0,4},{1,5},{2,6},{3,7},{4,0},{5,1},{6,2},{7,3},{8,12},{9,13},{10,... | collective-permute-start | bytes 6152 | tf_op jit(solution)/shard_map/ppermute | solution.py:62
  169.7 3.6 %collective-permute-start.27 = (f32[4,1,128]{2,1,0:T(1,128)S(1)}, f32[4,1,128]{2,1,0:T(1,128)S(1)}, u32[]{:S(2)}, u32[]{:S(2)}) collective-permute-start(f32[4,1,128]{2,1,0:T(1,128)S(1)} %add.30.s0_ref), channel_id=1, source_target_pairs={{0,6},{1,7},{2,0},{3,1},{4,2},{5,3},{6,4},{7,5},{8,14},{9,15},{10,... | collective-permute-start | bytes 6152 | tf_op jit(solution)/shard_map/ppermute | solution.py:62
  173.3 1.1 copy-start.5
Sparse Core Ops, SparseCore 0:
  46.9 43.4 all-gather.2
